TPU v7x, 512 devices: a whole 4x8x8 slice. The times are simulated.
512 devices in a mesh: batch: 16 (over y, core), proto: 32 (over x, z).
Axes of the slice: x: 4, y: 8, z: 8, core: 2. Of those that a mesh axis runs over, the one named last changes fastest.
Arguments:
- embeddings: bfloat16 [4096, 2, 768], P('batch'), may hold values from -6 to 6
- prototypes: bfloat16 [65536, 768], P(('batch', 'proto')), may hold values from -6 to 6
Outputs:
- grad_embed: bfloat16 [4096, 2, 768], P(('batch', 'proto'))
- grad_proto: bfloat16 [65536, 768], P(('batch', 'proto'))
All inputs are finite; a program needn't handle non-finite values.
Results may differ from a plain program's by a relative error of at most 0.019.
Values may be sent and summed in bfloat16 or wider, within the bound.
No kernel may reach another device: no remote copies, remote signals or barrier semaphores. Data moves between devices by JAX's collectives and lax.ppermute only.
A program may use at most 64 MiB of HBM per device.

v0:
```python
import jax
import jax.numpy as jnp
from jax import lax
from jax.sharding import PartitionSpec as P

PROTOS = 65536
ITERS = 3


sharpness_divisor = 0.1
entropy = 0.05
loss_factor = 16.0


def unit_rows(values):
    widened = values.astype(jnp.float32)
    return (widened * lax.rsqrt(jnp.sum(widened * widened, axis=-1, keepdims=True) + 1e-06)).astype(
        jnp.bfloat16
    )


def proto_sum(values):
    return lax.psum(values, "batch")


def clip_sum(partial_value):
    return (lax.psum(partial_value, "proto"), None)


def on_device(embeddings, prototypes):
    row_count = embeddings.shape[0]
    feature_dim = embeddings.shape[2]
    normed = unit_rows(embeddings)
    flat_rows = normed.reshape(row_count * 2, feature_dim)
    centers = unit_rows(prototypes)
    prototype_logits = lax.dot_general(
        flat_rows,
        lax.all_gather(centers, "batch", axis=0, tiled=True),
        (((1,), (1,)), ((), ())),
        preferred_element_type=jnp.float32,
    )
    block_size = prototype_logits.shape[1]
    prototype_logits = prototype_logits.reshape(row_count, 2, block_size)
    total_rows = row_count * lax.axis_size("batch")
    exponent_terms = jnp.exp(prototype_logits / sharpness_divisor)
    softmax_partial = jnp.sum(exponent_terms, axis=2)
    plan_exp = jnp.exp(prototype_logits / entropy)
    exponent_sum = None
    code_targets = plan_exp
    for sweep_index in range(ITERS):
        colsum = proto_sum(jnp.sum(code_targets, axis=0))
        code_targets = code_targets / (PROTOS * colsum)[None]
        rowsum, gathered_total = clip_sum(jnp.sum(code_targets, axis=2))
        if sweep_index == 0:
            exponent_sum = gathered_total
        code_targets = code_targets / (total_rows * rowsum)[:, :, None]
    code_targets = code_targets * total_rows
    exponent_sum = lax.psum(softmax_partial, "proto")
    predicted_likelihoods = exponent_terms / exponent_sum[:, :, None]
    score_gradient = (
        loss_factor / sharpness_divisor * (predicted_likelihoods - code_targets[:, ::-1, :])
    ).astype(jnp.bfloat16)
    flat_grad = score_gradient.reshape(row_count * 2, block_size)
    sliced = flat_grad
    grad_proto = lax.psum_scatter(
        lax.dot_general(
            sliced, flat_rows, (((0,), (0,)), ((), ())), preferred_element_type=jnp.float32
        ).astype(jnp.bfloat16),
        "batch",
        scatter_dimension=0,
        tiled=True,
    )
    sliced = flat_grad
    local_term = jnp.dot(
        sliced,
        lax.all_gather(centers, "batch", axis=0, tiled=True),
        preferred_element_type=jnp.float32,
    )
    grad_embed = lax.psum_scatter(
        local_term.reshape(row_count, 2, feature_dim).astype(jnp.bfloat16),
        "proto",
        scatter_dimension=0,
        tiled=True,
    )
    return (grad_embed, grad_proto)


def solution(mesh):
    in_specs = (P("batch", None, None), P(("batch", "proto"), None))
    out_specs = (P(("batch", "proto"), None, None), P(("batch", "proto"), None))
    return jax.shard_map(
        on_device, mesh=mesh, in_specs=in_specs, out_specs=out_specs, check_vma=False
    )
```

profile of v0, /device:TPU:1, one launch (start us, length us, event | category | flops | bytes accessed | tf_op | source)
XLA Modules:
  0.0 728.9 jit_solution(6362395790793925516)
XLA Ops:
  7.2 0.0 all-gather.2.cloned.1.call-start
  7.2 1.0 fusion.27
  8.3 1.7 fusion.28
  10.0 0.0 all-gather.2.cloned.1.call-update
  10.0 0.0 reduce-scatter.7.cloned.1.call-start
  10.0 2.0 fusion.16
  12.1 1.8 fusion.17
  13.9 46.2 %all-gather.2.cloned.1.call-done = bf16[2048,768]{1,0:T(8,128)(2,1)} async-done(((bf16[128,768]{1,0:T(8,128)(2,1)}), bf16[2048,768]{1,0:T(8,128)(2,1)}) %all-gather.2.cloned.1.call-update) | async-done | bytes 3145744 | tf_op jit(solution)/shard_map/all_gather | solution.py:38
  60.1 5.7 fusion.24
  65.8 44.0 %psum.50 = f32[2,2048]{1,0:T(2,128)S(1)} all-reduce(f32[2,2048]{1,0:T(2,128)S(1)} %get-tuple-element.10), channel_id=1, replica_groups=mesh['batch'=16,'proto'=32] {'batch'}, use_global_device_ids=true, to_apply=%region_5.0 | all-reduce | flops 4096 | bytes 32768 | tf_op jit(solution)/shard_map/psum | solution.py:23
  109.8 3.6 fusion.11
  113.5 61.8 %psum.51 = f32[256,2]{0,1:T(2,128)S(1)} all-reduce(f32[256,2]{0,1:T(2,128)S(1)} %get-tuple-element.7), channel_id=1, replica_groups=mesh['batch'=16,'proto'=32] {'proto'}, use_global_device_ids=true, to_apply=%region_7.0 | all-reduce | flops 512 | bytes 4096 | tf_op jit(solution)/shard_map/psum | solution.py:27
  175.3 3.3 fusion.7
  178.6 59.6 %psum.52 = f32[2,2048]{1,0:T(2,128)S(1)} all-reduce(f32[2,2048]{1,0:T(2,128)S(1)} %fusion.7), channel_id=1, replica_groups=mesh['batch'=16,'proto'=32] {'batch'}, use_global_device_ids=true, to_apply=%region_9.0 | all-reduce | flops 4096 | bytes 32768 | tf_op jit(solution)/shard_map/psum | solution.py:23
  238.2 3.4 fusion.8
  241.6 55.8 %psum.53 = f32[256,2]{0,1:T(2,128)S(1)} all-reduce(f32[256,2]{0,1:T(2,128)S(1)} %fusion.8), channel_id=1, replica_groups=mesh['batch'=16,'proto'=32] {'proto'}, use_global_device_ids=true, to_apply=%region_11.0 | all-reduce | flops 512 | bytes 4096 | tf_op jit(solution)/shard_map/psum | solution.py:27
  297.4 3.8 fusion.9
  301.2 59.6 %psum.54 = f32[2,2048]{1,0:T(2,128)S(1)} all-reduce(f32[2,2048]{1,0:T(2,128)S(1)} %fusion.9), channel_id=1, replica_groups=mesh['batch'=16,'proto'=32] {'batch'}, use_global_device_ids=true, to_apply=%region_13.0 | all-reduce | flops 4096 | bytes 32768 | tf_op jit(solution)/shard_map/psum | solution.py:23
  360.8 3.7 fusion.10
  364.5 57.9 %all-reduce = (f32[256,2]{0,1:T(2,128)S(1)}, f32[256,2]{0,1:T(2,128)S(1)}) all-reduce(f32[256,2]{0,1:T(2,128)S(1)} %fusion.10, f32[256,2]{0,1:T(2,128)S(1)} %get-tuple-element.6), channel_id=1, replica_groups=mesh['batch'=16,'proto'=32] {'proto'}, use_global_device_ids=true, to_apply=%region_15.0 | all-reduce | flops 1024 | bytes 8192 | tf_op jit(solution)/shard_map/psum | solution.py:27
  422.4 0.0 copy-start
  422.4 3.7 fusion.6
  426.1 0.0 copy-done
  426.1 0.0 copy-start.1
  426.1 1.4 multiply_convert_fusion
  427.5 0.5 copy-done.1
  428.0 1.8 fusion.21
  429.8 0.9 copy.15
  430.8 0.0 reduce-scatter.7.cloned.1.call-update
  430.8 0.0 reduce-scatter.5.cloned.1.call-start
  430.8 3.5 bitcast_convert_fusion
  434.4 0.0 reduce-scatter.5.cloned.1.call-update
  434.4 220.2 %reduce-scatter.7.cloned.1.call-done = bf16[8,1536]{1,0:T(8,128)(2,1)} async-done(((bf16[256,1536]{1,0:T(8,128)(2,1)}), bf16[8,1536]{1,0:T(8,128)(2,1)}) %reduce-scatter.7.cloned.1.call-update) | async-done | bytes 24592
  654.6 1.4 copy.11
  655.9 66.5 %reduce-scatter.5.cloned.1.call-done = bf16[128,768]{1,0:T(8,128)(2,1)} async-done(((bf16[2048,768]{1,0:T(8,128)(2,1)}), bf16[128,768]{1,0:T(8,128)(2,1)}) %reduce-scatter.5.cloned.1.call-update) | async-done | bytes 196624 | tf_op jit(solution)/shard_map/reduce_scatter | solution.py:65
  (8 shorter events, 0.1 us)
Async XLA Ops:
  7.2 53.0 %all-gather.2.cloned.1.call-start = ((), (), s32[]{:S(2)}) async-start(), calls=%async_computation.2 | async-start | bytes 3342336 | tf_op jit(solution)/shard_map/all_gather | solution.py:38
  10.0 644.6 %reduce-scatter.7.cloned.1.call-start = ((), (), s32[]{:S(2)}) async-start(), calls=%async_computation.4 | async-start | bytes 811008
  422.4 3.7 copy-start
  426.1 1.9 copy-start.1
  430.8 291.6 %reduce-scatter.5.cloned.1.call-start = ((), (), s32[]{:S(2)}) async-start(), calls=%async_computation.3 | async-start | bytes 3342336 | tf_op jit(solution)/shard_map/reduce_scatter | solution.py:65
Sparse Core Ops, SparseCore 0:
  10.7 49.3 all-gather.1
  430.9 223.6 reduce-scatter.6
  658.0 64.3 reduce-scatter.4
where the time goes:
time: 731 us; the launch traced here: 729 us
  blocking collectives  339 us (46%)
  waiting for transfers between devices  333 us (46%)
  other arithmetic  29.7 us (4%)
  between operations  13.8 us (2%)
  matrix products  11 us (2%)
    unnamed x4, waiting for transfers between devices  220 us
    psum x3, blocking collectives, clip_sum(): return (lax.psum(partial_value, 'proto'), None)  176 us
    psum x3, blocking collectives, proto_sum(): return lax.psum(values, 'batch')  163 us
    reduce_scatter x1, waiting for transfers between devices, on_device(): lax.psum_scatter(lax.dot_general(sliced, flat_rows, (((0,), (0,)), ((), (...  66.5 us
    all_gather x1, waiting for transfers between devices, on_device(): lax.all_gather(centers, 'batch', axis=0, tiled=True)  46.2 us
  transfers between devices with their start and end apart: 3, of which 3 were waited for; matrix products, arithmetic and copies ran while one was open for 1% of the time, Pallas kernels for 0%

commit v1 on v0

v1 whole, which is shorter than its diff:
```python
import jax
import jax.numpy as jnp
from jax import lax
from jax.sharding import Mesh, PartitionSpec as P

PROTOS = 65536
CLIPS = 4096
CORES, XS, ZS = 2, 4, 8
SCALE = 16.0 / 0.1


def unit_rows(values):
    widened = values.astype(jnp.float32)
    norm = lax.rsqrt(jnp.sum(widened * widened, axis=-1, keepdims=True) + 1e-06)
    return (widened * norm).astype(jnp.bfloat16)


def sum_over(part, axes, count):
    everyone = jnp.broadcast_to(part[None], (count,) + part.shape)
    return jnp.sum(lax.all_to_all(everyone, axes, 0, 0), axis=0)


def swap_cores(part):
    return lax.ppermute(part, "core", [(0, 1), (1, 0)])


def on_device(embeddings, prototypes):
    clips = embeddings.shape[0]
    width = embeddings.shape[2]
    ys = lax.axis_size("y")
    first = lax.axis_index("core") == 0

    centers = lax.all_gather(unit_rows(prototypes), "y", axis=0, tiled=True)
    mine = unit_rows(embeddings).transpose(1, 0, 2)
    rows = jnp.concatenate([mine, swap_cores(mine)], axis=1)
    protos = centers.shape[0]

    scores = lax.dot_general(
        rows, centers, (((2,), (1,)), ((), ())), preferred_element_type=jnp.float32
    )
    likely = jnp.exp(scores * 10.0)

    def col_scale(weighted):
        part = jnp.sum(weighted, axis=1)
        return 1.0 / (PROTOS * sum_over(part, "y", ys))

    def row_sums(parts):
        parts = parts.reshape(-1, 2, 2, clips)
        parts = jnp.where(first, parts, parts[:, :, ::-1])
        total = sum_over(parts, ("x", "z", "core"), XS * ZS * CORES)
        return jnp.where(first, total, total[:, :, ::-1]).reshape(-1, 2, 2 * clips)

    col = col_scale(likely * likely)
    both = row_sums(
        jnp.stack([jnp.sum(likely * likely * col[:, None, :], axis=2), jnp.sum(likely, axis=2)])
    )
    row, soft = 1.0 / (CLIPS * both[0]), both[1]
    for _ in range(2):
        col = col_scale(likely * likely * row[:, :, None])
        row = 1.0 / (CLIPS * row_sums(jnp.sum(likely * likely * col[:, None, :], axis=2)[None])[0])

    probs = likely * (SCALE / soft)[:, :, None]
    codes = likely * likely * (SCALE * CLIPS * row)[:, :, None] * col[:, None, :]
    grad = (probs - codes[::-1]).astype(jnp.bfloat16)

    grad_proto = lax.psum_scatter(
        lax.dot_general(
            grad, rows, (((0, 1), (0, 1)), ((), ())), preferred_element_type=jnp.float32
        ).astype(jnp.bfloat16),
        "y",
        scatter_dimension=0,
        tiled=True,
    )
    part = lax.dot_general(
        grad, centers, (((2,), (0,)), ((), ())), preferred_element_type=jnp.float32
    ).astype(jnp.bfloat16)
    part = part[:, :clips].astype(jnp.float32) + swap_cores(part[:, clips:]).astype(jnp.float32)
    part = part.astype(jnp.bfloat16).reshape(2, XS, clips // XS, width).transpose(1, 0, 2, 3)
    part = jnp.sum(lax.all_to_all(part, "x", 0, 0).astype(jnp.float32), axis=0)
    part = part.astype(jnp.bfloat16).reshape(2, ZS, clips // XS // ZS, width).transpose(1, 0, 2, 3)
    part = jnp.sum(lax.all_to_all(part, "z", 0, 0).astype(jnp.float32), axis=0)
    grad_embed = part.astype(jnp.bfloat16).transpose(1, 0, 2)
    return grad_embed, grad_proto


def solution(mesh):
    split = Mesh(mesh.devices.reshape(-1, CORES, XS, ZS), ("y", "core", "x", "z"))
    batch, every = ("y", "core"), ("y", "core", "x", "z")
    return jax.shard_map(
        on_device,
        mesh=split,
        in_specs=(P(batch, None, None), P(every, None)),
        out_specs=(P(every, None, None), P(every, None)),
        check_vma=False,
    )
```

time: 731 us -> 232 us (0.32)
  waiting for transfers between devices: 333 us -> 54 us
  blocking collectives: 339 us -> 98.8 us
  starting transfers between devices: 0.12 us -> 22.5 us
    psum x6 -> x0, blocking collectives: 339 us -> none  [the longest x3 176 us: clip_sum(): return (lax.psum(partial_value, 'proto'), None)]
    unnamed x4 -> x2, waiting for transfers between devices: 220 us -> 0.03 us
    all_to_all x0 -> x6, blocking collectives: none -> 98.8 us  [the longest x4 72.3 us: sum_over(): return jnp.sum(lax.all_to_all(everyone, axes, 0, 0), axis=0)]
    reduce_scatter x1, waiting for transfers between devices: 66.5 us -> 0.01 us  [on_device(): lax.psum_scatter(lax.dot_general(grad, rows, (((0, 1), (0, 1)), ((), ()))...]
    all_to_all x0 -> x2, waiting for transfers between devices: none -> 19 us  [sum_over(): return jnp.sum(lax.all_to_all(everyone, axes, 0, 0), axis=0)]
    all_gather x1, waiting for transfers between devices: 46.2 us -> 31.2 us  [on_device(): centers = lax.all_gather(unit_rows(prototypes), 'y', axis=0, tiled=True)]
    ppermute x0 -> x2, starting transfers between devices: none -> 11.1 us  [swap_cores(): return lax.ppermute(part, 'core', [(0, 1), (1, 0)])]
    all_to_all x0 -> x2, starting transfers between devices: none -> 11.1 us  [sum_over(): return jnp.sum(lax.all_to_all(everyone, axes, 0, 0), axis=0)]
  transfers between devices with their start and end apart: 3 -> 6, of which waited for: 3 -> 5; matrix products, arithmetic and copies ran while one was open for 1% -> 3% of each run, Pallas kernels for 0% -> 0%
where the time goes in v1:
time: 232 us; the launch traced here: 231 us
  blocking collectives  98.8 us (43%)
  waiting for transfers between devices  54 us (23%)
  other arithmetic  26 us (11%)
  starting transfers between devices  22.5 us (10%)
  between operations  14.3 us (6%)
  matrix products  11.4 us (5%)
  local copies, waits for them, and re-layouts  3.63 us (2%)
    all_to_all x4, blocking collectives, sum_over(): return jnp.sum(lax.all_to_all(everyone, axes, 0, 0), axis=0)  72.3 us
    all_gather x1, waiting for transfers between devices, on_device(): centers = lax.all_gather(unit_rows(prototypes), 'y', axis=0, tiled=True)  31.2 us
    all_to_all x2, waiting for transfers between devices, sum_over(): return jnp.sum(lax.all_to_all(everyone, axes, 0, 0), axis=0)  19 us
    all_to_all x1, blocking collectives, on_device(): part = jnp.sum(lax.all_to_all(part, 'x', 0, 0).astype(jnp.float32), axis=0)  15 us
    all_to_all x1, blocking collectives, on_device(): part = jnp.sum(lax.all_to_all(part, 'z', 0, 0).astype(jnp.float32), axis=0)  11.6 us
    ppermute x2, starting transfers between devices, swap_cores(): return lax.ppermute(part, 'core', [(0, 1), (1, 0)])  11.1 us
    all_to_all x2, starting transfers between devices, sum_over(): return jnp.sum(lax.all_to_all(everyone, axes, 0, 0), axis=0)  11.1 us
    reduce_sum x2, other arithmetic, on_device(): jnp.sum(likely * likely * col[:, None, :], axis=2)[None]  6.18 us
  transfers between devices with their start and end apart: 6, of which 5 were waited for; matrix products, arithmetic and copies ran while one was open for 3% of the time, Pallas kernels for 0%

profile of v1, /device:TPU:1, one launch (start us, length us, event | category | flops | bytes accessed | tf_op | source)
XLA Modules:
  0.0 230.6 jit_solution(3843149825402486345)
XLA Ops:
  7.2 1.0 fusion.8
  8.3 1.7 fusion.9
  10.0 1.4 fusion.2
  11.4 1.3 fusion.7
  12.7 8.8 %collective-permute-start = (bf16[2,256,768]{2,1,0:T(8,128)(2,1)S(1)}, bf16[2,256,768]{2,1,0:T(8,128)(2,1)S(1)}, u32[]{:S(2)}, u32[]{:S(2)}) collective-permute-start(bf16[2,256,768]{2,1,0:T(8,128)(2,1)S(1)} %fusion.7), channel_id=1, source_target_pairs={{0,32},{32,0},{1,33},{33,1},{2,34},{34,2},{3,35},{35,3},{4,36},{36... | collective-permute-start | bytes 2359304 | tf_op jit(solution)/shard_map/ppermute | solution.py:24
  21.5 1.9 collective-permute-done
  23.4 31.2 %all-gather.2.cloned.1.call-done = bf16[1024,768]{1,0:T(8,128)(2,1)} async-done(((bf16[128,768]{1,0:T(8,128)(2,1)}), bf16[1024,768]{1,0:T(8,128)(2,1)}) %all-gather.2.cloned.1.call-update) | async-done | bytes 1572880 | tf_op jit(solution)/shard_map/all_gather | solution.py:33
  54.6 5.2 %fusion.15 = (f32[2,1024]{1,0:T(2,128)S(1)}, f32[2,512,1024]{2,1,0:T(8,128)}) fusion(bf16[1024,768]{1,0:T(8,128)(2,1)} %all-gather.2.cloned.1.call-done, bf16[2,256,768]{2,1,0:T(8,128)(2,1)S(1)} %collective-permute-done, bf16[2,256,768]{2,1,0:T(8,128)(2,1)S(1)} %fusion.7), kind=kOutput, calls=%fused_computation.47 | convolution fusion | flops 1616902144 | bytes 7348224 | tf_op jit(solution)/shard_map/dot_general | solution.py:38
  59.8 0.6 broadcast_in_dim.16
  60.4 3.8 %all-to-all-start = ((f32[8,2,1024]{2,1,0:T(2,128)}), f32[8,2,1024]{2,1,0:T(2,128)S(1)}, u32[]{:S(2)}, u32[]{:S(2)}) async-start(f32[8,2,1024]{2,1,0:T(2,128)} %broadcast_in_dim.16), calls=%async_computation | async-start | bytes 131072 | tf_op jit(solution)/shard_map/all_to_all | solution.py:20
  64.2 7.2 %all-to-all-done = f32[8,2,1024]{2,1,0:T(2,128)S(1)} async-done(((f32[8,2,1024]{2,1,0:T(2,128)}), f32[8,2,1024]{2,1,0:T(2,128)S(1)}, u32[]{:S(2)}, u32[]{:S(2)}) %all-to-all-start) | async-done | bytes 65568 | tf_op jit(solution)/shard_map/all_to_all | solution.py:20
  71.5 3.3 %fusion = (f32[2,512]{1,0:T(2,128)S(1)}, f32[2,512]{1,0:T(2,128)S(1)}) fusion(f32[2,512,1024]{2,1,0:T(8,128)} %get-tuple-element.13, f32[2,1024]{1,0:T(2,128)S(1)} %multiply_divide_fusion.2), kind=kLoop, calls=%fused_computation.8 | loop fusion | flops 5240832 | bytes 4210688 | tf_op jit(solution)/shard_map/reduce_sum | solution.py:55
  74.9 0.1 rev.17
  75.0 0.1 broadcast_in_dim.17
  75.2 33.9 %all_to_all.40 = f32[64,2,2,2,256]{4,3,2,1,0:T(2,128)S(1)} all-to-all(f32[64,2,2,2,256]{4,3,2,1,0:T(2,128)S(1)} %broadcast_in_dim.17), channel_id=1, replica_groups=mesh['y'=8,'core'=2,'x'=4,'z'=8] {'x','z','core'}, dimensions={0} | all-to-all | bytes 1048576 | tf_op jit(solution)/shard_map/all_to_all | solution.py:20
  109.0 0.2 reduce_sum.165
  109.2 0.1 rev.18
  109.4 3.0 %multiply_reduce_fusion.3 = f32[2,1024]{1,0:T(2,128)S(1)} fusion(f32[2,512]{1,0:T(2,128)S(1)} %bitcast.45, f32[2,512,1024]{2,1,0:T(8,128)} %get-tuple-element.13), kind=kLoop, calls=%fused_computation.5 | loop fusion | flops 4192256 | bytes 4206592 | tf_op jit(solution)/shard_map/reduce_sum | solution.py:44
  112.5 9.5 %all_to_all.41 = f32[8,2,1024]{2,1,0:T(2,128)S(1)} all-to-all(f32[8,2,1024]{2,1,0:T(2,128)S(1)} %broadcast_in_dim.18), channel_id=1, replica_groups=mesh['y'=8,'core'=2,'x'=4,'z'=8] {'y'}, dimensions={0} | all-to-all | bytes 131072 | tf_op jit(solution)/shard_map/all_to_all | solution.py:20
  122.0 3.1 %multiply_reduce_fusion.2 = f32[2,512]{1,0:T(2,128)S(1)} fusion(f32[2,1024]{1,0:T(2,128)S(1)} %multiply_divide_fusion.1, f32[2,512,1024]{2,1,0:T(8,128)} %get-tuple-element.13), kind=kLoop, calls=%fused_computation.4 | loop fusion | flops 4193280 | bytes 4206592 | tf_op jit(solution)/shard_map/reduce_sum | solution.py:60
  125.1 0.1 rev.19
  125.2 0.1 broadcast_in_dim.20
  125.3 19.3 %all_to_all.42 = f32[64,1,2,2,256]{4,3,2,1,0:T(2,128)S(1)} all-to-all(f32[64,1,2,2,256]{4,3,2,1,0:T(2,128)S(1)} %broadcast_in_dim.20), channel_id=1, replica_groups=mesh['y'=8,'core'=2,'x'=4,'z'=8] {'x','z','core'}, dimensions={0} | all-to-all | bytes 524288 | tf_op jit(solution)/shard_map/all_to_all | solution.py:20
  144.6 0.1 reduce_sum.169
  144.7 0.1 reverse.6
  144.9 3.0 %multiply_reduce_fusion.1 = f32[2,1024]{1,0:T(2,128)S(1)} fusion(f32[2,512]{1,0:T(2,128)S(1)} %bitcast.46, f32[2,512,1024]{2,1,0:T(8,128)} %get-tuple-element.13), kind=kLoop, calls=%fused_computation.3 | loop fusion | flops 4192256 | bytes 4206592 | tf_op jit(solution)/shard_map/reduce_sum | solution.py:44
  147.9 9.6 %all_to_all.43 = f32[8,2,1024]{2,1,0:T(2,128)S(1)} all-to-all(f32[8,2,1024]{2,1,0:T(2,128)S(1)} %broadcast_in_dim.21), channel_id=1, replica_groups=mesh['y'=8,'core'=2,'x'=4,'z'=8] {'y'}, dimensions={0} | all-to-all | bytes 131072 | tf_op jit(solution)/shard_map/all_to_all | solution.py:20
  157.5 3.1 %multiply_reduce_fusion = f32[2,512]{1,0:T(2,128)S(1)} fusion(f32[2,1024]{1,0:T(2,128)S(1)} %multiply_divide_fusion, f32[2,512,1024]{2,1,0:T(8,128)} %get-tuple-element.13), kind=kLoop, calls=%fused_computation.2 | loop fusion | flops 4193280 | bytes 4206592 | tf_op jit(solution)/shard_map/reduce_sum | solution.py:60
  160.6 0.1 rev.20
  160.7 0.8 broadcast_in_dim.23
  161.5 7.2 %all-to-all-start.5 = ((f32[64,1,2,2,256]{4,3,2,1,0:T(2,128)}), f32[64,1,2,2,256]{4,3,2,1,0:T(2,128)S(1)}, u32[]{:S(2)}, u32[]{:S(2)}) async-start(f32[64,1,2,2,256]{4,3,2,1,0:T(2,128)} %broadcast_in_dim.23), calls=%async_computation.5 | async-start | bytes 524288 | tf_op jit(solution)/shard_map/all_to_all | solution.py:20
  168.7 0.2 reduce-scatter.2.cloned.1.call-start
  169.0 11.8 %all-to-all-done.5 = f32[64,1,2,2,256]{4,3,2,1,0:T(2,128)S(1)} async-done(((f32[64,1,2,2,256]{4,3,2,1,0:T(2,128)}), f32[64,1,2,2,256]{4,3,2,1,0:T(2,128)S(1)}, u32[]{:S(2)}, u32[]{:S(2)}) %all-to-all-start.5) | async-done | bytes 262176 | tf_op jit(solution)/shard_map/all_to_all | solution.py:20
  180.7 0.1 reduce_sum.173
  180.9 0.1 reverse.7
  181.0 3.2 %multiply_multiply_fusion = f32[2,512,1024]{2,1,0:T(8,128)S(1)} fusion(f32[2,512]{1,0:T(2,128)S(1)} %bitcast.44, f32[2,1024]{1,0:T(2,128)S(1)} %multiply_divide_fusion, f32[2,512,1024]{2,1,0:T(8,128)} %get-tuple-element.13), kind=kLoop, calls=%fused_computation.1 | loop fusion | flops 4194304 | bytes 8400896 | tf_op jit(solution)/shard_map/mul | solution.py:63
  184.2 0.3 copy-done
  184.4 0.8 subtract_convert_fusion
  185.2 0.3 copy-done.2
  185.6 3.0 %bitcast_convert_fusion = bf16[1024,768]{1,0:T(8,128)(2,1)} fusion(bf16[2,512,1024]{2,1,0:T(8,128)(2,1)S(1)} %subtract_convert_fusion, bf16[2,256,768]{2,1,0:T(8,128)(2,1)S(1)} %copy-done.2, bf16[2,256,768]{2,1,0:T(8,128)(2,1)S(1)} %fusion.7), kind=kOutput, calls=%fused_computation.10 | convolution fusion | flops 1614544896 | bytes 5242880 | tf_op jit(solution)/shard_map/dot_general | solution.py:67
  188.6 3.2 %convolution_convert_fusion = bf16[2,512,768]{2,1,0:T(8,128)(2,1)S(1)} fusion(bf16[2,512,1024]{2,1,0:T(8,128)(2,1)S(1)} %subtract_convert_fusion, bf16[1024,768]{1,0:T(8,128)(2,1)} %all-gather.2.cloned.1.call-done), kind=kOutput, calls=%fused_computation.13 | convolution fusion | flops 1611399168 | bytes 5242880 | tf_op jit(solution)/shard_map/dot_general | solution.py:74
  191.9 2.4 %collective-permute-start.1 = (bf16[2,256,768]{2,1,0:T(8,128)(2,1)S(1)}, bf16[2,256,768]{2,1,0:T(8,128)(2,1)S(1)}, u32[]{:S(2)}, u32[]{:S(2)}) collective-permute-start(bf16[2,256,768]{2,1,0:T(8,128)(2,1)S(1)} %slice.21), channel_id=1, source_target_pairs={{0,32},{32,0},{1,33},{33,1},{2,34},{34,2},{3,35},{35,3},{4,36},{36... | collective-permute-start | bytes 2359304 | tf_op jit(solution)/shard_map/ppermute | solution.py:24
  194.2 1.9 collective-permute-done.1
  196.1 0.2 add_convert_fusion
  196.4 15.0 %all_to_all.44 = bf16[4,2,64,768]{3,2,1,0:T(8,128)(2,1)S(1)} all-to-all(bf16[4,2,64,768]{3,2,1,0:T(8,128)(2,1)S(1)} %bitcast.39), channel_id=1, replica_groups=mesh['y'=8,'core'=2,'x'=4,'z'=8] {'x'}, dimensions={0} | all-to-all | bytes 1572864 | tf_op jit(solution)/shard_map/all_to_all | solution.py:79
  211.4 0.1 reduce_sum.174
  211.5 11.6 %all_to_all.45 = bf16[8,2,8,768]{3,2,1,0:T(8,128)(2,1)S(1)} all-to-all(bf16[8,2,8,768]{3,2,1,0:T(8,128)(2,1)S(1)} %copy.31), channel_id=1, replica_groups=mesh['y'=8,'core'=2,'x'=4,'z'=8] {'z'}, dimensions={0} | all-to-all | bytes 393216 | tf_op jit(solution)/shard_map/all_to_all | solution.py:81
  223.1 0.6 copy.33
  (39 shorter events, 0.6 us)
Async XLA Ops:
  7.2 47.4 %all-gather.2.cloned.1.call-start = ((), (), s32[]{:S(2)}) async-start(), calls=%async_computation.9 | async-start | bytes 1769472 | tf_op jit(solution)/shard_map/all_gather | solution.py:33
  12.7 10.7 %collective-permute-start = (bf16[2,256,768]{2,1,0:T(8,128)(2,1)S(1)}, bf16[2,256,768]{2,1,0:T(8,128)(2,1)S(1)}, u32[]{:S(2)}, u32[]{:S(2)}) collective-permute-start(bf16[2,256,768]{2,1,0:T(8,128)(2,1)S(1)} %fusion.7), channel_id=1, source_target_pairs={{0,32},{32,0},{1,33},{33,1},{2,34},{34,2},{3,35},{35,3},{4,36},{36... | collective-permute-start | bytes 2359304 | tf_op jit(solution)/shard_map/ppermute | solution.py:24
  23.4 36.4 %copy-start.1 = (bf16[2,256,768]{2,1,0:T(8,128)(2,1)}, bf16[2,256,768]{2,1,0:T(8,128)(2,1)S(1)}, u32[]{:S(2)}) copy-start(bf16[2,256,768]{2,1,0:T(8,128)(2,1)S(1)} %collective-permute-done) | copy-start | bytes 2359300
  60.4 11.1 %all-to-all-start = ((f32[8,2,1024]{2,1,0:T(2,128)}), f32[8,2,1024]{2,1,0:T(2,128)S(1)}, u32[]{:S(2)}, u32[]{:S(2)}) async-start(f32[8,2,1024]{2,1,0:T(2,128)} %broadcast_in_dim.16), calls=%async_computation | async-start | bytes 131072 | tf_op jit(solution)/shard_map/all_to_all | solution.py:20
  161.5 19.2 %all-to-all-start.5 = ((f32[64,1,2,2,256]{4,3,2,1,0:T(2,128)}), f32[64,1,2,2,256]{4,3,2,1,0:T(2,128)S(1)}, u32[]{:S(2)}, u32[]{:S(2)}) async-start(f32[64,1,2,2,256]{4,3,2,1,0:T(2,128)} %broadcast_in_dim.23), calls=%async_computation.5 | async-start | bytes 524288 | tf_op jit(solution)/shard_map/all_to_all | solution.py:20
  168.7 55.0 %reduce-scatter.2.cloned.1.call-start = ((), (), s32[]{:S(2)}) async-start(), calls=%async_computation.10 | async-start | bytes 1769472 | tf_op jit(solution)/shard_map/reduce_scatter | solution.py:66
  181.0 3.5 %copy-start = (f32[2,512,1024]{2,1,0:T(8,128)S(1)}, f32[2,512,1024]{2,1,0:T(8,128)}, u32[]{:S(2)}) copy-start(f32[2,512,1024]{2,1,0:T(8,128)} %get-tuple-element.13) | copy-start | bytes 12582916
  184.4 1.1 copy-start.2
  191.9 4.3 %collective-permute-start.1 = (bf16[2,256,768]{2,1,0:T(8,128)(2,1)S(1)}, bf16[2,256,768]{2,1,0:T(8,128)(2,1)S(1)}, u32[]{:S(2)}, u32[]{:S(2)}) collective-permute-start(bf16[2,256,768]{2,1,0:T(8,128)(2,1)S(1)} %slice.21), channel_id=1, source_target_pairs={{0,32},{32,0},{1,33},{33,1},{2,34},{34,2},{3,35},{35,3},{4,36},{36... | collective-permute-start | bytes 2359304 | tf_op jit(solution)/shard_map/ppermute | solution.py:24
Sparse Core Ops, SparseCore 0:
  10.7 43.8 all-gather.1
  188.7 30.2 reduce-scatter.1

commit v2 on v1

v2 whole, which is shorter than its diff:
```python
import functools

import jax
import jax.numpy as jnp
from jax import lax
from jax.experimental import pallas as pl
from jax.experimental.pallas import tpu as pltpu
from jax.sharding import Mesh, PartitionSpec as P

PROTOS = 65536
CLIPS = 4096
YS, CORES, XS, ZS = 8, 2, 4, 8
SCALE = 16.0 / 0.1
F32, BF16 = jnp.float32, jnp.bfloat16
LANES = 128
WIDTH = 768
RING = (0, 2, -2, 1, 3, -1, -3, 4)
MINE = 256
ROWS = CORES * MINE
COLS = len(RING) * LANES
GROUP = XS * ZS * CORES


def params():
    return pltpu.CompilerParams(
        dimension_semantics=("arbitrary",), vmem_limit_bytes=28 * 1024 * 1024
    )


def call(kernel, places, ins, in_blocks, outs, out_blocks, grid, scratch, flops):
    return pl.pallas_call(
        kernel,
        out_shape=outs,
        grid_spec=pltpu.PrefetchScalarGridSpec(
            num_scalar_prefetch=1,
            grid=(grid,),
            in_specs=in_blocks,
            out_specs=out_blocks,
            scratch_shapes=scratch,
        ),
        compiler_params=params(),
        cost_estimate=pl.CostEstimate(flops=flops, bytes_accessed=4 << 20, transcendentals=0),
    )(places, *ins)


def whole(shape):
    return pl.BlockSpec(shape, lambda g, s: (0,) * len(shape))


def turned(block):
    return jnp.sum(block.T, axis=0, keepdims=True)


def down(row):
    return jnp.broadcast_to(row, (LANES, LANES)).T


def clip_row(s, view, half, part):
    return view * 4 + jnp.bitwise_xor(s[0], half) * 2 + part


def unit_kernel(x_ref, o_ref):
    wide = x_ref[...].astype(F32)
    norm = lax.rsqrt(jnp.sum(wide * wide, axis=-1, keepdims=True) + 1e-06)
    o_ref[...] = (wide * norm).astype(BF16)


def put_clips(s, step, acc, out):
    view, half = step // 2, step % 2
    for part in range(2):
        block = acc[part * LANES : (part + 1) * LANES]
        out[pl.ds(clip_row(s, view, half, part), 1), :] = turned(block)


def put_cols(s, cols, out):
    for view in range(2):
        for slot in range(len(RING)):
            out[pl.ds(view * YS + s[1 + slot], 1), :] = cols[
                view : view + 1, slot * LANES : (slot + 1) * LANES
            ]


def col_scales(s, recv_ref, total, cols):
    total[...] = jnp.sum(recv_ref[...], axis=0)
    for view in range(2):
        for slot in range(len(RING)):
            value = total[pl.ds(view * YS + s[1 + slot], 1), :]
            cols[view : view + 1, slot * LANES : (slot + 1) * LANES] = 1.0 / (PROTOS * value)


def score_kernel(s, rows, c0, c1, c2, up, dn, ft, fe, e_ref, cols_ref, soft_ref, centers, cols, soft):
    step = pl.program_id(0)

    @pl.when(step == 0)
    def _():
        place = 0
        for piece in (c0, c1, c2, up, dn, ft, fe):
            count = piece.shape[0]
            centers[place : place + count] = piece[...]
            place += count
        cols[...] = jnp.zeros_like(cols)

    scores = lax.dot_general(
        rows[0], centers[...], (((1,), (1,)), ((), ())), preferred_element_type=F32
    )
    likely = jnp.exp(scores * 10.0)
    e_ref[0] = likely
    acc = likely[:, :LANES]
    for slot in range(1, len(RING)):
        acc = acc + likely[:, slot * LANES : (slot + 1) * LANES]
    put_clips(s, step, acc, soft)
    view = step // 2
    cols[pl.ds(view, 1), :] += jnp.sum(likely * likely, axis=0, keepdims=True)

    @pl.when(step == 3)
    def _():
        soft_ref[...] = soft[...]
        put_cols(s, cols[...], soft)
        cols_ref[...] = jnp.broadcast_to(soft[...][None], cols_ref.shape)


def row_kernel(first, s, e_ref, recv_ref, *refs):
    if first:
        soft_ref, out_ref, total, cols, sums = refs
    else:
        out_ref, total, cols, sums = refs
    step = pl.program_id(0)

    @pl.when(step == 0)
    def _():
        col_scales(s, recv_ref, total, cols)

    view = step // 2
    scale = cols[pl.ds(view, 1), :]
    acc = None
    for slot in range(len(RING)):
        lanes = slice(slot * LANES, (slot + 1) * LANES)
        likely = e_ref[0, :, lanes]
        term = likely * likely * scale[:, lanes]
        acc = term if acc is None else acc + term
    put_clips(s, step, acc, sums)

    @pl.when(step == 3)
    def _():
        if first:
            both = jnp.concatenate([sums[...], soft_ref[...][:8]]).astype(BF16)
        else:
            both = sums[...]
        out_ref[...] = jnp.broadcast_to(both[None], out_ref.shape)


def col_kernel(first, s, e_ref, recv_ref, *refs):
    if first:
        out_ref, soft_ref, total, cols, sums = refs
    else:
        out_ref, total, cols, sums = refs
    step = pl.program_id(0)

    @pl.when(step == 0)
    def _():
        total[...] = jnp.sum(recv_ref[...].astype(F32), axis=0)
        cols[...] = jnp.zeros_like(cols)
        if first:
            soft_ref[...] = total[8:]

    view, half = step // 2, step % 2
    part_sums = []
    scale = [
        down(1.0 / (CLIPS * total[pl.ds(clip_row(s, view, half, part), 1), :])) for part in range(2)
    ]
    scale = jnp.concatenate(scale)
    for slot in range(len(RING)):
        likely = e_ref[0, :, slot * LANES : (slot + 1) * LANES]
        part_sums.append(jnp.sum(likely * likely * scale, axis=0, keepdims=True))
    cols[pl.ds(view, 1), :] += jnp.concatenate(part_sums, axis=1)

    @pl.when(step == 3)
    def _():
        put_cols(s, cols[...], sums)
        out_ref[...] = jnp.broadcast_to(sums[...][None], out_ref.shape)


def grad_kernel(
    s, e_ref, row_ref, col_ref, soft_ref, c0, c1, c2, up, dn, ft, fe,
    g_ref, mine_ref, other_ref, total, clips, cols, centers,
):
    step = pl.program_id(0)

    @pl.when(step == 0)
    def _():
        col_scales(s, col_ref, total, cols)
        clips[...] = jnp.sum(row_ref[...], axis=0)
        place = 0
        for piece in (c0, c1, c2, up, dn, ft, fe):
            count = piece.shape[0]
            centers[place : place + count] = piece[...]
            place += count

    block = (step + 2) % 4
    half, part = block // 2, block % 2
    for view in range(2):
        soft = down(SCALE / soft_ref[pl.ds(clip_row(s, view, half, part), 1), :])
        code = clips[pl.ds(clip_row(s, 1 - view, half, part), 1), :]
        code = down(SCALE * CLIPS / (CLIPS * code))
        for slot in range(len(RING)):
            lanes = slice(slot * LANES, (slot + 1) * LANES)
            mine, swapped = e_ref[view, :, lanes], e_ref[1 - view, :, lanes]
            codes = swapped * swapped * code * cols[1 - view : 2 - view, lanes]
            g_ref[view, :, lanes] = (mine * soft - codes).astype(BF16)
    for view in range(2):
        out = jnp.dot(g_ref[view], centers[...], preferred_element_type=F32).astype(BF16)

        @pl.when(step < 2)
        def _(out=out, view=view):
            other_ref[view] = out

        @pl.when(step >= 2)
        def _(out=out, view=view):
            mine_ref[view] = out


def proto_kernel(s, rows_ref, g_ref, rest_ref, up_ref, dn_ref, far_ref):
    step = pl.program_id(0)
    out = jnp.dot(rows_ref[:, :ROWS], g_ref[0], preferred_element_type=F32)
    out = out + jnp.dot(rows_ref[:, ROWS:], g_ref[1], preferred_element_type=F32)
    out = out.astype(BF16)
    one, two = out[:, :LANES], out[:, LANES:]

    @pl.when(step == 0)
    def _():
        rest_ref[0] = one
        rest_ref[1] = two

    @pl.when(step == 1)
    def _():
        rest_ref[2] = one
        up_ref[0] = two

    @pl.when(step == 2)
    def _():
        up_ref[1] = one
        dn_ref[0] = two

    @pl.when(step == 3)
    def _():
        dn_ref[1] = one
        far_ref[0] = two[: WIDTH // 2]
        far_ref[1] = two[WIDTH // 2 :]


def shift(part, axis, size, by):
    return lax.ppermute(part, axis, [(i, (i + by) % size) for i in range(size)])


def add(*parts):
    total = parts[0].astype(F32)
    for part in parts[1:]:
        total = total + part.astype(F32)
    return total.astype(BF16)


def gather_y(shard):
    below = shift(shard, "y", YS, 2)
    above = shift(shard, "y", YS, -2)
    up = shift(jnp.concatenate([shard, above]), "y", YS, -1)
    dn = shift(jnp.concatenate([shard, below]), "y", YS, 1)
    half = shard.shape[0] // 2
    far_top = shift(above[:half], "y", YS, -2)
    far_end = shift(below[half:], "y", YS, 2)
    return shard, above, below, up, dn, far_top, far_end


def scatter_y(rest, up, dn, far):
    below = shift(up, "y", YS, 1)
    above = shift(dn, "y", YS, -1)
    far_below = shift(far[0], "y", YS, 2)
    far_above = shift(far[1], "y", YS, -2)
    half = WIDTH // 2
    plus = add(rest[1], below[1], jnp.pad(far_below, ((0, half), (0, 0))))
    minus = add(rest[2], above[1], jnp.pad(far_above, ((half, 0), (0, 0))))
    return add(rest[0], below[0], above[0], shift(plus, "y", YS, 2), shift(minus, "y", YS, -2))


def unit_rows(values):
    wide = values.astype(F32)
    norm = lax.rsqrt(jnp.sum(wide * wide, axis=-1, keepdims=True) + 1e-06)
    return (wide * norm).astype(BF16)


def on_device(embeddings, prototypes):
    y, core = lax.axis_index("y"), lax.axis_index("core")
    places = jnp.stack([core] + [lax.rem(y + d + YS, YS) for d in RING]).astype(jnp.int32)

    theirs = shift(embeddings, "core", CORES, 1)
    shard = pl.pallas_call(
        unit_kernel,
        out_shape=jax.ShapeDtypeStruct(prototypes.shape, BF16),
        compiler_params=pltpu.CompilerParams(vmem_limit_bytes=28 * 1024 * 1024),
    )(prototypes)
    pieces = gather_y(shard)
    piece_blocks = [whole(p.shape) for p in pieces]
    rows = jnp.concatenate(
        [unit_rows(embeddings).transpose(1, 0, 2), unit_rows(theirs).transpose(1, 0, 2)], axis=1
    )
    flat = rows.reshape(2 * ROWS, WIDTH).T

    e_shape = jax.ShapeDtypeStruct((2, ROWS, COLS), F32)
    e_block = pl.BlockSpec((1, MINE, COLS), lambda g, s: (g // 2, g % 2, 0))
    col_shape = jax.ShapeDtypeStruct((YS, 2 * YS, LANES), F32)
    row_shape = jax.ShapeDtypeStruct((GROUP, 8, LANES), F32)
    both_shape = jax.ShapeDtypeStruct((GROUP, 16, LANES), BF16)
    col_scratch = pltpu.VMEM((2 * YS, LANES), F32)
    row_scratch = pltpu.VMEM((8, LANES), F32)
    cols = pltpu.VMEM((2, COLS), F32)
    vpu = 4 * ROWS * COLS

    likely, col_part, soft = call(
        score_kernel, places, (rows, *pieces),
        [pl.BlockSpec((1, MINE, WIDTH), lambda g, s: (g // 2, g % 2, 0)), *piece_blocks],
        (e_shape, col_shape, jax.ShapeDtypeStruct((2 * YS, LANES), F32)),
        (e_block, whole(col_shape.shape), whole((2 * YS, LANES))),
        4, [pltpu.VMEM((COLS, WIDTH), BF16), cols, col_scratch], 4 * ROWS * COLS * WIDTH,
    )

    def y_sum(part):
        return lax.all_to_all(part, "y", 0, 0)

    def xzc_sum(part):
        return lax.all_to_all(part, ("x", "z", "core"), 0, 0)

    col_part = y_sum(col_part)
    row_part = call(
        functools.partial(row_kernel, True), places, (likely, col_part, soft),
        [e_block, whole(col_shape.shape), whole((2 * YS, LANES))],
        both_shape, whole(both_shape.shape), 4, [col_scratch, cols, row_scratch], vpu,
    )
    row_part = xzc_sum(row_part)
    col_part, soft = call(
        functools.partial(col_kernel, True), places, (likely, row_part),
        [e_block, whole(both_shape.shape)],
        (col_shape, jax.ShapeDtypeStruct((8, LANES), F32)),
        (whole(col_shape.shape), whole((8, LANES))),
        4, [col_scratch, cols, col_scratch], vpu,
    )
    for sweep in range(2):
        col_part = y_sum(col_part)
        row_part = call(
            functools.partial(row_kernel, False), places, (likely, col_part),
            [e_block, whole(col_shape.shape)],
            row_shape, whole(row_shape.shape), 4, [col_scratch, cols, row_scratch], vpu,
        )
        row_part = xzc_sum(row_part)
        if sweep == 0:
            col_part = call(
                functools.partial(col_kernel, False), places, (likely, row_part),
                [e_block, whole(row_shape.shape)],
                col_shape, whole(col_shape.shape), 4, [row_scratch, cols, col_scratch], vpu,
            )

    block = (2, LANES, WIDTH)
    half_shape = jax.ShapeDtypeStruct((2, MINE, WIDTH), BF16)
    grad, mine, other = call(
        grad_kernel, places, (likely, row_part, col_part, soft, *pieces),
        [
            pl.BlockSpec((2, LANES, COLS), lambda g, s: (0, (g + 2) % 4, 0)),
            whole(row_shape.shape), whole(col_shape.shape), whole((8, LANES)), *piece_blocks,
        ],
        (jax.ShapeDtypeStruct((2, ROWS, COLS), BF16), half_shape, half_shape),
        (
            pl.BlockSpec((2, LANES, COLS), lambda g, s: (0, (g + 2) % 4, 0)),
            pl.BlockSpec(block, lambda g, s: (0, jnp.maximum(g - 2, 0), 0)),
            pl.BlockSpec(block, lambda g, s: (0, jnp.minimum(g, 1), 0)),
        ),
        4, [col_scratch, row_scratch, cols, pltpu.VMEM((COLS, WIDTH), BF16)],
        4 * ROWS * COLS * WIDTH,
    )
    theirs = shift(other, "core", CORES, 1)
    out_shapes = [(3, WIDTH, LANES), (2, WIDTH, LANES), (2, WIDTH, LANES), (2, WIDTH // 2, LANES)]
    sums = call(
        proto_kernel, places, (flat, grad),
        [whole(flat.shape), pl.BlockSpec((2, ROWS, 2 * LANES), lambda g, s: (0, 0, g))],
        tuple(jax.ShapeDtypeStruct(shape, BF16) for shape in out_shapes),
        tuple(whole(shape) for shape in out_shapes),
        4, [], 4 * ROWS * COLS * WIDTH,
    )
    grad_proto = scatter_y(*sums).T

    part = add(mine, theirs).reshape(2, XS, MINE // XS, WIDTH).transpose(1, 0, 2, 3)
    part = jnp.sum(lax.all_to_all(part, "x", 0, 0).astype(F32), axis=0).astype(BF16)
    part = part.reshape(2, ZS, MINE // XS // ZS, WIDTH).transpose(1, 0, 2, 3)
    part = jnp.sum(lax.all_to_all(part, "z", 0, 0).astype(F32), axis=0).astype(BF16)
    return part.transpose(1, 0, 2), grad_proto


def solution(mesh):
    split = Mesh(mesh.devices.reshape(YS, CORES, XS, ZS), ("y", "core", "x", "z"))
    batch, every = ("y", "core"), ("y", "core", "x", "z")
    return jax.shard_map(
        on_device,
        mesh=split,
        in_specs=(P(batch, None, None), P(every, None)),
        out_specs=(P(every, None, None), P(every, None)),
        check_vma=False,
    )
```

time: 232 us -> 214 us (0.922); the launches traced: 231 us -> 210 us
  starting transfers between devices: 22.5 us -> 62.2 us
  waiting for transfers between devices: 54 us -> 16.9 us
  other arithmetic: 26 us -> 2.78 us
  Pallas kernels: 0 us -> 20.4 us
  between operations: 14.3 us -> 1 us
  matrix products: 11.4 us -> 0 us
  local copies, waits for them, and re-layouts: 3.63 us -> 9.91 us
    ppermute x2 -> x14, starting transfers between devices: 11.1 us -> 54.5 us  [shift(): return lax.ppermute(part, axis, [(i, (i + by) % size) for i in range(size)])]
    all_gather x1 -> x0, waiting for transfers between devices: 31.2 us -> none  [on_device(): centers = lax.all_gather(unit_rows(prototypes), 'y', axis=0, tiled=True)]
    pallas_call x0 -> x9, Pallas kernels: none -> 20.4 us  [the longest x8 20.3 us: call(): pl.pallas_call(kernel, out_shape=outs, grid_spec=pltpu.PrefetchScalarGrid...]
    reduce_sum x15 -> x4, other arithmetic: 18.7 us -> 0.61 us  [the longest x2 0.46 us: unit_rows(): norm = lax.rsqrt(jnp.sum(wide * wide, axis=-1, keepdims=True) + 1e-06)]
    all_to_all x2, waiting for transfers between devices: 19 us -> 4.77 us  [the longest x1 4.77 us: on_device(): lax.all_to_all(part, 'z', 0, 0).astype(F32)]
    dot_general x3 -> x0, matrix products: 11.4 us -> none  [the longest x1 5.16 us: on_device(): lax.dot_general(rows, centers, (((2,), (1,)), ((), ())), preferred_elemen...]
    ppermute x2 -> x14, waiting for transfers between devices: 3.78 us -> 12.1 us  [shift(): return lax.ppermute(part, axis, [(i, (i + by) % size) for i in range(size)])]
    unnamed x12 -> x15, local copies, waits for them, and re-layouts: 1.25 us -> 7.4 us
  transfers between devices with their start and end apart: 6 -> 16, of which waited for: 5 -> 7; matrix products, arithmetic and copies ran while one was open for 3% -> 3% of each run, Pallas kernels for 0% -> 2%
where the time goes in v2:
time: 214 us; the launch traced here: 210 us
  blocking collectives  96.8 us (45%)
  starting transfers between devices  62.2 us (29%)
  Pallas kernels  20.4 us (10%)
  waiting for transfers between devices  16.9 us (8%)
  local copies, waits for them, and re-layouts  9.91 us (5%)
  other arithmetic  2.78 us (1%)
    all_to_all x3, blocking collectives, xzc_sum(): return lax.all_to_all(part, ('x', 'z', 'core'), 0, 0)  66 us
    ppermute x14, starting transfers between devices, shift(): return lax.ppermute(part, axis, [(i, (i + by) % size) for i in range(size)])  54.5 us
    all_to_all x3, blocking collectives, y_sum(): return lax.all_to_all(part, 'y', 0, 0)  30.8 us
    pallas_call x8, Pallas kernels, call(): pl.pallas_call(kernel, out_shape=outs, grid_spec=pltpu.PrefetchScalarGrid...  20.3 us
    ppermute x14, waiting for transfers between devices, shift(): return lax.ppermute(part, axis, [(i, (i + by) % size) for i in range(size)])  12.1 us
    unnamed x15, local copies, waits for them, and re-layouts  7.4 us
    all_to_all x1, waiting for transfers between devices, on_device(): lax.all_to_all(part, 'z', 0, 0).astype(F32)  4.77 us
  transfers between devices with their start and end apart: 16, of which 7 were waited for; matrix products, arithmetic and copies ran while one was open for 3% of the time, Pallas kernels for 2%

profile of v2, /device:TPU:1, one launch (start us, length us, event | category | flops | bytes accessed | tf_op | source)
XLA Modules:
  0.0 209.9 jit_solution(3609994024243222913)
XLA Ops:
  0.6 0.9 copy-done.2
  1.7 5.2 %collective-permute-start.2 = (bf16[128,768]{1,0:T(8,128)(2,1)S(1)}, bf16[128,768]{1,0:T(8,128)(2,1)S(1)}, u32[]{:S(2)}, u32[]{:S(2)}) collective-permute-start(bf16[128,768]{1,0:T(8,128)(2,1)S(1)} %shard_map.41.c0), channel_id=1, source_target_pairs={{0,128},{64,192},{128,256},{192,320},{256,384},{320,448},{384,0},{... | collective-permute-start | bytes 589832 | tf_op jit(solution)/shard_map/ppermute | solution.py:252
  6.9 3.6 %collective-permute-start.1 = (bf16[128,768]{1,0:T(8,128)(2,1)S(1)}, bf16[128,768]{1,0:T(8,128)(2,1)S(1)}, u32[]{:S(2)}, u32[]{:S(2)}) collective-permute-start(bf16[128,768]{1,0:T(8,128)(2,1)S(1)} %shard_map.41.c0), channel_id=1, source_target_pairs={{0,384},{64,448},{128,0},{192,64},{256,128},{320,192},{384,256},{4... | collective-permute-start | bytes 589832 | tf_op jit(solution)/shard_map/ppermute | solution.py:252
  10.5 1.2 copy.19
  11.7 8.1 %collective-permute-start = (bf16[256,2,768]{2,0,1:T(8,128)(2,1)S(1)}, bf16[256,2,768]{2,0,1:T(8,128)(2,1)S(1)}, u32[]{:S(2)}, u32[]{:S(2)}) collective-permute-start(bf16[256,2,768]{2,0,1:T(8,128)(2,1)S(1)} %copy.19), channel_id=1, source_target_pairs={{0,32},{32,0},{1,33},{33,1},{2,34},{34,2},{3,35},{35,3},{4,36},{36... | collective-permute-start | bytes 2359304 | tf_op jit(solution)/shard_map/ppermute | solution.py:252
  20.4 1.9 collective-permute-start.6
  22.3 5.5 %collective-permute-start.5 = (bf16[64,768]{1,0:T(8,128)(2,1)S(1)}, bf16[64,768]{1,0:T(8,128)(2,1)S(1)}, u32[]{:S(2)}, u32[]{:S(2)}) collective-permute-start(bf16[64,768]{1,0:T(8,128)(2,1)S(1)} %slice.44), channel_id=1, source_target_pairs={{0,384},{64,448},{128,0},{192,64},{256,128},{320,192},{384,256},{4... | collective-permute-start | bytes 294920 | tf_op jit(solution)/shard_map/ppermute | solution.py:252
  27.9 1.9 collective-permute-start.4
  29.8 4.6 %collective-permute-start.3 = (bf16[256,768]{1,0:T(8,128)(2,1)S(1)}, bf16[256,768]{1,0:T(8,128)(2,1)S(1)}, u32[]{:S(2)}, u32[]{:S(2)}) collective-permute-start(bf16[256,768]{1,0:T(8,128)(2,1)S(1)} %get-tuple-element.39), channel_id=1, source_target_pairs={{0,448},{64,0},{128,64},{192,128},{256,192},{320,256},{384,320},{4... | collective-permute-start | bytes 1179656 | tf_op jit(solution)/shard_map/ppermute | solution.py:252
  35.0 5.8 %collective-permute-done.4.dn = bf16[256,768]{1,0:T(8,128)(2,1)S(1)} collective-permute-done((bf16[256,768]{1,0:T(8,128)(2,1)S(1)}, bf16[256,768]{1,0:T(8,128)(2,1)S(1)}, u32[]{:S(2)}, u32[]{:S(2)}) %collective-permute-start.4) | collective-permute-done | bytes 393248 | tf_op jit(solution)/shard_map/ppermute | solution.py:252
  40.8 0.9 collective-permute-done.3.up
  41.7 3.7 %shard_map.42 = (f32[2,512,1024]{2,1,0:T(8,128)S(1)}, f32[8,16,128]{2,1,0:T(8,128)S(1)}, f32[16,128]{1,0:T(8,128)S(1)}) custom-call(s32[9]{0:T(128)S(1)} %stack.39.s, bf16[2,512,768]{2,1,0:T(8,128)(2,1)S(1)} %pad_maximum_fusion.rows, bf16[128,768]{1,0:T(8,128)(2,1)S(1)} %shard_map.41.c0, bf16[128,768]{1,0:T(8,128)(2,1)S(1)} %collective-permute-done.1.c1, ...), custom_call_target="tpu_custom_call" | custom-call | flops 1610612736 | bytes 4194304 | tf_op jit(solution)/shard_map/pallas_call | solution.py:31
  45.4 11.7 %all_to_all.40.recv_ref = f32[8,16,128]{2,1,0:T(8,128)S(1)} all-to-all(f32[8,16,128]{2,1,0:T(8,128)S(1)} %get-tuple-element.15), channel_id=1, replica_groups=mesh['y'=8,'core'=2,'x'=4,'z'=8] {'y'}, dimensions={0} | all-to-all | bytes 131072 | tf_op jit(solution)/shard_map/all_to_all | solution.py:326
  57.1 1.4 shard_map.43
  58.5 27.9 %all_to_all.41.recv_ref = bf16[64,16,128]{2,1,0:T(8,128)(2,1)S(1)} all-to-all(bf16[64,16,128]{2,1,0:T(8,128)(2,1)S(1)} %shard_map.43), channel_id=1, replica_groups=mesh['y'=8,'core'=2,'x'=4,'z'=8] {'x','z','core'}, dimensions={0} | all-to-all | bytes 524288 | tf_op jit(solution)/shard_map/all_to_all | solution.py:329
  86.4 1.4 shard_map.44
  87.8 9.6 %all_to_all.42.recv_ref = f32[8,16,128]{2,1,0:T(8,128)S(1)} all-to-all(f32[8,16,128]{2,1,0:T(8,128)S(1)} %get-tuple-element.17), channel_id=1, replica_groups=mesh['y'=8,'core'=2,'x'=4,'z'=8] {'y'}, dimensions={0} | all-to-all | bytes 131072 | tf_op jit(solution)/shard_map/all_to_all | solution.py:326
  97.4 1.4 shard_map.45
  98.7 19.0 %all_to_all.43.recv_ref = f32[64,8,128]{2,1,0:T(8,128)S(1)} all-to-all(f32[64,8,128]{2,1,0:T(8,128)S(1)} %shard_map.45), channel_id=1, replica_groups=mesh['y'=8,'core'=2,'x'=4,'z'=8] {'x','z','core'}, dimensions={0} | all-to-all | bytes 524288 | tf_op jit(solution)/shard_map/all_to_all | solution.py:329
  117.8 1.4 shard_map.46
  119.2 9.6 %all_to_all.44.recv_ref.col_ref = f32[8,16,128]{2,1,0:T(8,128)S(1)} all-to-all(f32[8,16,128]{2,1,0:T(8,128)S(1)} %shard_map.46), channel_id=1, replica_groups=mesh['y'=8,'core'=2,'x'=4,'z'=8] {'y'}, dimensions={0} | all-to-all | bytes 131072 | tf_op jit(solution)/shard_map/all_to_all | solution.py:326
  128.7 1.4 shard_map.47
  130.1 19.0 %all_to_all.45.row_ref = f32[64,8,128]{2,1,0:T(8,128)S(1)} all-to-all(f32[64,8,128]{2,1,0:T(8,128)S(1)} %shard_map.47), channel_id=1, replica_groups=mesh['y'=8,'core'=2,'x'=4,'z'=8] {'x','z','core'}, dimensions={0} | all-to-all | bytes 524288 | tf_op jit(solution)/shard_map/all_to_all | solution.py:329
  149.1 6.3 %shard_map.48 = (bf16[2,512,1024]{2,1,0:T(8,128)(2,1)S(1)}, bf16[2,256,768]{2,1,0:T(8,128)(2,1)S(1)}, bf16[2,256,768]{2,1,0:T(8,128)(2,1)}) custom-call(s32[9]{0:T(128)S(1)} %stack.39.s, f32[2,512,1024]{2,1,0:T(8,128)S(1)} %get-tuple-element.14.e_ref, f32[64,8,128]{2,1,0:T(8,128)S(1)} %all_to_all.45.row_ref, f32[8,16,128]{2,1,0:T(8,128)S(1)} %all_to_all.44.recv_ref.col_ref, ...), custom_call_target="tpu_custom_call" | custom-call | flops 1610612736 | bytes 4194304 | tf_op jit(solution)/shard_map/pallas_call | solution.py:31
  155.5 0.9 copy-done
  156.3 1.3 copy-done.3
  157.7 2.4 %collective-permute-start.7 = (bf16[2,256,768]{2,1,0:T(8,128)(2,1)}, bf16[2,256,768]{2,1,0:T(8,128)(2,1)}, u32[]{:S(2)}, u32[]{:S(2)}) collective-permute-start(bf16[2,256,768]{2,1,0:T(8,128)(2,1)} %get-tuple-element.20), channel_id=1, source_target_pairs={{0,32},{32,0},{1,33},{33,1},{2,34},{34,2},{3,35},{35,3},{4,36},{36... | collective-permute-start | bytes 2359304 | tf_op jit(solution)/shard_map/ppermute | solution.py:252
  160.1 0.8 copy.26
  160.8 1.6 copy-done.4
  162.4 3.4 %shard_map.49 = (bf16[3,768,128]{2,1,0:T(8,128)(2,1)S(1)}, bf16[2,768,128]{2,1,0:T(8,128)(2,1)S(1)}, bf16[2,768,128]{2,1,0:T(8,128)(2,1)S(1)}, bf16[2,384,128]{2,1,0:T(8,128)(2,1)S(1)}) custom-call(s32[9]{0:T(128)S(1)} %stack.39.s, bf16[768,1024]{1,0:T(8,128)(2,1)S(1)} %bitcast.46, bf16[2,512,1024]{2,1,0:T(8,128)(2,1)S(1)} %copy-done.4), custom_call_target="tpu_custom_call" | custom-call | flops 1610612736 | bytes 4194304 | tf_op jit(solution)/shard_map/pallas_call | solution.py:31
  165.8 2.2 %collective-permute-start.8 = (bf16[2,768,128]{2,1,0:T(8,128)(2,1)S(1)}, bf16[2,768,128]{2,1,0:T(8,128)(2,1)S(1)}, u32[]{:S(2)}, u32[]{:S(2)}) collective-permute-start(bf16[2,768,128]{2,1,0:T(8,128)(2,1)S(1)} %get-tuple-element.23), channel_id=1, source_target_pairs={{0,64},{64,128},{128,192},{192,256},{256,320},{320,384},{384,448},... | collective-permute-start | bytes 1179656 | tf_op jit(solution)/shard_map/ppermute | solution.py:252
  168.0 4.3 %collective-permute-start.9 = (bf16[2,768,128]{2,1,0:T(8,128)(2,1)S(1)}, bf16[2,768,128]{2,1,0:T(8,128)(2,1)S(1)}, u32[]{:S(2)}, u32[]{:S(2)}) collective-permute-start(bf16[2,768,128]{2,1,0:T(8,128)(2,1)S(1)} %get-tuple-element.24), channel_id=1, source_target_pairs={{0,448},{64,0},{128,64},{192,128},{256,192},{320,256},{384,320},{4... | collective-permute-start | bytes 1179656 | tf_op jit(solution)/shard_map/ppermute | solution.py:252
  172.3 1.3 add_convert_fusion
  173.7 0.9 copy.30
  174.6 3.7 %all-to-all-start.6 = ((bf16[4,2,64,768]{3,2,1,0:T(8,128)(2,1)}), bf16[4,2,64,768]{3,2,1,0:T(8,128)(2,1)S(1)}, u32[]{:S(2)}, u32[]{:S(2)}) async-start(bf16[4,2,64,768]{3,2,1,0:T(8,128)(2,1)} %bitcast.44), calls=%async_computation.6 | async-start | bytes 1572864 | tf_op jit(solution)/shard_map/all_to_all | solution.py:389
  178.4 1.9 collective-permute-start.10
  180.3 5.5 %collective-permute-start.12 = (bf16[384,128]{1,0:T(8,128)(2,1)S(1)}, bf16[384,128]{1,0:T(8,128)(2,1)S(1)}, u32[]{:S(2)}, u32[]{:S(2)}) collective-permute-start(bf16[384,128]{1,0:T(8,128)(2,1)S(1)} %get-tuple-element.37), channel_id=1, source_target_pairs={{0,384},{64,448},{128,0},{192,64},{256,128},{320,192},{384,256},{4... | collective-permute-start | bytes 294920 | tf_op jit(solution)/shard_map/ppermute | solution.py:252
  185.8 1.5 collective-permute-done.10
  187.3 0.9 collective-permute-done.12
  188.3 4.4 %collective-permute-start.11 = (bf16[768,128]{1,0:T(8,128)(2,1)S(1)}, bf16[768,128]{1,0:T(8,128)(2,1)S(1)}, u32[]{:S(2)}, u32[]{:S(2)}) collective-permute-start(bf16[768,128]{1,0:T(8,128)(2,1)S(1)} %get-tuple-element.34), channel_id=1, source_target_pairs={{0,128},{64,192},{128,256},{192,320},{256,384},{320,448},{384,0},{... | collective-permute-start | bytes 589832 | tf_op jit(solution)/shard_map/ppermute | solution.py:252
  192.7 3.0 %collective-permute-start.13 = (bf16[768,128]{1,0:T(8,128)(2,1)S(1)}, bf16[768,128]{1,0:T(8,128)(2,1)S(1)}, u32[]{:S(2)}, u32[]{:S(2)}) collective-permute-start(bf16[768,128]{1,0:T(8,128)(2,1)S(1)} %get-tuple-element.35), channel_id=1, source_target_pairs={{0,384},{64,448},{128,0},{192,64},{256,128},{320,192},{384,256},{4... | collective-permute-start | bytes 589832 | tf_op jit(solution)/shard_map/ppermute | solution.py:252
  195.9 0.7 copy.22
  196.6 4.0 %all-to-all-start.7 = ((bf16[8,2,8,768]{3,2,1,0:T(8,128)(2,1)}), bf16[8,2,8,768]{3,2,1,0:T(8,128)(2,1)S(1)}, u32[]{:S(2)}, u32[]{:S(2)}) async-start(bf16[8,2,8,768]{3,2,1,0:T(8,128)(2,1)} %copy.22), calls=%async_computation.7 | async-start | bytes 393216 | tf_op jit(solution)/shard_map/all_to_all | solution.py:391
  200.5 1.2 collective-permute-done.11
  201.7 1.8 collective-permute-done.13
  203.7 0.8 copy.25
  204.5 4.8 %all-to-all-done.7 = bf16[8,2,8,768]{3,2,1,0:T(8,128)(2,1)S(1)} async-done(((bf16[8,2,8,768]{3,2,1,0:T(8,128)(2,1)}), bf16[8,2,8,768]{3,2,1,0:T(8,128)(2,1)S(1)}, u32[]{:S(2)}, u32[]{:S(2)}) %all-to-all-start.7) | async-done | bytes 196640 | tf_op jit(solution)/shard_map/all_to_all | solution.py:391
  209.3 0.6 copy.24
  (34 shorter events, 1.7 us)
Async XLA Ops:
  0.6 0.9 copy-start.2
  1.6 18.3 %copy-start.5 = (bf16[256,2,768]{2,1,0:T(2,128)(2,1)S(1)}, bf16[256,2,768]{2,1,0:T(2,128)(2,1)}, u32[]{:S(2)}) copy-start(bf16[256,2,768]{2,1,0:T(2,128)(2,1)} %param.2) | copy-start | bytes 2359300
  1.7 18.7 %collective-permute-start.2 = (bf16[128,768]{1,0:T(8,128)(2,1)S(1)}, bf16[128,768]{1,0:T(8,128)(2,1)S(1)}, u32[]{:S(2)}, u32[]{:S(2)}) collective-permute-start(bf16[128,768]{1,0:T(8,128)(2,1)S(1)} %shard_map.41.c0), channel_id=1, source_target_pairs={{0,128},{64,192},{128,256},{192,320},{256,384},{320,448},{384,0},{... | collective-permute-start | bytes 589832 | tf_op jit(solution)/shard_map/ppermute | solution.py:252
  6.9 15.4 %collective-permute-start.1 = (bf16[128,768]{1,0:T(8,128)(2,1)S(1)}, bf16[128,768]{1,0:T(8,128)(2,1)S(1)}, u32[]{:S(2)}, u32[]{:S(2)}) collective-permute-start(bf16[128,768]{1,0:T(8,128)(2,1)S(1)} %shard_map.41.c0), channel_id=1, source_target_pairs={{0,384},{64,448},{128,0},{192,64},{256,128},{320,192},{384,256},{4... | collective-permute-start | bytes 589832 | tf_op jit(solution)/shard_map/ppermute | solution.py:252
  11.7 22.7 %collective-permute-start = (bf16[256,2,768]{2,0,1:T(8,128)(2,1)S(1)}, bf16[256,2,768]{2,0,1:T(8,128)(2,1)S(1)}, u32[]{:S(2)}, u32[]{:S(2)}) collective-permute-start(bf16[256,2,768]{2,0,1:T(8,128)(2,1)S(1)} %copy.19), channel_id=1, source_target_pairs={{0,32},{32,0},{1,33},{33,1},{2,34},{34,2},{3,35},{35,3},{4,36},{36... | collective-permute-start | bytes 2359304 | tf_op jit(solution)/shard_map/ppermute | solution.py:252
  20.4 14.6 %collective-permute-start.6 = (bf16[64,768]{1,0:T(8,128)(2,1)S(1)}, bf16[64,768]{1,0:T(8,128)(2,1)S(1)}, u32[]{:S(2)}, u32[]{:S(2)}) collective-permute-start(bf16[64,768]{1,0:T(8,128)(2,1)S(1)} %slice.45), channel_id=1, source_target_pairs={{0,128},{64,192},{128,256},{192,320},{256,384},{320,448},{384,0},{... | collective-permute-start | bytes 294920 | tf_op jit(solution)/shard_map/ppermute | solution.py:252
  22.3 12.6 %collective-permute-start.5 = (bf16[64,768]{1,0:T(8,128)(2,1)S(1)}, bf16[64,768]{1,0:T(8,128)(2,1)S(1)}, u32[]{:S(2)}, u32[]{:S(2)}) collective-permute-start(bf16[64,768]{1,0:T(8,128)(2,1)S(1)} %slice.44), channel_id=1, source_target_pairs={{0,384},{64,448},{128,0},{192,64},{256,128},{320,192},{384,256},{4... | collective-permute-start | bytes 294920 | tf_op jit(solution)/shard_map/ppermute | solution.py:252
  27.9 12.9 %collective-permute-start.4 = (bf16[256,768]{1,0:T(8,128)(2,1)S(1)}, bf16[256,768]{1,0:T(8,128)(2,1)S(1)}, u32[]{:S(2)}, u32[]{:S(2)}) collective-permute-start(bf16[256,768]{1,0:T(8,128)(2,1)S(1)} %get-tuple-element.38), channel_id=1, source_target_pairs={{0,64},{64,128},{128,192},{192,256},{256,320},{320,384},{384,448},... | collective-permute-start | bytes 1179656 | tf_op jit(solution)/shard_map/ppermute | solution.py:252
  29.8 11.9 %collective-permute-start.3 = (bf16[256,768]{1,0:T(8,128)(2,1)S(1)}, bf16[256,768]{1,0:T(8,128)(2,1)S(1)}, u32[]{:S(2)}, u32[]{:S(2)}) collective-permute-start(bf16[256,768]{1,0:T(8,128)(2,1)S(1)} %get-tuple-element.39), channel_id=1, source_target_pairs={{0,448},{64,0},{128,64},{192,128},{256,192},{320,256},{384,320},{4... | collective-permute-start | bytes 1179656 | tf_op jit(solution)/shard_map/ppermute | solution.py:252
  155.5 0.9 copy-start
  156.3 1.3 copy-start.3
  157.7 14.6 %collective-permute-start.7 = (bf16[2,256,768]{2,1,0:T(8,128)(2,1)}, bf16[2,256,768]{2,1,0:T(8,128)(2,1)}, u32[]{:S(2)}, u32[]{:S(2)}) collective-permute-start(bf16[2,256,768]{2,1,0:T(8,128)(2,1)} %get-tuple-element.20), channel_id=1, source_target_pairs={{0,32},{32,0},{1,33},{33,1},{2,34},{34,2},{3,35},{35,3},{4,36},{36... | collective-permute-start | bytes 2359304 | tf_op jit(solution)/shard_map/ppermute | solution.py:252
  160.8 1.6 copy-start.4
  162.4 9.9 %copy-start.1 = (bf16[2,256,768]{2,1,0:T(8,128)(2,1)S(1)}, bf16[2,256,768]{2,1,0:T(8,128)(2,1)}, u32[]{:S(2)}) copy-start(bf16[2,256,768]{2,1,0:T(8,128)(2,1)} %copy-done) | copy-start | bytes 2359300
  165.8 22.3 %collective-permute-start.8 = (bf16[2,768,128]{2,1,0:T(8,128)(2,1)S(1)}, bf16[2,768,128]{2,1,0:T(8,128)(2,1)S(1)}, u32[]{:S(2)}, u32[]{:S(2)}) collective-permute-start(bf16[2,768,128]{2,1,0:T(8,128)(2,1)S(1)} %get-tuple-element.23), channel_id=1, source_target_pairs={{0,64},{64,128},{128,192},{192,256},{256,320},{320,384},{384,448},... | collective-permute-start | bytes 1179656 | tf_op jit(solution)/shard_map/ppermute | solution.py:252
  168.0 20.1 %collective-permute-start.9 = (bf16[2,768,128]{2,1,0:T(8,128)(2,1)S(1)}, bf16[2,768,128]{2,1,0:T(8,128)(2,1)S(1)}, u32[]{:S(2)}, u32[]{:S(2)}) collective-permute-start(bf16[2,768,128]{2,1,0:T(8,128)(2,1)S(1)} %get-tuple-element.24), channel_id=1, source_target_pairs={{0,448},{64,0},{128,64},{192,128},{256,192},{320,256},{384,320},{4... | collective-permute-start | bytes 1179656 | tf_op jit(solution)/shard_map/ppermute | solution.py:252
  174.6 21.1 %all-to-all-start.6 = ((bf16[4,2,64,768]{3,2,1,0:T(8,128)(2,1)}), bf16[4,2,64,768]{3,2,1,0:T(8,128)(2,1)S(1)}, u32[]{:S(2)}, u32[]{:S(2)}) async-start(bf16[4,2,64,768]{3,2,1,0:T(8,128)(2,1)} %bitcast.44), calls=%async_computation.6 | async-start | bytes 1572864 | tf_op jit(solution)/shard_map/all_to_all | solution.py:389
  178.4 8.9 %collective-permute-start.10 = (bf16[384,128]{1,0:T(8,128)(2,1)S(1)}, bf16[384,128]{1,0:T(8,128)(2,1)S(1)}, u32[]{:S(2)}, u32[]{:S(2)}) collective-permute-start(bf16[384,128]{1,0:T(8,128)(2,1)S(1)} %get-tuple-element.36), channel_id=1, source_target_pairs={{0,128},{64,192},{128,256},{192,320},{256,384},{320,448},{384,0},{... | collective-permute-start | bytes 294920 | tf_op jit(solution)/shard_map/ppermute | solution.py:252
  180.3 7.8 %collective-permute-start.12 = (bf16[384,128]{1,0:T(8,128)(2,1)S(1)}, bf16[384,128]{1,0:T(8,128)(2,1)S(1)}, u32[]{:S(2)}, u32[]{:S(2)}) collective-permute-start(bf16[384,128]{1,0:T(8,128)(2,1)S(1)} %get-tuple-element.37), channel_id=1, source_target_pairs={{0,384},{64,448},{128,0},{192,64},{256,128},{320,192},{384,256},{4... | collective-permute-start | bytes 294920 | tf_op jit(solution)/shard_map/ppermute | solution.py:252
  188.3 13.5 %collective-permute-start.11 = (bf16[768,128]{1,0:T(8,128)(2,1)S(1)}, bf16[768,128]{1,0:T(8,128)(2,1)S(1)}, u32[]{:S(2)}, u32[]{:S(2)}) collective-permute-start(bf16[768,128]{1,0:T(8,128)(2,1)S(1)} %get-tuple-element.34), channel_id=1, source_target_pairs={{0,128},{64,192},{128,256},{192,320},{256,384},{320,448},{384,0},{... | collective-permute-start | bytes 589832 | tf_op jit(solution)/shard_map/ppermute | solution.py:252
  192.7 10.8 %collective-permute-start.13 = (bf16[768,128]{1,0:T(8,128)(2,1)S(1)}, bf16[768,128]{1,0:T(8,128)(2,1)S(1)}, u32[]{:S(2)}, u32[]{:S(2)}) collective-permute-start(bf16[768,128]{1,0:T(8,128)(2,1)S(1)} %get-tuple-element.35), channel_id=1, source_target_pairs={{0,384},{64,448},{128,0},{192,64},{256,128},{320,192},{384,256},{4... | collective-permute-start | bytes 589832 | tf_op jit(solution)/shard_map/ppermute | solution.py:252
  196.6 12.7 %all-to-all-start.7 = ((bf16[8,2,8,768]{3,2,1,0:T(8,128)(2,1)}), bf16[8,2,8,768]{3,2,1,0:T(8,128)(2,1)S(1)}, u32[]{:S(2)}, u32[]{:S(2)}) async-start(bf16[8,2,8,768]{3,2,1,0:T(8,128)(2,1)} %copy.22), calls=%async_computation.7 | async-start | bytes 393216 | tf_op jit(solution)/shard_map/all_to_all | solution.py:391

commit v3 on v1

v3 whole, which is shorter than its diff:
```python
import functools

import jax
import jax.numpy as jnp
from jax import lax
from jax.experimental import pallas as pl
from jax.experimental.pallas import tpu as pltpu
from jax.sharding import Mesh, PartitionSpec as P

PROTOS = 65536
CLIPS = 4096
YS, CORES, XS, ZS = 8, 2, 4, 8
SCALE = 16.0 / 0.1
F32, BF16 = jnp.float32, jnp.bfloat16
LANES = 128
WIDTH = 768
RING = (0, 1, -1, 2, -2, -3, 3, 4)
EARLY = 6
MINE = 256
ROWS = CORES * MINE
SPLIT = EARLY * LANES
COLS = len(RING) * LANES
GROUP = XS * ZS * CORES
VIEWS = 2
BLOCKS = [(view, half) for view in range(VIEWS) for half in range(CORES)]


def call(kernel, ins, outs, scratch=(), flops=4 * ROWS * COLS):
    scalars = 1 if ins[0].dtype == jnp.int32 else 0
    blocks = [pl.BlockSpec(memory_space=pltpu.SMEM)] * scalars
    blocks += [pl.BlockSpec(memory_space=pltpu.VMEM)] * (len(ins) - scalars)
    out_blocks = [pl.BlockSpec(memory_space=pltpu.VMEM)] * len(outs)
    return pl.pallas_call(
        kernel,
        out_shape=[jax.ShapeDtypeStruct(shape, dtype) for shape, dtype in outs],
        in_specs=blocks,
        out_specs=out_blocks,
        scratch_shapes=[pltpu.VMEM(shape, dtype) for shape, dtype in scratch],
        compiler_params=pltpu.CompilerParams(vmem_limit_bytes=16 * 1024 * 1024),
        cost_estimate=pl.CostEstimate(flops=flops, bytes_accessed=2 << 20, transcendentals=0),
    )(*ins)


def turned(block):
    return jnp.sum(block.T, axis=0, keepdims=True)


def down(row):
    return jnp.broadcast_to(row, (LANES, LANES)).T


def lanes_of(slot):
    return slice(slot * LANES, (slot + 1) * LANES)


def clips_of(half):
    return slice(half * MINE, (half + 1) * MINE)


def clip_row(s, view, half, part):
    return view * 4 + jnp.bitwise_xor(s[0], half) * 2 + part


def put_clips(s, view, half, acc, out):
    for part in range(2):
        block = acc[part * LANES : (part + 1) * LANES]
        out[pl.ds(clip_row(s, view, half, part), 1), :] = turned(block)


def clip_scale(s, view, half, ref, scale):
    rows = [ref[pl.ds(clip_row(s, view, half, part), 1), :] for part in range(2)]
    return jnp.concatenate([down(scale / row) for row in rows])


def put_cols(s, view, slot, value, out):
    out[pl.ds(view * YS + s[1 + slot], 1), :] = value


def col_scale(s, view, slot, ref):
    return 1.0 / (PROTOS * ref[pl.ds(view * YS + s[1 + slot], 1), :])


def copies(ref, value):
    ref[...] = jnp.broadcast_to(value[None], ref.shape)


def units(values):
    wide = values.astype(F32)
    norm = lax.rsqrt(jnp.sum(wide * wide, axis=-1, keepdims=True) + 1e-06)
    return (wide * norm).astype(BF16)


def unit_kernel(x_ref, o_ref):
    o_ref[...] = units(x_ref[...])


def rows_kernel(mine_ref, theirs_ref, rows_ref, flat_ref):
    for half, ref in enumerate((mine_ref, theirs_ref)):
        for view in range(VIEWS):
            unit = units(ref[view])
            rows_ref[view, clips_of(half)] = unit
            start = (half * VIEWS + view) * MINE
            flat_ref[:, start : start + MINE] = unit.T


def score(s, slots, rows, pieces, e_ref, centers, part, soft):
    for place, piece in enumerate(pieces):
        centers[lanes_of(place)] = piece[...]
    for view in range(VIEWS):
        acc = None
        for chunk in range(0, len(slots), 2):
            lanes = slice(chunk * LANES, (chunk + 2) * LANES)
            scores = lax.dot_general(
                rows[view], centers[lanes], (((1,), (1,)), ((), ())), preferred_element_type=F32
            )
            likely = jnp.exp(scores * 10.0)
            e_ref[view, :, lanes] = likely
            sums = jnp.sum(likely * likely, axis=0, keepdims=True)
            put_cols(s, view, slots[chunk], sums[:, :LANES], part)
            put_cols(s, view, slots[chunk + 1], sums[:, LANES:], part)
            both = likely[:, :LANES] + likely[:, LANES:]
            acc = both if acc is None else acc + both
        for half in range(CORES):
            put_clips(s, view, half, acc[clips_of(half)], soft)


def early_kernel(s, rows, *refs):
    pieces, (e_ref, part, soft, centers) = refs[:EARLY], refs[EARLY:]
    part[...] = jnp.zeros_like(part)
    score(s, range(EARLY), rows, pieces, e_ref, centers, part, soft)


def late_kernel(s, rows, *refs):
    late = len(RING) - EARLY
    pieces, (early_part, early_soft, e_ref, cols_ref, soft_ref, centers, part, soft) = (
        refs[:late],
        refs[late:],
    )
    part[...] = jnp.zeros_like(part)
    score(s, range(EARLY, len(RING)), rows, pieces, e_ref, centers, part, soft)
    soft_ref[...] = early_soft[...] + soft[...]
    copies(cols_ref, early_part[...] + part[...])


def likely_of(e_refs, view, rows, slot):
    early, late = e_refs
    return early[view, rows, lanes_of(slot)] if slot < EARLY else late[view, rows, lanes_of(slot - EARLY)]


def row_kernel(first, s, early, late, recv_ref, *refs):
    if first:
        soft_ref, out_ref, total, sums = refs
    else:
        out_ref, total, sums = refs
    total[...] = jnp.sum(recv_ref[...], axis=0)
    for view, half in BLOCKS:
        acc = None
        for slot in range(len(RING)):
            likely = likely_of((early, late), view, clips_of(half), slot)
            term = likely * likely * col_scale(s, view, slot, total)
            acc = term if acc is None else acc + term
        put_clips(s, view, half, acc, sums)
    both = sums[...]
    if first:
        both = jnp.concatenate([both, soft_ref[...]]).astype(BF16)
    copies(out_ref, both)


def col_kernel(first, s, early, late, recv_ref, *refs):
    if first:
        out_ref, soft_ref, total, sums = refs
    else:
        out_ref, total, sums = refs
    total[...] = jnp.sum(recv_ref[...].astype(F32), axis=0)
    if first:
        soft_ref[...] = total[8:]
    for view in range(VIEWS):
        scale = [clip_scale(s, view, half, total, 1.0 / CLIPS) for half in range(CORES)]
        scale = jnp.concatenate(scale)
        for slot in range(len(RING)):
            likely = likely_of((early, late), view, slice(None), slot)
            value = jnp.sum(likely * likely * scale, axis=0, keepdims=True)
            put_cols(s, view, slot, value, sums)
    copies(out_ref, sums[...])


def grad_kernel(
    s, early, late, row_ref, col_ref, soft_ref, near_centers, far_centers,
    mine_ref, other_ref, grads, total, clips,
):
    total[...] = jnp.sum(col_ref[...], axis=0)
    clips[...] = jnp.sum(row_ref[...], axis=0)
    for half, ref in ((1, other_ref), (0, mine_ref)):
        rows = clips_of(half)
        code = [clip_scale(s, view, half, clips, SCALE) for view in range(VIEWS)]
        start = half * VIEWS * MINE
        for view in range(VIEWS):
            soft = clip_scale(s, view, half, soft_ref, SCALE)
            for slot in range(len(RING)):
                likely = likely_of((early, late), view, rows, slot)
                swapped = likely_of((early, late), 1 - view, rows, slot)
                scale = col_scale(s, 1 - view, slot, total)
                value = likely * soft - swapped * swapped * code[1 - view] * scale
                place = start + view * MINE
                grads[place : place + MINE, lanes_of(slot)] = value.astype(BF16)
        part = slice(start, start + VIEWS * MINE)
        out = jnp.dot(grads[part, :SPLIT], near_centers[...], preferred_element_type=F32)
        out = out + jnp.dot(grads[part, SPLIT:], far_centers[...], preferred_element_type=F32)
        for place in range(XS * ZS):
            eight = [out[view * MINE + place * 8 : view * MINE + place * 8 + 8] for view in range(2)]
            ref[place] = jnp.concatenate(eight).astype(BF16)


def proto_kernel(flat_ref, grads, *outs):
    for chunk in range(0, len(RING), 2):
        lanes = slice(chunk * LANES, (chunk + 2) * LANES)
        out = jnp.dot(flat_ref[...], grads[:, lanes], preferred_element_type=F32).astype(BF16)
        outs[chunk][...] = out[:, :LANES]
        outs[chunk + 1][...] = out[:, LANES:]


def last_kernel(own, one, two, out_ref):
    total = own[...].astype(F32) + one[...].astype(F32) + two[...].astype(F32)
    out_ref[...] = total.T.astype(BF16)


def shift(part, axis, size, by):
    return lax.ppermute(part, axis, [(i, (i + by) % size) for i in range(size)])


def add(*parts):
    total = parts[0].astype(F32)
    for part in parts[1:]:
        total = total + part.astype(F32)
    return total.astype(BF16)


def swap(part, side):
    low = [(y + side) % YS for y in range(0, YS, 2)]
    pairs = [(y, (y + 1) % YS) for y in low]
    return lax.ppermute(part, "y", pairs + [(b, a) for a, b in pairs])


def gather_y(shard):
    pieces, one, two = [shard], shard, shard
    for _ in range(3):
        one, two = swap(two, 0), swap(one, 1)
        pieces += [one, two]
    return *pieces[:5], two, one, swap(two, 0)


def scatter_y(own, *sums):
    one, two = sums[5], add(sums[4], swap(sums[6], 0))
    for at in (2, 0):
        one, two = add(sums[at], swap(two, 1)), add(sums[at + 1], swap(one, 0))
    (out,) = call(last_kernel, (own, swap(one, 0), swap(two, 1)), [((LANES, WIDTH), BF16)])
    return out


def y_sums(part):
    return lax.all_to_all(part, "y", 0, 0)


def group_sums(part):
    return lax.all_to_all(part, ("x", "z", "core"), 0, 0)


def on_device(embeddings, prototypes):
    y, core = lax.axis_index("y"), lax.axis_index("core")
    sign = 1 - 2 * lax.rem(y, 2)
    places = jnp.stack([core] + [lax.rem(y + sign * d + YS, YS) for d in RING]).astype(jnp.int32)

    (shard,) = call(unit_kernel, (prototypes,), [(prototypes.shape, BF16)])
    mine, shard = lax.optimization_barrier((embeddings.transpose(1, 0, 2), shard))
    theirs = shift(mine, "core", CORES, 1)
    pieces = gather_y(shard)
    rows, flat = call(
        rows_kernel,
        (mine, theirs),
        [((VIEWS, ROWS, WIDTH), BF16), ((WIDTH, VIEWS * ROWS), BF16)],
    )

    cols, rows8, rows16 = ((16, LANES), F32), ((8, LANES), F32), ((16, LANES), F32)
    col_out = ((YS, 16, LANES), F32)
    row_out = ((GROUP, 8, LANES), F32)
    both_out = ((GROUP, 16, LANES), BF16)
    work = 4 * ROWS * WIDTH
    early, col_part, soft, near_centers = call(
        early_kernel, (places, rows, *pieces[:EARLY]),
        [((VIEWS, ROWS, SPLIT), F32), cols, rows8, ((SPLIT, WIDTH), BF16)], (), work * SPLIT,
    )
    late, col_part, soft, far_centers = call(
        late_kernel, (places, rows, *pieces[EARLY:], col_part, soft),
        [((VIEWS, ROWS, COLS - SPLIT), F32), col_out, rows8, ((COLS - SPLIT, WIDTH), BF16)],
        [cols, rows8], work * (COLS - SPLIT),
    )
    col_part = y_sums(col_part)
    (row_part,) = call(
        functools.partial(row_kernel, True), (places, early, late, col_part, soft), [both_out],
        [cols, rows8],
    )
    row_part = group_sums(row_part)
    col_part, soft = call(
        functools.partial(col_kernel, True), (places, early, late, row_part), [col_out, rows8],
        [rows16, cols],
    )
    col_part = y_sums(col_part)
    (row_part,) = call(
        functools.partial(row_kernel, False), (places, early, late, col_part), [row_out], [cols, rows8]
    )
    row_part = group_sums(row_part)
    (col_part,) = call(
        functools.partial(col_kernel, False), (places, early, late, row_part), [col_out], [rows8, cols]
    )
    col_part = y_sums(col_part)
    (row_part,) = call(
        functools.partial(row_kernel, False), (places, early, late, col_part), [row_out], [cols, rows8]
    )
    row_part = group_sums(row_part)

    ge_out = ((XS * ZS, 16, WIDTH), BF16)
    mine, other, grads = call(
        grad_kernel,
        (places, early, late, row_part, col_part, soft, near_centers, far_centers),
        [ge_out, ge_out, ((VIEWS * ROWS, COLS), BF16)], [cols, rows8], work * COLS,
    )
    sums = call(
        proto_kernel, (flat, grads), [((WIDTH, LANES), BF16)] * len(RING), (), work * COLS
    )
    part = add(mine, shift(other, "core", CORES, 1))
    grad_proto = scatter_y(*sums)
    part = lax.all_to_all(part, ("x", "z"), 0, 0)
    part = jnp.sum(part.astype(F32), axis=0).astype(BF16)
    return part.reshape(2, 8, WIDTH).transpose(1, 0, 2), grad_proto


def solution(mesh):
    split = Mesh(mesh.devices.reshape(YS, CORES, XS, ZS), ("y", "core", "x", "z"))
    batch, every = ("y", "core"), ("y", "core", "x", "z")
    return jax.shard_map(
        on_device,
        mesh=split,
        in_specs=(P(batch, None, None), P(every, None)),
        out_specs=(P(every, None, None), P(every, None)),
        check_vma=False,
    )
```

time: 232 us -> 194 us (0.84); the launches traced: 231 us -> 190 us
  waiting for transfers between devices: 54 us -> 25.5 us
  other arithmetic: 26 us -> 1.47 us
  starting transfers between devices: 22.5 us -> 46.8 us
  Pallas kernels: 0 us -> 16.1 us
  between operations: 14.3 us -> 0.92 us
  matrix products: 11.4 us -> 0 us
  blocking collectives: 98.8 us -> 96.2 us
    all_gather x1 -> x0, waiting for transfers between devices: 31.2 us -> none  [on_device(): centers = lax.all_gather(unit_rows(prototypes), 'y', axis=0, tiled=True)]
    ppermute x2 -> x16, starting transfers between devices: 11.1 us -> 41.7 us  [the longest x14 30.5 us: swap(): return lax.ppermute(part, 'y', pairs + [(b, a) for a, b in pairs])]
    ppermute x2 -> x16, waiting for transfers between devices: 3.78 us -> 25.5 us  [the longest x14 25.5 us: swap(): return lax.ppermute(part, 'y', pairs + [(b, a) for a, b in pairs])]
    all_to_all x2 -> x1, waiting for transfers between devices: 19 us -> 0.01 us  [on_device(): part = lax.all_to_all(part, ('x', 'z'), 0, 0)]
    reduce_sum x15 -> x1, other arithmetic: 18.7 us -> 0.12 us  [on_device(): part = jnp.sum(part.astype(F32), axis=0).astype(BF16)]
    pallas_call x0 -> x12, Pallas kernels: none -> 16.1 us  [call(): pl.pallas_call(kernel, out_shape=[jax.ShapeDtypeStruct(shape, dtype) for...]
    dot_general x3 -> x0, matrix products: 11.4 us -> none  [the longest x1 5.16 us: on_device(): lax.dot_general(rows, centers, (((2,), (1,)), ((), ())), preferred_elemen...]
    all_to_all x2 -> x1, starting transfers between devices: 11.1 us -> 5.14 us  [on_device(): part = lax.all_to_all(part, ('x', 'z'), 0, 0)]
  transfers between devices with their start and end apart: 6 -> 17, of which waited for: 5 -> 11; matrix products, arithmetic and copies ran while one was open for 3% -> 1% of each run, Pallas kernels for 0% -> 3%
where the time goes in v3:
time: 194 us; the launch traced here: 190 us
  blocking collectives  96.2 us (50%)
  starting transfers between devices  46.8 us (24%)
  waiting for transfers between devices  25.5 us (13%)
  Pallas kernels  16.1 us (8%)
  local copies, waits for them, and re-layouts  2.85 us (1%)
    all_to_all x3, blocking collectives, group_sums(): return lax.all_to_all(part, ('x', 'z', 'core'), 0, 0)  67.2 us
    ppermute x14, starting transfers between devices, swap(): return lax.ppermute(part, 'y', pairs + [(b, a) for a, b in pairs])  30.5 us
    all_to_all x3, blocking collectives, y_sums(): return lax.all_to_all(part, 'y', 0, 0)  28.9 us
    ppermute x14, waiting for transfers between devices, swap(): return lax.ppermute(part, 'y', pairs + [(b, a) for a, b in pairs])  25.5 us
    pallas_call x12, Pallas kernels, call(): pl.pallas_call(kernel, out_shape=[jax.ShapeDtypeStruct(shape, dtype) for...  16.1 us
    ppermute x2, starting transfers between devices, shift(): return lax.ppermute(part, axis, [(i, (i + by) % size) for i in range(size)])  11.1 us
    all_to_all x1, starting transfers between devices, on_device(): part = lax.all_to_all(part, ('x', 'z'), 0, 0)  5.14 us
  transfers between devices with their start and end apart: 17, of which 11 were waited for; matrix products, arithmetic and copies ran while one was open for 1% of the time, Pallas kernels for 3%

profile of v3, /device:TPU:1, one launch (start us, length us, event | category | flops | bytes accessed | tf_op | source)
XLA Modules:
  0.0 189.8 jit_solution(1254017475128266192)
XLA Ops:
  0.6 0.9 copy-done
  1.7 1.2 copy.8
  2.9 8.8 %collective-permute-start = (bf16[2,256,768]{2,1,0:T(8,128)(2,1)S(1)}, bf16[2,256,768]{2,1,0:T(8,128)(2,1)S(1)}, u32[]{:S(2)}, u32[]{:S(2)}) collective-permute-start(bf16[2,256,768]{2,1,0:T(8,128)(2,1)S(1)} %bitcast.15), channel_id=1, source_target_pairs={{0,32},{32,0},{1,33},{33,1},{2,34},{34,2},{3,35},{35,3},{4,36},{36... | collective-permute-start | bytes 2359304 | tf_op jit(solution)/shard_map/ppermute | solution.py:228
  11.7 1.9 %collective-permute-start.2 = (bf16[128,768]{1,0:T(8,128)(2,1)S(1)}, bf16[128,768]{1,0:T(8,128)(2,1)S(1)}, u32[]{:S(2)}, u32[]{:S(2)}) collective-permute-start(bf16[128,768]{1,0:T(8,128)(2,1)S(1)} %shard_map.41.refs_0_), channel_id=1, source_target_pairs={{64,128},{192,256},{320,384},{448,0},{128,64},{256,192},{384,320},... | collective-permute-start | bytes 589832 | tf_op jit(solution)/shard_map/ppermute | solution.py:241
  13.6 1.9 %collective-permute-start.1 = (bf16[128,768]{1,0:T(8,128)(2,1)S(1)}, bf16[128,768]{1,0:T(8,128)(2,1)S(1)}, u32[]{:S(2)}, u32[]{:S(2)}) collective-permute-start(bf16[128,768]{1,0:T(8,128)(2,1)S(1)} %shard_map.41.refs_0_), channel_id=1, source_target_pairs={{0,64},{128,192},{256,320},{384,448},{64,0},{192,128},{320,256},{4... | collective-permute-start | bytes 589832 | tf_op jit(solution)/shard_map/ppermute | solution.py:241
  15.6 5.8 %collective-permute-done.2.refs_2_ = bf16[128,768]{1,0:T(8,128)(2,1)S(1)} collective-permute-done((bf16[128,768]{1,0:T(8,128)(2,1)S(1)}, bf16[128,768]{1,0:T(8,128)(2,1)S(1)}, u32[]{:S(2)}, u32[]{:S(2)}) %collective-permute-start.2) | collective-permute-done | bytes 196640 | tf_op jit(solution)/shard_map/ppermute | solution.py:241
  21.3 1.9 %collective-permute-start.3 = (bf16[128,768]{1,0:T(8,128)(2,1)S(1)}, bf16[128,768]{1,0:T(8,128)(2,1)S(1)}, u32[]{:S(2)}, u32[]{:S(2)}) collective-permute-start(bf16[128,768]{1,0:T(8,128)(2,1)S(1)} %collective-permute-done.2.refs_2_), channel_id=1, source_target_pairs={{0,64},{128,192},{256,320},{384,448},{64,0},{192,128},{320,256},{4... | collective-permute-start | bytes 589832 | tf_op jit(solution)/shard_map/ppermute | solution.py:241
  23.3 3.0 %collective-permute-start.4 = (bf16[128,768]{1,0:T(8,128)(2,1)S(1)}, bf16[128,768]{1,0:T(8,128)(2,1)S(1)}, u32[]{:S(2)}, u32[]{:S(2)}) collective-permute-start(bf16[128,768]{1,0:T(8,128)(2,1)S(1)} %collective-permute-done.1.refs_1_), channel_id=1, source_target_pairs={{64,128},{192,256},{320,384},{448,0},{128,64},{256,192},{384,320},... | collective-permute-start | bytes 589832 | tf_op jit(solution)/shard_map/ppermute | solution.py:241
  26.3 2.5 %collective-permute-done.3.refs_3_ = bf16[128,768]{1,0:T(8,128)(2,1)S(1)} collective-permute-done((bf16[128,768]{1,0:T(8,128)(2,1)S(1)}, bf16[128,768]{1,0:T(8,128)(2,1)S(1)}, u32[]{:S(2)}, u32[]{:S(2)}) %collective-permute-start.3) | collective-permute-done | bytes 196640 | tf_op jit(solution)/shard_map/ppermute | solution.py:241
  28.8 2.3 %collective-permute-start.5 = (bf16[128,768]{1,0:T(8,128)(2,1)S(1)}, bf16[128,768]{1,0:T(8,128)(2,1)S(1)}, u32[]{:S(2)}, u32[]{:S(2)}) collective-permute-start(bf16[128,768]{1,0:T(8,128)(2,1)S(1)} %collective-permute-done.3.refs_3_), channel_id=1, source_target_pairs={{64,128},{192,256},{320,384},{448,0},{128,64},{256,192},{384,320},... | collective-permute-start | bytes 589832 | tf_op jit(solution)/shard_map/ppermute | solution.py:241
  31.2 0.8 collective-permute-done.4.refs_4_
  32.0 1.9 %collective-permute-start.6 = (bf16[128,768]{1,0:T(8,128)(2,1)S(1)}, bf16[128,768]{1,0:T(8,128)(2,1)S(1)}, u32[]{:S(2)}, u32[]{:S(2)}) collective-permute-start(bf16[128,768]{1,0:T(8,128)(2,1)S(1)} %collective-permute-done.4.refs_4_), channel_id=1, source_target_pairs={{0,64},{128,192},{256,320},{384,448},{64,0},{192,128},{320,256},{4... | collective-permute-start | bytes 589832 | tf_op jit(solution)/shard_map/ppermute | solution.py:241
  33.9 2.5 %collective-permute-done.5.refs_5_ = bf16[128,768]{1,0:T(8,128)(2,1)S(1)} collective-permute-done((bf16[128,768]{1,0:T(8,128)(2,1)S(1)}, bf16[128,768]{1,0:T(8,128)(2,1)S(1)}, u32[]{:S(2)}, u32[]{:S(2)}) %collective-permute-start.5) | collective-permute-done | bytes 196640 | tf_op jit(solution)/shard_map/ppermute | solution.py:241
  36.5 1.9 %collective-permute-start.7 = (bf16[128,768]{1,0:T(8,128)(2,1)S(1)}, bf16[128,768]{1,0:T(8,128)(2,1)S(1)}, u32[]{:S(2)}, u32[]{:S(2)}) collective-permute-start(bf16[128,768]{1,0:T(8,128)(2,1)S(1)} %collective-permute-done.5.refs_5_), channel_id=1, source_target_pairs={{0,64},{128,192},{256,320},{384,448},{64,0},{192,128},{320,256},{4... | collective-permute-start | bytes 589832 | tf_op jit(solution)/shard_map/ppermute | solution.py:241
  38.5 0.9 shard_map.42
  39.4 2.2 %shard_map.43 = (f32[2,512,768]{2,1,0:T(8,128)S(1)}, f32[16,128]{1,0:T(8,128)S(1)}, f32[8,128]{1,0:T(8,128)S(1)}, bf16[768,768]{1,0:T(8,128)(2,1)S(1)}) custom-call(s32[9]{0:T(128)S(1)} %stack.39.s, bf16[2,512,768]{2,1,0:T(8,128)(2,1)S(1)} %get-tuple-element.28.rows, bf16[128,768]{1,0:T(8,128)(2,1)S(1)} %shard_map.41.refs_0_, ...), custom_call_target="tpu_custom_call" | custom-call | flops 1207959552 | bytes 2097152 | tf_op jit(solution)/shard_map/pallas_call | solution.py:33
  41.6 1.2 collective-permute-done.7.refs_1_
  42.9 1.3 shard_map.44
  44.2 9.8 %all_to_all.35.recv_ref = f32[8,16,128]{2,1,0:T(8,128)S(1)} all-to-all(f32[8,16,128]{2,1,0:T(8,128)S(1)} %get-tuple-element.34), channel_id=1, replica_groups=mesh['y'=8,'core'=2,'x'=4,'z'=8] {'y'}, dimensions={0} | all-to-all | bytes 131072 | tf_op jit(solution)/shard_map/all_to_all | solution.py:261
  54.0 1.1 shard_map.45
  55.1 29.2 %all_to_all.36.recv_ref = bf16[64,16,128]{2,1,0:T(8,128)(2,1)S(1)} all-to-all(bf16[64,16,128]{2,1,0:T(8,128)(2,1)S(1)} %shard_map.45), channel_id=1, replica_groups=mesh['y'=8,'core'=2,'x'=4,'z'=8] {'x','z','core'}, dimensions={0} | all-to-all | bytes 524288 | tf_op jit(solution)/shard_map/all_to_all | solution.py:265
  84.3 1.1 shard_map.46
  85.4 9.6 %all_to_all.37.recv_ref = f32[8,16,128]{2,1,0:T(8,128)S(1)} all-to-all(f32[8,16,128]{2,1,0:T(8,128)S(1)} %get-tuple-element.36), channel_id=1, replica_groups=mesh['y'=8,'core'=2,'x'=4,'z'=8] {'y'}, dimensions={0} | all-to-all | bytes 131072 | tf_op jit(solution)/shard_map/all_to_all | solution.py:261
  95.0 1.1 shard_map.47
  96.1 19.0 %all_to_all.38.recv_ref = f32[64,8,128]{2,1,0:T(8,128)S(1)} all-to-all(f32[64,8,128]{2,1,0:T(8,128)S(1)} %shard_map.47), channel_id=1, replica_groups=mesh['y'=8,'core'=2,'x'=4,'z'=8] {'x','z','core'}, dimensions={0} | all-to-all | bytes 524288 | tf_op jit(solution)/shard_map/all_to_all | solution.py:265
  115.1 1.1 shard_map.48
  116.3 9.6 %all_to_all.39.recv_ref.col_ref = f32[8,16,128]{2,1,0:T(8,128)S(1)} all-to-all(f32[8,16,128]{2,1,0:T(8,128)S(1)} %shard_map.48), channel_id=1, replica_groups=mesh['y'=8,'core'=2,'x'=4,'z'=8] {'y'}, dimensions={0} | all-to-all | bytes 131072 | tf_op jit(solution)/shard_map/all_to_all | solution.py:261
  125.8 1.1 shard_map.49
  126.9 19.0 %all_to_all.40.row_ref = f32[64,8,128]{2,1,0:T(8,128)S(1)} all-to-all(f32[64,8,128]{2,1,0:T(8,128)S(1)} %shard_map.49), channel_id=1, replica_groups=mesh['y'=8,'core'=2,'x'=4,'z'=8] {'x','z','core'}, dimensions={0} | all-to-all | bytes 524288 | tf_op jit(solution)/shard_map/all_to_all | solution.py:265
  145.9 3.4 %shard_map.50 = (bf16[32,16,768]{2,1,0:T(8,128)(2,1)S(1)}, bf16[32,16,768]{2,1,0:T(8,128)(2,1)S(1)}, bf16[1024,1024]{1,0:T(8,128)(2,1)S(1)}) custom-call(s32[9]{0:T(128)S(1)} %stack.39.s, f32[2,512,768]{2,1,0:T(8,128)S(1)} %get-tuple-element.30.early, f32[2,512,256]{2,1,0:T(8,128)S(1)} %get-tuple-element.33.late, f32[64,8,128]{2,1,0:T(8,128)S(1)} %all_to_all.40.row_ref, ...), custom_call_target="tpu_custom_call" | custom-call | flops 1610612736 | bytes 2097152 | tf_op jit(solution)/shard_map/pallas_call | solution.py:33
  149.3 2.4 %collective-permute-start.8 = (bf16[32,16,768]{2,1,0:T(8,128)(2,1)S(1)}, bf16[32,16,768]{2,1,0:T(8,128)(2,1)S(1)}, u32[]{:S(2)}, u32[]{:S(2)}) collective-permute-start(bf16[32,16,768]{2,1,0:T(8,128)(2,1)S(1)} %get-tuple-element.41), channel_id=1, source_target_pairs={{0,32},{32,0},{1,33},{33,1},{2,34},{34,2},{3,35},{35,3},{4,36},{36... | collective-permute-start | bytes 2359304 | tf_op jit(solution)/shard_map/ppermute | solution.py:228
  151.7 1.8 shard_map.51
  153.5 2.2 %collective-permute-start.12 = (bf16[768,128]{1,0:T(8,128)(2,1)S(1)}, bf16[768,128]{1,0:T(8,128)(2,1)S(1)}, u32[]{:S(2)}, u32[]{:S(2)}) collective-permute-start(bf16[768,128]{1,0:T(8,128)(2,1)S(1)} %get-tuple-element.51), channel_id=1, source_target_pairs={{0,64},{128,192},{256,320},{384,448},{64,0},{192,128},{320,256},{4... | collective-permute-start | bytes 589832 | tf_op jit(solution)/shard_map/ppermute | solution.py:241
  155.7 1.1 add_convert_fusion
  156.8 5.1 %all-to-all-start.6 = ((bf16[32,16,768]{2,1,0:T(8,128)(2,1)}), bf16[32,16,768]{2,1,0:T(8,128)(2,1)S(1)}, u32[]{:S(2)}, u32[]{:S(2)}) async-start(bf16[32,16,768]{2,1,0:T(8,128)(2,1)} %add_convert_fusion), calls=%async_computation.6 | async-start | bytes 1572864 | tf_op jit(solution)/shard_map/all_to_all | solution.py:332
  161.9 3.1 %collective-permute-start.9 = (bf16[768,128]{1,0:T(8,128)(2,1)S(1)}, bf16[768,128]{1,0:T(8,128)(2,1)S(1)}, u32[]{:S(2)}, u32[]{:S(2)}) collective-permute-start(bf16[768,128]{1,0:T(8,128)(2,1)S(1)} %get-tuple-element.47), channel_id=1, source_target_pairs={{0,64},{128,192},{256,320},{384,448},{64,0},{192,128},{320,256},{4... | collective-permute-start | bytes 589832 | tf_op jit(solution)/shard_map/ppermute | solution.py:241
  165.1 1.9 %collective-permute-start.13 = (bf16[768,128]{1,0:T(8,128)(2,1)S(1)}, bf16[768,128]{1,0:T(8,128)(2,1)S(1)}, u32[]{:S(2)}, u32[]{:S(2)}) collective-permute-start(bf16[768,128]{1,0:T(8,128)(2,1)S(1)} %add_convert_fusion.3), channel_id=1, source_target_pairs={{64,128},{192,256},{320,384},{448,0},{128,64},{256,192},{384,320},... | collective-permute-start | bytes 589832 | tf_op jit(solution)/shard_map/ppermute | solution.py:241
  167.0 2.7 %collective-permute-done.9 = bf16[768,128]{1,0:T(8,128)(2,1)S(1)} collective-permute-done((bf16[768,128]{1,0:T(8,128)(2,1)S(1)}, bf16[768,128]{1,0:T(8,128)(2,1)S(1)}, u32[]{:S(2)}, u32[]{:S(2)}) %collective-permute-start.9) | collective-permute-done | bytes 196640 | tf_op jit(solution)/shard_map/ppermute | solution.py:241
  169.8 2.0 %collective-permute-start.10 = (bf16[768,128]{1,0:T(8,128)(2,1)S(1)}, bf16[768,128]{1,0:T(8,128)(2,1)S(1)}, u32[]{:S(2)}, u32[]{:S(2)}) collective-permute-start(bf16[768,128]{1,0:T(8,128)(2,1)S(1)} %add_convert_fusion.5), channel_id=1, source_target_pairs={{64,128},{192,256},{320,384},{448,0},{128,64},{256,192},{384,320},... | collective-permute-start | bytes 589832 | tf_op jit(solution)/shard_map/ppermute | solution.py:241
  171.8 2.0 %collective-permute-done.13 = bf16[768,128]{1,0:T(8,128)(2,1)S(1)} collective-permute-done((bf16[768,128]{1,0:T(8,128)(2,1)S(1)}, bf16[768,128]{1,0:T(8,128)(2,1)S(1)}, u32[]{:S(2)}, u32[]{:S(2)}) %collective-permute-start.13) | collective-permute-done | bytes 196640 | tf_op jit(solution)/shard_map/ppermute | solution.py:241
  173.8 1.9 %collective-permute-start.14 = (bf16[768,128]{1,0:T(8,128)(2,1)S(1)}, bf16[768,128]{1,0:T(8,128)(2,1)S(1)}, u32[]{:S(2)}, u32[]{:S(2)}) collective-permute-start(bf16[768,128]{1,0:T(8,128)(2,1)S(1)} %add_convert_fusion.2), channel_id=1, source_target_pairs={{0,64},{128,192},{256,320},{384,448},{64,0},{192,128},{320,256},{4... | collective-permute-start | bytes 589832 | tf_op jit(solution)/shard_map/ppermute | solution.py:241
  175.8 2.1 %collective-permute-done.10 = bf16[768,128]{1,0:T(8,128)(2,1)S(1)} collective-permute-done((bf16[768,128]{1,0:T(8,128)(2,1)S(1)}, bf16[768,128]{1,0:T(8,128)(2,1)S(1)}, u32[]{:S(2)}, u32[]{:S(2)}) %collective-permute-start.10) | collective-permute-done | bytes 196640 | tf_op jit(solution)/shard_map/ppermute | solution.py:241
  177.9 1.9 %collective-permute-start.11 = (bf16[768,128]{1,0:T(8,128)(2,1)S(1)}, bf16[768,128]{1,0:T(8,128)(2,1)S(1)}, u32[]{:S(2)}, u32[]{:S(2)}) collective-permute-start(bf16[768,128]{1,0:T(8,128)(2,1)S(1)} %add_convert_fusion.4), channel_id=1, source_target_pairs={{0,64},{128,192},{256,320},{384,448},{64,0},{192,128},{320,256},{4... | collective-permute-start | bytes 589832 | tf_op jit(solution)/shard_map/ppermute | solution.py:241
  179.9 0.7 collective-permute-done.14
  180.6 2.5 %collective-permute-start.15 = (bf16[768,128]{1,0:T(8,128)(2,1)S(1)}, bf16[768,128]{1,0:T(8,128)(2,1)S(1)}, u32[]{:S(2)}, u32[]{:S(2)}) collective-permute-start(bf16[768,128]{1,0:T(8,128)(2,1)S(1)} %add_convert_fusion.1), channel_id=1, source_target_pairs={{64,128},{192,256},{320,384},{448,0},{128,64},{256,192},{384,320},... | collective-permute-start | bytes 589832 | tf_op jit(solution)/shard_map/ppermute | solution.py:241
  183.1 1.7 collective-permute-done.11.one
  184.9 3.4 %collective-permute-done.15.two = bf16[768,128]{1,0:T(8,128)(2,1)S(1)} collective-permute-done((bf16[768,128]{1,0:T(8,128)(2,1)S(1)}, bf16[768,128]{1,0:T(8,128)(2,1)S(1)}, u32[]{:S(2)}, u32[]{:S(2)}) %collective-permute-start.15) | collective-permute-done | bytes 196640 | tf_op jit(solution)/shard_map/ppermute | solution.py:241
  188.2 0.8 shard_map.52
  (16 shorter events, 1.2 us)
Async XLA Ops:
  0.6 0.9 copy-start
  2.9 35.6 %collective-permute-start = (bf16[2,256,768]{2,1,0:T(8,128)(2,1)S(1)}, bf16[2,256,768]{2,1,0:T(8,128)(2,1)S(1)}, u32[]{:S(2)}, u32[]{:S(2)}) collective-permute-start(bf16[2,256,768]{2,1,0:T(8,128)(2,1)S(1)} %bitcast.15), channel_id=1, source_target_pairs={{0,32},{32,0},{1,33},{33,1},{2,34},{34,2},{3,35},{35,3},{4,36},{36... | collective-permute-start | bytes 2359304 | tf_op jit(solution)/shard_map/ppermute | solution.py:228
  11.7 9.6 %collective-permute-start.2 = (bf16[128,768]{1,0:T(8,128)(2,1)S(1)}, bf16[128,768]{1,0:T(8,128)(2,1)S(1)}, u32[]{:S(2)}, u32[]{:S(2)}) collective-permute-start(bf16[128,768]{1,0:T(8,128)(2,1)S(1)} %shard_map.41.refs_0_), channel_id=1, source_target_pairs={{64,128},{192,256},{320,384},{448,0},{128,64},{256,192},{384,320},... | collective-permute-start | bytes 589832 | tf_op jit(solution)/shard_map/ppermute | solution.py:241
  13.6 9.6 %collective-permute-start.1 = (bf16[128,768]{1,0:T(8,128)(2,1)S(1)}, bf16[128,768]{1,0:T(8,128)(2,1)S(1)}, u32[]{:S(2)}, u32[]{:S(2)}) collective-permute-start(bf16[128,768]{1,0:T(8,128)(2,1)S(1)} %shard_map.41.refs_0_), channel_id=1, source_target_pairs={{0,64},{128,192},{256,320},{384,448},{64,0},{192,128},{320,256},{4... | collective-permute-start | bytes 589832 | tf_op jit(solution)/shard_map/ppermute | solution.py:241
  21.3 7.5 %collective-permute-start.3 = (bf16[128,768]{1,0:T(8,128)(2,1)S(1)}, bf16[128,768]{1,0:T(8,128)(2,1)S(1)}, u32[]{:S(2)}, u32[]{:S(2)}) collective-permute-start(bf16[128,768]{1,0:T(8,128)(2,1)S(1)} %collective-permute-done.2.refs_2_), channel_id=1, source_target_pairs={{0,64},{128,192},{256,320},{384,448},{64,0},{192,128},{320,256},{4... | collective-permute-start | bytes 589832 | tf_op jit(solution)/shard_map/ppermute | solution.py:241
  23.3 8.7 %collective-permute-start.4 = (bf16[128,768]{1,0:T(8,128)(2,1)S(1)}, bf16[128,768]{1,0:T(8,128)(2,1)S(1)}, u32[]{:S(2)}, u32[]{:S(2)}) collective-permute-start(bf16[128,768]{1,0:T(8,128)(2,1)S(1)} %collective-permute-done.1.refs_1_), channel_id=1, source_target_pairs={{64,128},{192,256},{320,384},{448,0},{128,64},{256,192},{384,320},... | collective-permute-start | bytes 589832 | tf_op jit(solution)/shard_map/ppermute | solution.py:241
  28.8 7.6 %collective-permute-start.5 = (bf16[128,768]{1,0:T(8,128)(2,1)S(1)}, bf16[128,768]{1,0:T(8,128)(2,1)S(1)}, u32[]{:S(2)}, u32[]{:S(2)}) collective-permute-start(bf16[128,768]{1,0:T(8,128)(2,1)S(1)} %collective-permute-done.3.refs_3_), channel_id=1, source_target_pairs={{64,128},{192,256},{320,384},{448,0},{128,64},{256,192},{384,320},... | collective-permute-start | bytes 589832 | tf_op jit(solution)/shard_map/ppermute | solution.py:241
  32.0 9.6 %collective-permute-start.6 = (bf16[128,768]{1,0:T(8,128)(2,1)S(1)}, bf16[128,768]{1,0:T(8,128)(2,1)S(1)}, u32[]{:S(2)}, u32[]{:S(2)}) collective-permute-start(bf16[128,768]{1,0:T(8,128)(2,1)S(1)} %collective-permute-done.4.refs_4_), channel_id=1, source_target_pairs={{0,64},{128,192},{256,320},{384,448},{64,0},{192,128},{320,256},{4... | collective-permute-start | bytes 589832 | tf_op jit(solution)/shard_map/ppermute | solution.py:241
  36.5 6.4 %collective-permute-start.7 = (bf16[128,768]{1,0:T(8,128)(2,1)S(1)}, bf16[128,768]{1,0:T(8,128)(2,1)S(1)}, u32[]{:S(2)}, u32[]{:S(2)}) collective-permute-start(bf16[128,768]{1,0:T(8,128)(2,1)S(1)} %collective-permute-done.5.refs_5_), channel_id=1, source_target_pairs={{0,64},{128,192},{256,320},{384,448},{64,0},{192,128},{320,256},{4... | collective-permute-start | bytes 589832 | tf_op jit(solution)/shard_map/ppermute | solution.py:241
  149.3 6.4 %collective-permute-start.8 = (bf16[32,16,768]{2,1,0:T(8,128)(2,1)S(1)}, bf16[32,16,768]{2,1,0:T(8,128)(2,1)S(1)}, u32[]{:S(2)}, u32[]{:S(2)}) collective-permute-start(bf16[32,16,768]{2,1,0:T(8,128)(2,1)S(1)} %get-tuple-element.41), channel_id=1, source_target_pairs={{0,32},{32,0},{1,33},{33,1},{2,34},{34,2},{3,35},{35,3},{4,36},{36... | collective-permute-start | bytes 2359304 | tf_op jit(solution)/shard_map/ppermute | solution.py:228
  153.5 11.5 %collective-permute-start.12 = (bf16[768,128]{1,0:T(8,128)(2,1)S(1)}, bf16[768,128]{1,0:T(8,128)(2,1)S(1)}, u32[]{:S(2)}, u32[]{:S(2)}) collective-permute-start(bf16[768,128]{1,0:T(8,128)(2,1)S(1)} %get-tuple-element.51), channel_id=1, source_target_pairs={{0,64},{128,192},{256,320},{384,448},{64,0},{192,128},{320,256},{4... | collective-permute-start | bytes 589832 | tf_op jit(solution)/shard_map/ppermute | solution.py:241
  156.8 32.3 %all-to-all-start.6 = ((bf16[32,16,768]{2,1,0:T(8,128)(2,1)}), bf16[32,16,768]{2,1,0:T(8,128)(2,1)S(1)}, u32[]{:S(2)}, u32[]{:S(2)}) async-start(bf16[32,16,768]{2,1,0:T(8,128)(2,1)} %add_convert_fusion), calls=%async_computation.6 | async-start | bytes 1572864 | tf_op jit(solution)/shard_map/all_to_all | solution.py:332
  161.9 7.8 %collective-permute-start.9 = (bf16[768,128]{1,0:T(8,128)(2,1)S(1)}, bf16[768,128]{1,0:T(8,128)(2,1)S(1)}, u32[]{:S(2)}, u32[]{:S(2)}) collective-permute-start(bf16[768,128]{1,0:T(8,128)(2,1)S(1)} %get-tuple-element.47), channel_id=1, source_target_pairs={{0,64},{128,192},{256,320},{384,448},{64,0},{192,128},{320,256},{4... | collective-permute-start | bytes 589832 | tf_op jit(solution)/shard_map/ppermute | solution.py:241
  165.1 8.7 %collective-permute-start.13 = (bf16[768,128]{1,0:T(8,128)(2,1)S(1)}, bf16[768,128]{1,0:T(8,128)(2,1)S(1)}, u32[]{:S(2)}, u32[]{:S(2)}) collective-permute-start(bf16[768,128]{1,0:T(8,128)(2,1)S(1)} %add_convert_fusion.3), channel_id=1, source_target_pairs={{64,128},{192,256},{320,384},{448,0},{128,64},{256,192},{384,320},... | collective-permute-start | bytes 589832 | tf_op jit(solution)/shard_map/ppermute | solution.py:241
  169.8 8.1 %collective-permute-start.10 = (bf16[768,128]{1,0:T(8,128)(2,1)S(1)}, bf16[768,128]{1,0:T(8,128)(2,1)S(1)}, u32[]{:S(2)}, u32[]{:S(2)}) collective-permute-start(bf16[768,128]{1,0:T(8,128)(2,1)S(1)} %add_convert_fusion.5), channel_id=1, source_target_pairs={{64,128},{192,256},{320,384},{448,0},{128,64},{256,192},{384,320},... | collective-permute-start | bytes 589832 | tf_op jit(solution)/shard_map/ppermute | solution.py:241
  173.8 6.7 %collective-permute-start.14 = (bf16[768,128]{1,0:T(8,128)(2,1)S(1)}, bf16[768,128]{1,0:T(8,128)(2,1)S(1)}, u32[]{:S(2)}, u32[]{:S(2)}) collective-permute-start(bf16[768,128]{1,0:T(8,128)(2,1)S(1)} %add_convert_fusion.2), channel_id=1, source_target_pairs={{0,64},{128,192},{256,320},{384,448},{64,0},{192,128},{320,256},{4... | collective-permute-start | bytes 589832 | tf_op jit(solution)/shard_map/ppermute | solution.py:241
  177.9 6.9 %collective-permute-start.11 = (bf16[768,128]{1,0:T(8,128)(2,1)S(1)}, bf16[768,128]{1,0:T(8,128)(2,1)S(1)}, u32[]{:S(2)}, u32[]{:S(2)}) collective-permute-start(bf16[768,128]{1,0:T(8,128)(2,1)S(1)} %add_convert_fusion.4), channel_id=1, source_target_pairs={{0,64},{128,192},{256,320},{384,448},{64,0},{192,128},{320,256},{4... | collective-permute-start | bytes 589832 | tf_op jit(solution)/shard_map/ppermute | solution.py:241
  180.6 7.6 %collective-permute-start.15 = (bf16[768,128]{1,0:T(8,128)(2,1)S(1)}, bf16[768,128]{1,0:T(8,128)(2,1)S(1)}, u32[]{:S(2)}, u32[]{:S(2)}) collective-permute-start(bf16[768,128]{1,0:T(8,128)(2,1)S(1)} %add_convert_fusion.1), channel_id=1, source_target_pairs={{64,128},{192,256},{320,384},{448,0},{128,64},{256,192},{384,320},... | collective-permute-start | bytes 589832 | tf_op jit(solution)/shard_map/ppermute | solution.py:241

commit v4 on v3

--- a/solution.py
+++ b/solution.py
@@ -4,6 +4,7 @@
 import jax.numpy as jnp
 from jax import lax
 from jax.experimental import pallas as pl
+from jax.experimental.layout import Layout, with_layout_constraint
 from jax.experimental.pallas import tpu as pltpu
 from jax.sharding import Mesh, PartitionSpec as P
 
@@ -26,19 +27,21 @@
 
 
 def call(kernel, ins, outs, scratch=(), flops=4 * ROWS * COLS):
-    scalars = 1 if ins[0].dtype == jnp.int32 else 0
-    blocks = [pl.BlockSpec(memory_space=pltpu.SMEM)] * scalars
-    blocks += [pl.BlockSpec(memory_space=pltpu.VMEM)] * (len(ins) - scalars)
-    out_blocks = [pl.BlockSpec(memory_space=pltpu.VMEM)] * len(outs)
     return pl.pallas_call(
         kernel,
         out_shape=[jax.ShapeDtypeStruct(shape, dtype) for shape, dtype in outs],
-        in_specs=blocks,
-        out_specs=out_blocks,
+        in_specs=[pl.BlockSpec(memory_space=pltpu.VMEM)] * len(ins),
+        out_specs=[pl.BlockSpec(memory_space=pltpu.VMEM)] * len(outs),
         scratch_shapes=[pltpu.VMEM(shape, dtype) for shape, dtype in scratch],
         compiler_params=pltpu.CompilerParams(vmem_limit_bytes=16 * 1024 * 1024),
         cost_estimate=pl.CostEstimate(flops=flops, bytes_accessed=2 << 20, transcendentals=0),
     )(*ins)
+
+
+def places():
+    y, core = lax.axis_index("y"), lax.axis_index("core")
+    sign = 1 - 2 * lax.rem(y, 2)
+    return [core] + [lax.rem(y + sign * d + YS, YS) for d in RING]
 
 
 def turned(block):
@@ -124,13 +127,15 @@
             put_clips(s, view, half, acc[clips_of(half)], soft)
 
 
-def early_kernel(s, rows, *refs):
+def early_kernel(rows, *refs):
+    s = places()
     pieces, (e_ref, part, soft, centers) = refs[:EARLY], refs[EARLY:]
     part[...] = jnp.zeros_like(part)
     score(s, range(EARLY), rows, pieces, e_ref, centers, part, soft)
 
 
-def late_kernel(s, rows, *refs):
+def late_kernel(rows, *refs):
+    s = places()
     late = len(RING) - EARLY
     pieces, (early_part, early_soft, e_ref, cols_ref, soft_ref, centers, part, soft) = (
         refs[:late],
@@ -147,7 +152,8 @@
     return early[view, rows, lanes_of(slot)] if slot < EARLY else late[view, rows, lanes_of(slot - EARLY)]
 
 
-def row_kernel(first, s, early, late, recv_ref, *refs):
+def row_kernel(first, early, late, recv_ref, *refs):
+    s = places()
     if first:
         soft_ref, out_ref, total, sums = refs
     else:
@@ -166,7 +172,8 @@
     copies(out_ref, both)
 
 
-def col_kernel(first, s, early, late, recv_ref, *refs):
+def col_kernel(first, early, late, recv_ref, *refs):
+    s = places()
     if first:
         out_ref, soft_ref, total, sums = refs
     else:
@@ -185,9 +192,10 @@
 
 
 def grad_kernel(
-    s, early, late, row_ref, col_ref, soft_ref, near_centers, far_centers,
+    early, late, row_ref, col_ref, soft_ref, near_centers, far_centers,
     mine_ref, other_ref, grads, total, clips,
 ):
+    s = places()
     total[...] = jnp.sum(col_ref[...], axis=0)
     clips[...] = jnp.sum(row_ref[...], axis=0)
     for half, ref in ((1, other_ref), (0, mine_ref)):
@@ -266,72 +274,70 @@
 
 
 def on_device(embeddings, prototypes):
-    y, core = lax.axis_index("y"), lax.axis_index("core")
-    sign = 1 - 2 * lax.rem(y, 2)
-    places = jnp.stack([core] + [lax.rem(y + sign * d + YS, YS) for d in RING]).astype(jnp.int32)
-
     (shard,) = call(unit_kernel, (prototypes,), [(prototypes.shape, BF16)])
-    mine, shard = lax.optimization_barrier((embeddings.transpose(1, 0, 2), shard))
-    theirs = shift(mine, "core", CORES, 1)
+    mine = embeddings.transpose(1, 0, 2)
+    as_given = Layout(major_to_minor=(0, 1, 2))
+    theirs = shift(with_layout_constraint(embeddings, as_given), "core", CORES, 1)
+    theirs = with_layout_constraint(theirs, as_given).transpose(1, 0, 2)
     pieces = gather_y(shard)
     rows, flat = call(
         rows_kernel,
         (mine, theirs),
         [((VIEWS, ROWS, WIDTH), BF16), ((WIDTH, VIEWS * ROWS), BF16)],
     )
-
     cols, rows8, rows16 = ((16, LANES), F32), ((8, LANES), F32), ((16, LANES), F32)
     col_out = ((YS, 16, LANES), F32)
     row_out = ((GROUP, 8, LANES), F32)
     both_out = ((GROUP, 16, LANES), BF16)
     work = 4 * ROWS * WIDTH
     early, col_part, soft, near_centers = call(
-        early_kernel, (places, rows, *pieces[:EARLY]),
+        early_kernel, (rows, *pieces[:EARLY]),
         [((VIEWS, ROWS, SPLIT), F32), cols, rows8, ((SPLIT, WIDTH), BF16)], (), work * SPLIT,
     )
     late, col_part, soft, far_centers = call(
-        late_kernel, (places, rows, *pieces[EARLY:], col_part, soft),
+        late_kernel, (rows, *pieces[EARLY:], col_part, soft),
         [((VIEWS, ROWS, COLS - SPLIT), F32), col_out, rows8, ((COLS - SPLIT, WIDTH), BF16)],
         [cols, rows8], work * (COLS - SPLIT),
     )
     col_part = y_sums(col_part)
     (row_part,) = call(
-        functools.partial(row_kernel, True), (places, early, late, col_part, soft), [both_out],
+        functools.partial(row_kernel, True), (early, late, col_part, soft), [both_out],
         [cols, rows8],
     )
     row_part = group_sums(row_part)
     col_part, soft = call(
-        functools.partial(col_kernel, True), (places, early, late, row_part), [col_out, rows8],
+        functools.partial(col_kernel, True), (early, late, row_part), [col_out, rows8],
         [rows16, cols],
     )
     col_part = y_sums(col_part)
     (row_part,) = call(
-        functools.partial(row_kernel, False), (places, early, late, col_part), [row_out], [cols, rows8]
+        functools.partial(row_kernel, False), (early, late, col_part), [row_out], [cols, rows8]
     )
     row_part = group_sums(row_part)
     (col_part,) = call(
-        functools.partial(col_kernel, False), (places, early, late, row_part), [col_out], [rows8, cols]
+        functools.partial(col_kernel, False), (early, late, row_part), [col_out], [rows8, cols]
     )
     col_part = y_sums(col_part)
     (row_part,) = call(
-        functools.partial(row_kernel, False), (places, early, late, col_part), [row_out], [cols, rows8]
+        functools.partial(row_kernel, False), (early, late, col_part), [row_out], [cols, rows8]
     )
     row_part = group_sums(row_part)
 
     ge_out = ((XS * ZS, 16, WIDTH), BF16)
     mine, other, grads = call(
         grad_kernel,
-        (places, early, late, row_part, col_part, soft, near_centers, far_centers),
+        (early, late, row_part, col_part, soft, near_centers, far_centers),
         [ge_out, ge_out, ((VIEWS * ROWS, COLS), BF16)], [cols, rows8], work * COLS,
     )
     sums = call(
         proto_kernel, (flat, grads), [((WIDTH, LANES), BF16)] * len(RING), (), work * COLS
     )
     part = add(mine, shift(other, "core", CORES, 1))
-    grad_proto = scatter_y(*sums)
     part = lax.all_to_all(part, ("x", "z"), 0, 0)
     part = jnp.sum(part.astype(F32), axis=0).astype(BF16)
-    return part.reshape(2, 8, WIDTH).transpose(1, 0, 2), grad_proto
+    grad_embed = part.reshape(2, 8, WIDTH).transpose(1, 0, 2)
+    own, grad_embed = lax.optimization_barrier((sums[0], grad_embed))
+    return grad_embed, scatter_y(own, *sums[1:])
 
 
 def solution(mesh):

time: 194 us -> 188 us (0.969)
  the two profiles are of different devices: /device:TPU:1 before, /device:TPU:2 now
where the time goes in v4:
time: 188 us; the launch traced here: 187 us
  blocking collectives  96.7 us (51%)
  starting transfers between devices  48.5 us (26%)
  waiting for transfers between devices  24.6 us (13%)
  Pallas kernels  11.9 us (6%)
  local copies, waits for them, and re-layouts  2.84 us (2%)
    all_to_all x3, blocking collectives, group_sums(): return lax.all_to_all(part, ('x', 'z', 'core'), 0, 0)  60.9 us
    ppermute x14, starting transfers between devices, swap(): return lax.ppermute(part, 'y', pairs + [(b, a) for a, b in pairs])  38.6 us
    all_to_all x3, blocking collectives, y_sums(): return lax.all_to_all(part, 'y', 0, 0)  35.9 us
    ppermute x14, waiting for transfers between devices, swap(): return lax.ppermute(part, 'y', pairs + [(b, a) for a, b in pairs])  24.6 us
    pallas_call x12, Pallas kernels, call(): pl.pallas_call(kernel, out_shape=[jax.ShapeDtypeStruct(shape, dtype) for...  11.9 us
    all_to_all x1, starting transfers between devices, on_device(): part = lax.all_to_all(part, ('x', 'z'), 0, 0)  5.93 us
    ppermute x2, starting transfers between devices, shift(): return lax.ppermute(part, axis, [(i, (i + by) % size) for i in range(size)])  3.98 us
  transfers between devices with their start and end apart: 17, of which 10 were waited for; matrix products, arithmetic and copies ran while one was open for 2% of the time, Pallas kernels for 2%

profile of v4, /device:TPU:2, one launch (start us, length us, event | category | flops | bytes accessed | tf_op | source)
XLA Modules:
  0.0 187.0 jit_solution(14016403122094883037)
XLA Ops:
  0.6 1.9 %collective-permute-start = (bf16[256,2,768]{2,1,0:T(2,128)(2,1)}, bf16[256,2,768]{2,1,0:T(2,128)(2,1)S(1)}, u32[]{:S(2)}, u32[]{:S(2)}) collective-permute-start(bf16[256,2,768]{2,1,0:T(2,128)(2,1)} %param.2), channel_id=1, source_target_pairs={{0,32},{32,0},{1,33},{33,1},{2,34},{34,2},{3,35},{35,3},{4,36},{36... | collective-permute-start | bytes 2359304 | tf_op jit(solution)/shard_map/ppermute | solution.py:236
  2.6 0.9 copy-done
  3.6 5.4 %collective-permute-start.2 = (bf16[128,768]{1,0:T(8,128)(2,1)S(1)}, bf16[128,768]{1,0:T(8,128)(2,1)S(1)}, u32[]{:S(2)}, u32[]{:S(2)}) collective-permute-start(bf16[128,768]{1,0:T(8,128)(2,1)S(1)} %shard_map.42.refs_0_), channel_id=1, source_target_pairs={{64,128},{192,256},{320,384},{448,0},{128,64},{256,192},{384,320},... | collective-permute-start | bytes 589832 | tf_op jit(solution)/shard_map/ppermute | solution.py:249
  9.0 1.9 %collective-permute-start.1 = (bf16[128,768]{1,0:T(8,128)(2,1)S(1)}, bf16[128,768]{1,0:T(8,128)(2,1)S(1)}, u32[]{:S(2)}, u32[]{:S(2)}) collective-permute-start(bf16[128,768]{1,0:T(8,128)(2,1)S(1)} %shard_map.42.refs_0_), channel_id=1, source_target_pairs={{0,64},{128,192},{256,320},{384,448},{64,0},{192,128},{320,256},{4... | collective-permute-start | bytes 589832 | tf_op jit(solution)/shard_map/ppermute | solution.py:249
  10.9 3.6 %collective-permute-done.2.refs_2_ = bf16[128,768]{1,0:T(8,128)(2,1)S(1)} collective-permute-done((bf16[128,768]{1,0:T(8,128)(2,1)S(1)}, bf16[128,768]{1,0:T(8,128)(2,1)S(1)}, u32[]{:S(2)}, u32[]{:S(2)}) %collective-permute-start.2) | collective-permute-done | bytes 196640 | tf_op jit(solution)/shard_map/ppermute | solution.py:249
  14.6 1.9 %collective-permute-start.3 = (bf16[128,768]{1,0:T(8,128)(2,1)S(1)}, bf16[128,768]{1,0:T(8,128)(2,1)S(1)}, u32[]{:S(2)}, u32[]{:S(2)}) collective-permute-start(bf16[128,768]{1,0:T(8,128)(2,1)S(1)} %collective-permute-done.2.refs_2_), channel_id=1, source_target_pairs={{0,64},{128,192},{256,320},{384,448},{64,0},{192,128},{320,256},{4... | collective-permute-start | bytes 589832 | tf_op jit(solution)/shard_map/ppermute | solution.py:249
  16.5 1.5 collective-permute-done.1.refs_1_
  17.9 3.5 %collective-permute-start.4 = (bf16[128,768]{1,0:T(8,128)(2,1)S(1)}, bf16[128,768]{1,0:T(8,128)(2,1)S(1)}, u32[]{:S(2)}, u32[]{:S(2)}) collective-permute-start(bf16[128,768]{1,0:T(8,128)(2,1)S(1)} %collective-permute-done.1.refs_1_), channel_id=1, source_target_pairs={{64,128},{192,256},{320,384},{448,0},{128,64},{256,192},{384,320},... | collective-permute-start | bytes 589832 | tf_op jit(solution)/shard_map/ppermute | solution.py:249
  21.5 1.7 collective-permute-done.3.refs_3_
  23.2 4.6 %collective-permute-start.5 = (bf16[128,768]{1,0:T(8,128)(2,1)S(1)}, bf16[128,768]{1,0:T(8,128)(2,1)S(1)}, u32[]{:S(2)}, u32[]{:S(2)}) collective-permute-start(bf16[128,768]{1,0:T(8,128)(2,1)S(1)} %collective-permute-done.3.refs_3_), channel_id=1, source_target_pairs={{64,128},{192,256},{320,384},{448,0},{128,64},{256,192},{384,320},... | collective-permute-start | bytes 589832 | tf_op jit(solution)/shard_map/ppermute | solution.py:249
  27.8 1.9 %collective-permute-start.6 = (bf16[128,768]{1,0:T(8,128)(2,1)S(1)}, bf16[128,768]{1,0:T(8,128)(2,1)S(1)}, u32[]{:S(2)}, u32[]{:S(2)}) collective-permute-start(bf16[128,768]{1,0:T(8,128)(2,1)S(1)} %collective-permute-done.4.refs_4_), channel_id=1, source_target_pairs={{0,64},{128,192},{256,320},{384,448},{64,0},{192,128},{320,256},{4... | collective-permute-start | bytes 589832 | tf_op jit(solution)/shard_map/ppermute | solution.py:249
  29.7 2.4 %collective-permute-done.5.refs_5_ = bf16[128,768]{1,0:T(8,128)(2,1)S(1)} collective-permute-done((bf16[128,768]{1,0:T(8,128)(2,1)S(1)}, bf16[128,768]{1,0:T(8,128)(2,1)S(1)}, u32[]{:S(2)}, u32[]{:S(2)}) %collective-permute-start.5) | collective-permute-done | bytes 196640 | tf_op jit(solution)/shard_map/ppermute | solution.py:249
  32.1 1.9 %collective-permute-start.7 = (bf16[128,768]{1,0:T(8,128)(2,1)S(1)}, bf16[128,768]{1,0:T(8,128)(2,1)S(1)}, u32[]{:S(2)}, u32[]{:S(2)}) collective-permute-start(bf16[128,768]{1,0:T(8,128)(2,1)S(1)} %collective-permute-done.5.refs_5_), channel_id=1, source_target_pairs={{0,64},{128,192},{256,320},{384,448},{64,0},{192,128},{320,256},{4... | collective-permute-start | bytes 589832 | tf_op jit(solution)/shard_map/ppermute | solution.py:249
  34.0 1.2 copy.12
  35.3 0.9 shard_map.41
  36.3 1.7 shard_map.43
  38.0 1.7 collective-permute-done.7.refs_1_
  39.7 0.8 shard_map.44
  40.5 14.4 %all_to_all.35.recv_ref = f32[8,16,128]{2,1,0:T(8,128)S(1)} all-to-all(f32[8,16,128]{2,1,0:T(8,128)S(1)} %get-tuple-element.33), channel_id=1, replica_groups=mesh['y'=8,'core'=2,'x'=4,'z'=8] {'y'}, dimensions={0} | all-to-all | bytes 131072 | tf_op jit(solution)/shard_map/all_to_all | solution.py:269
  54.8 0.6 shard_map.45
  55.4 25.2 %all_to_all.36.recv_ref = bf16[64,16,128]{2,1,0:T(8,128)(2,1)S(1)} all-to-all(bf16[64,16,128]{2,1,0:T(8,128)(2,1)S(1)} %shard_map.45), channel_id=1, replica_groups=mesh['y'=8,'core'=2,'x'=4,'z'=8] {'x','z','core'}, dimensions={0} | all-to-all | bytes 524288 | tf_op jit(solution)/shard_map/all_to_all | solution.py:273
  80.6 0.6 shard_map.46
  81.2 10.8 %all_to_all.37.recv_ref = f32[8,16,128]{2,1,0:T(8,128)S(1)} all-to-all(f32[8,16,128]{2,1,0:T(8,128)S(1)} %get-tuple-element.35), channel_id=1, replica_groups=mesh['y'=8,'core'=2,'x'=4,'z'=8] {'y'}, dimensions={0} | all-to-all | bytes 131072 | tf_op jit(solution)/shard_map/all_to_all | solution.py:269
  92.0 0.6 shard_map.47
  92.5 17.8 %all_to_all.38.recv_ref = f32[64,8,128]{2,1,0:T(8,128)S(1)} all-to-all(f32[64,8,128]{2,1,0:T(8,128)S(1)} %shard_map.47), channel_id=1, replica_groups=mesh['y'=8,'core'=2,'x'=4,'z'=8] {'x','z','core'}, dimensions={0} | all-to-all | bytes 524288 | tf_op jit(solution)/shard_map/all_to_all | solution.py:273
  110.4 0.6 shard_map.48
  111.0 10.8 %all_to_all.39.recv_ref.col_ref = f32[8,16,128]{2,1,0:T(8,128)S(1)} all-to-all(f32[8,16,128]{2,1,0:T(8,128)S(1)} %shard_map.48), channel_id=1, replica_groups=mesh['y'=8,'core'=2,'x'=4,'z'=8] {'y'}, dimensions={0} | all-to-all | bytes 131072 | tf_op jit(solution)/shard_map/all_to_all | solution.py:269
  121.7 0.6 shard_map.49
  122.3 17.8 %all_to_all.40.row_ref = f32[64,8,128]{2,1,0:T(8,128)S(1)} all-to-all(f32[64,8,128]{2,1,0:T(8,128)S(1)} %shard_map.49), channel_id=1, replica_groups=mesh['y'=8,'core'=2,'x'=4,'z'=8] {'x','z','core'}, dimensions={0} | all-to-all | bytes 524288 | tf_op jit(solution)/shard_map/all_to_all | solution.py:273
  140.1 2.8 %shard_map.50 = (bf16[32,16,768]{2,1,0:T(8,128)(2,1)S(1)}, bf16[32,16,768]{2,1,0:T(8,128)(2,1)S(1)}, bf16[1024,1024]{1,0:T(8,128)(2,1)S(1)}) custom-call(f32[2,512,768]{2,1,0:T(8,128)S(1)} %get-tuple-element.29.early, f32[2,512,256]{2,1,0:T(8,128)S(1)} %get-tuple-element.32.late, f32[64,8,128]{2,1,0:T(8,128)S(1)} %all_to_all.40.row_ref, ...), custom_call_target="tpu_custom_call" | custom-call | flops 1610612736 | bytes 2097152 | tf_op jit(solution)/shard_map/pallas_call | solution.py:30
  143.0 2.1 %collective-permute-start.8 = (bf16[32,16,768]{2,1,0:T(8,128)(2,1)S(1)}, bf16[32,16,768]{2,1,0:T(8,128)(2,1)S(1)}, u32[]{:S(2)}, u32[]{:S(2)}) collective-permute-start(bf16[32,16,768]{2,1,0:T(8,128)(2,1)S(1)} %get-tuple-element.42), channel_id=1, source_target_pairs={{0,32},{32,0},{1,33},{33,1},{2,34},{34,2},{3,35},{35,3},{4,36},{36... | collective-permute-start | bytes 2359304 | tf_op jit(solution)/shard_map/ppermute | solution.py:236
  145.0 1.8 shard_map.51
  146.8 2.5 %collective-permute-start.12 = (bf16[768,128]{1,0:T(8,128)(2,1)S(1)}, bf16[768,128]{1,0:T(8,128)(2,1)S(1)}, u32[]{:S(2)}, u32[]{:S(2)}) collective-permute-start(bf16[768,128]{1,0:T(8,128)(2,1)S(1)} %get-tuple-element.51), channel_id=1, source_target_pairs={{0,64},{128,192},{256,320},{384,448},{64,0},{192,128},{320,256},{4... | collective-permute-start | bytes 589832 | tf_op jit(solution)/shard_map/ppermute | solution.py:249
  149.3 1.1 add_convert_fusion
  150.4 5.9 %all-to-all-start.6 = ((bf16[32,16,768]{2,1,0:T(8,128)(2,1)}), bf16[32,16,768]{2,1,0:T(8,128)(2,1)S(1)}, u32[]{:S(2)}, u32[]{:S(2)}) async-start(bf16[32,16,768]{2,1,0:T(8,128)(2,1)} %add_convert_fusion), calls=%async_computation.6 | async-start | bytes 1572864 | tf_op jit(solution)/shard_map/all_to_all | solution.py:336
  156.4 3.4 %collective-permute-start.9 = (bf16[768,128]{1,0:T(8,128)(2,1)S(1)}, bf16[768,128]{1,0:T(8,128)(2,1)S(1)}, u32[]{:S(2)}, u32[]{:S(2)}) collective-permute-start(bf16[768,128]{1,0:T(8,128)(2,1)S(1)} %get-tuple-element.47), channel_id=1, source_target_pairs={{0,64},{128,192},{256,320},{384,448},{64,0},{192,128},{320,256},{4... | collective-permute-start | bytes 589832 | tf_op jit(solution)/shard_map/ppermute | solution.py:249
  159.8 2.1 %collective-permute-start.13 = (bf16[768,128]{1,0:T(8,128)(2,1)S(1)}, bf16[768,128]{1,0:T(8,128)(2,1)S(1)}, u32[]{:S(2)}, u32[]{:S(2)}) collective-permute-start(bf16[768,128]{1,0:T(8,128)(2,1)S(1)} %add_convert_fusion.3), channel_id=1, source_target_pairs={{64,128},{192,256},{320,384},{448,0},{128,64},{256,192},{384,320},... | collective-permute-start | bytes 589832 | tf_op jit(solution)/shard_map/ppermute | solution.py:249
  161.9 2.8 %collective-permute-done.9 = bf16[768,128]{1,0:T(8,128)(2,1)S(1)} collective-permute-done((bf16[768,128]{1,0:T(8,128)(2,1)S(1)}, bf16[768,128]{1,0:T(8,128)(2,1)S(1)}, u32[]{:S(2)}, u32[]{:S(2)}) %collective-permute-start.9) | collective-permute-done | bytes 196640 | tf_op jit(solution)/shard_map/ppermute | solution.py:249
  164.8 2.3 %collective-permute-start.10 = (bf16[768,128]{1,0:T(8,128)(2,1)S(1)}, bf16[768,128]{1,0:T(8,128)(2,1)S(1)}, u32[]{:S(2)}, u32[]{:S(2)}) collective-permute-start(bf16[768,128]{1,0:T(8,128)(2,1)S(1)} %add_convert_fusion.5), channel_id=1, source_target_pairs={{64,128},{192,256},{320,384},{448,0},{128,64},{256,192},{384,320},... | collective-permute-start | bytes 589832 | tf_op jit(solution)/shard_map/ppermute | solution.py:249
  167.1 2.0 %collective-permute-done.13 = bf16[768,128]{1,0:T(8,128)(2,1)S(1)} collective-permute-done((bf16[768,128]{1,0:T(8,128)(2,1)S(1)}, bf16[768,128]{1,0:T(8,128)(2,1)S(1)}, u32[]{:S(2)}, u32[]{:S(2)}) %collective-permute-start.13) | collective-permute-done | bytes 196640 | tf_op jit(solution)/shard_map/ppermute | solution.py:249
  169.2 1.9 %collective-permute-start.14 = (bf16[768,128]{1,0:T(8,128)(2,1)S(1)}, bf16[768,128]{1,0:T(8,128)(2,1)S(1)}, u32[]{:S(2)}, u32[]{:S(2)}) collective-permute-start(bf16[768,128]{1,0:T(8,128)(2,1)S(1)} %add_convert_fusion.2), channel_id=1, source_target_pairs={{0,64},{128,192},{256,320},{384,448},{64,0},{192,128},{320,256},{4... | collective-permute-start | bytes 589832 | tf_op jit(solution)/shard_map/ppermute | solution.py:249
  171.1 2.5 %collective-permute-done.10 = bf16[768,128]{1,0:T(8,128)(2,1)S(1)} collective-permute-done((bf16[768,128]{1,0:T(8,128)(2,1)S(1)}, bf16[768,128]{1,0:T(8,128)(2,1)S(1)}, u32[]{:S(2)}, u32[]{:S(2)}) %collective-permute-start.10) | collective-permute-done | bytes 196640 | tf_op jit(solution)/shard_map/ppermute | solution.py:249
  173.6 2.2 %collective-permute-start.11 = (bf16[768,128]{1,0:T(8,128)(2,1)S(1)}, bf16[768,128]{1,0:T(8,128)(2,1)S(1)}, u32[]{:S(2)}, u32[]{:S(2)}) collective-permute-start(bf16[768,128]{1,0:T(8,128)(2,1)S(1)} %add_convert_fusion.4), channel_id=1, source_target_pairs={{0,64},{128,192},{256,320},{384,448},{64,0},{192,128},{320,256},{4... | collective-permute-start | bytes 589832 | tf_op jit(solution)/shard_map/ppermute | solution.py:249
  175.8 1.6 collective-permute-done.14
  177.4 3.0 %collective-permute-start.15 = (bf16[768,128]{1,0:T(8,128)(2,1)S(1)}, bf16[768,128]{1,0:T(8,128)(2,1)S(1)}, u32[]{:S(2)}, u32[]{:S(2)}) collective-permute-start(bf16[768,128]{1,0:T(8,128)(2,1)S(1)} %add_convert_fusion.1), channel_id=1, source_target_pairs={{64,128},{192,256},{320,384},{448,0},{128,64},{256,192},{384,320},... | collective-permute-start | bytes 589832 | tf_op jit(solution)/shard_map/ppermute | solution.py:249
  180.6 0.6 copy.8
  181.2 5.0 %collective-permute-done.15.two = bf16[768,128]{1,0:T(8,128)(2,1)S(1)} collective-permute-done((bf16[768,128]{1,0:T(8,128)(2,1)S(1)}, bf16[768,128]{1,0:T(8,128)(2,1)S(1)}, u32[]{:S(2)}, u32[]{:S(2)}) %collective-permute-start.15) | collective-permute-done | bytes 196640 | tf_op jit(solution)/shard_map/ppermute | solution.py:249
  186.2 0.8 shard_map.52
  (16 shorter events, 0.6 us)
Async XLA Ops:
  0.6 34.6 %collective-permute-start = (bf16[256,2,768]{2,1,0:T(2,128)(2,1)}, bf16[256,2,768]{2,1,0:T(2,128)(2,1)S(1)}, u32[]{:S(2)}, u32[]{:S(2)}) collective-permute-start(bf16[256,2,768]{2,1,0:T(2,128)(2,1)} %param.2), channel_id=1, source_target_pairs={{0,32},{32,0},{1,33},{33,1},{2,34},{34,2},{3,35},{35,3},{4,36},{36... | collective-permute-start | bytes 2359304 | tf_op jit(solution)/shard_map/ppermute | solution.py:236
  2.6 0.9 copy-start
  3.6 10.9 %collective-permute-start.2 = (bf16[128,768]{1,0:T(8,128)(2,1)S(1)}, bf16[128,768]{1,0:T(8,128)(2,1)S(1)}, u32[]{:S(2)}, u32[]{:S(2)}) collective-permute-start(bf16[128,768]{1,0:T(8,128)(2,1)S(1)} %shard_map.42.refs_0_), channel_id=1, source_target_pairs={{64,128},{192,256},{320,384},{448,0},{128,64},{256,192},{384,320},... | collective-permute-start | bytes 589832 | tf_op jit(solution)/shard_map/ppermute | solution.py:249
  9.0 8.9 %collective-permute-start.1 = (bf16[128,768]{1,0:T(8,128)(2,1)S(1)}, bf16[128,768]{1,0:T(8,128)(2,1)S(1)}, u32[]{:S(2)}, u32[]{:S(2)}) collective-permute-start(bf16[128,768]{1,0:T(8,128)(2,1)S(1)} %shard_map.42.refs_0_), channel_id=1, source_target_pairs={{0,64},{128,192},{256,320},{384,448},{64,0},{192,128},{320,256},{4... | collective-permute-start | bytes 589832 | tf_op jit(solution)/shard_map/ppermute | solution.py:249
  14.6 8.6 %collective-permute-start.3 = (bf16[128,768]{1,0:T(8,128)(2,1)S(1)}, bf16[128,768]{1,0:T(8,128)(2,1)S(1)}, u32[]{:S(2)}, u32[]{:S(2)}) collective-permute-start(bf16[128,768]{1,0:T(8,128)(2,1)S(1)} %collective-permute-done.2.refs_2_), channel_id=1, source_target_pairs={{0,64},{128,192},{256,320},{384,448},{64,0},{192,128},{320,256},{4... | collective-permute-start | bytes 589832 | tf_op jit(solution)/shard_map/ppermute | solution.py:249
  17.9 9.9 %collective-permute-start.4 = (bf16[128,768]{1,0:T(8,128)(2,1)S(1)}, bf16[128,768]{1,0:T(8,128)(2,1)S(1)}, u32[]{:S(2)}, u32[]{:S(2)}) collective-permute-start(bf16[128,768]{1,0:T(8,128)(2,1)S(1)} %collective-permute-done.1.refs_1_), channel_id=1, source_target_pairs={{64,128},{192,256},{320,384},{448,0},{128,64},{256,192},{384,320},... | collective-permute-start | bytes 589832 | tf_op jit(solution)/shard_map/ppermute | solution.py:249
  23.2 9.0 %collective-permute-start.5 = (bf16[128,768]{1,0:T(8,128)(2,1)S(1)}, bf16[128,768]{1,0:T(8,128)(2,1)S(1)}, u32[]{:S(2)}, u32[]{:S(2)}) collective-permute-start(bf16[128,768]{1,0:T(8,128)(2,1)S(1)} %collective-permute-done.3.refs_3_), channel_id=1, source_target_pairs={{64,128},{192,256},{320,384},{448,0},{128,64},{256,192},{384,320},... | collective-permute-start | bytes 589832 | tf_op jit(solution)/shard_map/ppermute | solution.py:249
  27.8 10.2 %collective-permute-start.6 = (bf16[128,768]{1,0:T(8,128)(2,1)S(1)}, bf16[128,768]{1,0:T(8,128)(2,1)S(1)}, u32[]{:S(2)}, u32[]{:S(2)}) collective-permute-start(bf16[128,768]{1,0:T(8,128)(2,1)S(1)} %collective-permute-done.4.refs_4_), channel_id=1, source_target_pairs={{0,64},{128,192},{256,320},{384,448},{64,0},{192,128},{320,256},{4... | collective-permute-start | bytes 589832 | tf_op jit(solution)/shard_map/ppermute | solution.py:249
  32.1 7.6 %collective-permute-start.7 = (bf16[128,768]{1,0:T(8,128)(2,1)S(1)}, bf16[128,768]{1,0:T(8,128)(2,1)S(1)}, u32[]{:S(2)}, u32[]{:S(2)}) collective-permute-start(bf16[128,768]{1,0:T(8,128)(2,1)S(1)} %collective-permute-done.5.refs_5_), channel_id=1, source_target_pairs={{0,64},{128,192},{256,320},{384,448},{64,0},{192,128},{320,256},{4... | collective-permute-start | bytes 589832 | tf_op jit(solution)/shard_map/ppermute | solution.py:249
  143.0 6.4 %collective-permute-start.8 = (bf16[32,16,768]{2,1,0:T(8,128)(2,1)S(1)}, bf16[32,16,768]{2,1,0:T(8,128)(2,1)S(1)}, u32[]{:S(2)}, u32[]{:S(2)}) collective-permute-start(bf16[32,16,768]{2,1,0:T(8,128)(2,1)S(1)} %get-tuple-element.42), channel_id=1, source_target_pairs={{0,32},{32,0},{1,33},{33,1},{2,34},{34,2},{3,35},{35,3},{4,36},{36... | collective-permute-start | bytes 2359304 | tf_op jit(solution)/shard_map/ppermute | solution.py:236
  146.8 12.9 %collective-permute-start.12 = (bf16[768,128]{1,0:T(8,128)(2,1)S(1)}, bf16[768,128]{1,0:T(8,128)(2,1)S(1)}, u32[]{:S(2)}, u32[]{:S(2)}) collective-permute-start(bf16[768,128]{1,0:T(8,128)(2,1)S(1)} %get-tuple-element.51), channel_id=1, source_target_pairs={{0,64},{128,192},{256,320},{384,448},{64,0},{192,128},{320,256},{4... | collective-permute-start | bytes 589832 | tf_op jit(solution)/shard_map/ppermute | solution.py:249
  150.4 30.1 %all-to-all-start.6 = ((bf16[32,16,768]{2,1,0:T(8,128)(2,1)}), bf16[32,16,768]{2,1,0:T(8,128)(2,1)S(1)}, u32[]{:S(2)}, u32[]{:S(2)}) async-start(bf16[32,16,768]{2,1,0:T(8,128)(2,1)} %add_convert_fusion), calls=%async_computation.6 | async-start | bytes 1572864 | tf_op jit(solution)/shard_map/all_to_all | solution.py:336
  156.4 8.4 %collective-permute-start.9 = (bf16[768,128]{1,0:T(8,128)(2,1)S(1)}, bf16[768,128]{1,0:T(8,128)(2,1)S(1)}, u32[]{:S(2)}, u32[]{:S(2)}) collective-permute-start(bf16[768,128]{1,0:T(8,128)(2,1)S(1)} %get-tuple-element.47), channel_id=1, source_target_pairs={{0,64},{128,192},{256,320},{384,448},{64,0},{192,128},{320,256},{4... | collective-permute-start | bytes 589832 | tf_op jit(solution)/shard_map/ppermute | solution.py:249
  159.8 9.3 %collective-permute-start.13 = (bf16[768,128]{1,0:T(8,128)(2,1)S(1)}, bf16[768,128]{1,0:T(8,128)(2,1)S(1)}, u32[]{:S(2)}, u32[]{:S(2)}) collective-permute-start(bf16[768,128]{1,0:T(8,128)(2,1)S(1)} %add_convert_fusion.3), channel_id=1, source_target_pairs={{64,128},{192,256},{320,384},{448,0},{128,64},{256,192},{384,320},... | collective-permute-start | bytes 589832 | tf_op jit(solution)/shard_map/ppermute | solution.py:249
  164.8 8.8 %collective-permute-start.10 = (bf16[768,128]{1,0:T(8,128)(2,1)S(1)}, bf16[768,128]{1,0:T(8,128)(2,1)S(1)}, u32[]{:S(2)}, u32[]{:S(2)}) collective-permute-start(bf16[768,128]{1,0:T(8,128)(2,1)S(1)} %add_convert_fusion.5), channel_id=1, source_target_pairs={{64,128},{192,256},{320,384},{448,0},{128,64},{256,192},{384,320},... | collective-permute-start | bytes 589832 | tf_op jit(solution)/shard_map/ppermute | solution.py:249
  169.2 8.2 %collective-permute-start.14 = (bf16[768,128]{1,0:T(8,128)(2,1)S(1)}, bf16[768,128]{1,0:T(8,128)(2,1)S(1)}, u32[]{:S(2)}, u32[]{:S(2)}) collective-permute-start(bf16[768,128]{1,0:T(8,128)(2,1)S(1)} %add_convert_fusion.2), channel_id=1, source_target_pairs={{0,64},{128,192},{256,320},{384,448},{64,0},{192,128},{320,256},{4... | collective-permute-start | bytes 589832 | tf_op jit(solution)/shard_map/ppermute | solution.py:249
  173.6 7.6 %collective-permute-start.11 = (bf16[768,128]{1,0:T(8,128)(2,1)S(1)}, bf16[768,128]{1,0:T(8,128)(2,1)S(1)}, u32[]{:S(2)}, u32[]{:S(2)}) collective-permute-start(bf16[768,128]{1,0:T(8,128)(2,1)S(1)} %add_convert_fusion.4), channel_id=1, source_target_pairs={{0,64},{128,192},{256,320},{384,448},{64,0},{192,128},{320,256},{4... | collective-permute-start | bytes 589832 | tf_op jit(solution)/shard_map/ppermute | solution.py:249
  177.4 8.8 %collective-permute-start.15 = (bf16[768,128]{1,0:T(8,128)(2,1)S(1)}, bf16[768,128]{1,0:T(8,128)(2,1)S(1)}, u32[]{:S(2)}, u32[]{:S(2)}) collective-permute-start(bf16[768,128]{1,0:T(8,128)(2,1)S(1)} %add_convert_fusion.1), channel_id=1, source_target_pairs={{64,128},{192,256},{320,384},{448,0},{128,64},{256,192},{384,320},... | collective-permute-start | bytes 589832 | tf_op jit(solution)/shard_map/ppermute | solution.py:249

commit v5 on v4

--- a/solution.py
+++ b/solution.py
@@ -15,12 +15,12 @@
 F32, BF16 = jnp.float32, jnp.bfloat16
 LANES = 128
 WIDTH = 768
-RING = (0, 1, -1, 2, -2, -3, 3, 4)
+SLOTS = 8
 EARLY = 6
 MINE = 256
 ROWS = CORES * MINE
 SPLIT = EARLY * LANES
-COLS = len(RING) * LANES
+COLS = SLOTS * LANES
 GROUP = XS * ZS * CORES
 VIEWS = 2
 BLOCKS = [(view, half) for view in range(VIEWS) for half in range(CORES)]
@@ -38,10 +38,15 @@
     )(*ins)
 
 
+def sides():
+    y, core = lax.axis_index("y"), lax.axis_index("core")
+    return 1 - 2 * lax.rem(y + core, 2), 1 - 2 * lax.rem(y // 2 + core, 2)
+
+
 def places():
-    y, core = lax.axis_index("y"), lax.axis_index("core")
-    sign = 1 - 2 * lax.rem(y, 2)
-    return [core] + [lax.rem(y + sign * d + YS, YS) for d in RING]
+    y, (one, two) = lax.axis_index("y"), sides()
+    steps = (0, one, -one, 2 * two, -2 * two, -3 * one, 3 * one, 4)
+    return [lax.axis_index("core")] + [lax.rem(y + step + YS, YS) for step in steps]
 
 
 def turned(block):
@@ -91,10 +96,6 @@
     wide = values.astype(F32)
     norm = lax.rsqrt(jnp.sum(wide * wide, axis=-1, keepdims=True) + 1e-06)
     return (wide * norm).astype(BF16)
-
-
-def unit_kernel(x_ref, o_ref):
-    o_ref[...] = units(x_ref[...])
 
 
 def rows_kernel(mine_ref, theirs_ref, rows_ref, flat_ref):
@@ -108,7 +109,7 @@
 
 def score(s, slots, rows, pieces, e_ref, centers, part, soft):
     for place, piece in enumerate(pieces):
-        centers[lanes_of(place)] = piece[...]
+        centers[lanes_of(place)] = units(piece[...])
     for view in range(VIEWS):
         acc = None
         for chunk in range(0, len(slots), 2):
@@ -136,13 +137,13 @@
 
 def late_kernel(rows, *refs):
     s = places()
-    late = len(RING) - EARLY
+    late = SLOTS - EARLY
     pieces, (early_part, early_soft, e_ref, cols_ref, soft_ref, centers, part, soft) = (
         refs[:late],
         refs[late:],
     )
     part[...] = jnp.zeros_like(part)
-    score(s, range(EARLY, len(RING)), rows, pieces, e_ref, centers, part, soft)
+    score(s, range(EARLY, SLOTS), rows, pieces, e_ref, centers, part, soft)
     soft_ref[...] = early_soft[...] + soft[...]
     copies(cols_ref, early_part[...] + part[...])
 
@@ -161,7 +162,7 @@
     total[...] = jnp.sum(recv_ref[...], axis=0)
     for view, half in BLOCKS:
         acc = None
-        for slot in range(len(RING)):
+        for slot in range(SLOTS):
             likely = likely_of((early, late), view, clips_of(half), slot)
             term = likely * likely * col_scale(s, view, slot, total)
             acc = term if acc is None else acc + term
@@ -184,7 +185,7 @@
     for view in range(VIEWS):
         scale = [clip_scale(s, view, half, total, 1.0 / CLIPS) for half in range(CORES)]
         scale = jnp.concatenate(scale)
-        for slot in range(len(RING)):
+        for slot in range(SLOTS):
             likely = likely_of((early, late), view, slice(None), slot)
             value = jnp.sum(likely * likely * scale, axis=0, keepdims=True)
             put_cols(s, view, slot, value, sums)
@@ -204,7 +205,7 @@
         start = half * VIEWS * MINE
         for view in range(VIEWS):
             soft = clip_scale(s, view, half, soft_ref, SCALE)
-            for slot in range(len(RING)):
+            for slot in range(SLOTS):
                 likely = likely_of((early, late), view, rows, slot)
                 swapped = likely_of((early, late), 1 - view, rows, slot)
                 scale = col_scale(s, 1 - view, slot, total)
@@ -220,15 +221,18 @@
 
 
 def proto_kernel(flat_ref, grads, *outs):
-    for chunk in range(0, len(RING), 2):
+    for chunk in range(0, SLOTS, 2):
         lanes = slice(chunk * LANES, (chunk + 2) * LANES)
         out = jnp.dot(flat_ref[...], grads[:, lanes], preferred_element_type=F32).astype(BF16)
         outs[chunk][...] = out[:, :LANES]
         outs[chunk + 1][...] = out[:, LANES:]
 
 
-def last_kernel(own, one, two, out_ref):
-    total = own[...].astype(F32) + one[...].astype(F32) + two[...].astype(F32)
+def last_kernel(own, *refs):
+    *parts, out_ref = refs
+    total = own[...].astype(F32)
+    for part in parts:
+        total = total + part[...].astype(F32)
     out_ref[...] = total.T.astype(BF16)
 
 
@@ -243,25 +247,33 @@
     return total.astype(BF16)
 
 
-def swap(part, side):
-    low = [(y + side) % YS for y in range(0, YS, 2)]
-    pairs = [(y, (y + 1) % YS) for y in low]
-    return lax.ppermute(part, "y", pairs + [(b, a) for a, b in pairs])
+def swap(part, side, by):
+    pairs = []
+    for core in range(CORES):
+        for y in range(YS):
+            if (y // by) % 2 == (side + core) % 2:
+                one, two = y * CORES + core, (y + by) % YS * CORES + core
+                pairs += [(one, two), (two, one)]
+    return lax.ppermute(part, ("y", "core"), pairs)
 
 
 def gather_y(shard):
-    pieces, one, two = [shard], shard, shard
-    for _ in range(3):
-        one, two = swap(two, 0), swap(one, 1)
-        pieces += [one, two]
-    return *pieces[:5], two, one, swap(two, 0)
-
-
-def scatter_y(own, *sums):
-    one, two = sums[5], add(sums[4], swap(sums[6], 0))
-    for at in (2, 0):
-        one, two = add(sums[at], swap(two, 1)), add(sums[at + 1], swap(one, 0))
-    (out,) = call(last_kernel, (own, swap(one, 0), swap(two, 1)), [((LANES, WIDTH), BF16)])
+    one, two = sides()
+    up1, dn1 = swap(shard, 0, 1), swap(shard, 1, 1)
+    up2, dn2 = swap(shard, 0, 2), swap(shard, 1, 2)
+    ahead, behind = jnp.where(one == two, up2, dn2), jnp.where(one == two, dn2, up2)
+    up3, dn3 = swap(behind, 0, 1), swap(ahead, 1, 1)
+    return shard, up1, dn1, up2, dn2, dn3, up3, swap(dn2, 0, 2)
+
+
+def scatter_y(own, up1, dn1, up2, dn2, dn3, up3, far):
+    one, two = sides()
+    far = swap(far, 0, 2)
+    behind, ahead = swap(up3, 0, 1), swap(dn3, 1, 1)
+    up2 = add(up2, jnp.where(one == two, ahead, behind))
+    dn2 = add(dn2, jnp.where(one == two, behind, ahead), far)
+    parts = swap(up1, 0, 1), swap(dn1, 1, 1), swap(up2, 0, 2), swap(dn2, 1, 2)
+    (out,) = call(last_kernel, (own, *parts), [((LANES, WIDTH), BF16)])
     return out
 
 
@@ -274,12 +286,11 @@
 
 
 def on_device(embeddings, prototypes):
-    (shard,) = call(unit_kernel, (prototypes,), [(prototypes.shape, BF16)])
     mine = embeddings.transpose(1, 0, 2)
     as_given = Layout(major_to_minor=(0, 1, 2))
     theirs = shift(with_layout_constraint(embeddings, as_given), "core", CORES, 1)
     theirs = with_layout_constraint(theirs, as_given).transpose(1, 0, 2)
-    pieces = gather_y(shard)
+    pieces = gather_y(prototypes)
     rows, flat = call(
         rows_kernel,
         (mine, theirs),
@@ -330,9 +341,11 @@
         [ge_out, ge_out, ((VIEWS * ROWS, COLS), BF16)], [cols, rows8], work * COLS,
     )
     sums = call(
-        proto_kernel, (flat, grads), [((WIDTH, LANES), BF16)] * len(RING), (), work * COLS
-    )
-    part = add(mine, shift(other, "core", CORES, 1))
+        proto_kernel, (flat, grads), [((WIDTH, LANES), BF16)] * SLOTS, (), work * COLS
+    )
+    theirs = shift(other, "core", CORES, 1)
+    mine, sums = lax.optimization_barrier((mine, sums))
+    part = add(mine, theirs)
     part = lax.all_to_all(part, ("x", "z"), 0, 0)
     part = jnp.sum(part.astype(F32), axis=0).astype(BF16)
     grad_embed = part.reshape(2, 8, WIDTH).transpose(1, 0, 2)

time: 188 us -> 184 us (0.979)
  the two profiles are of different devices: /device:TPU:2 before, /device:TPU:1 now
where the time goes in v5:
time: 184 us; the launch traced here: 183 us
  blocking collectives  94.5 us (51%)
  starting transfers between devices  55.5 us (30%)
  waiting for transfers between devices  16.9 us (9%)
  Pallas kernels  12.2 us (7%)
  local copies, waits for them, and re-layouts  1.93 us (1%)
    all_to_all x3, blocking collectives, group_sums(): return lax.all_to_all(part, ('x', 'z', 'core'), 0, 0)  64.5 us
    ppermute x14, starting transfers between devices, swap(): return lax.ppermute(part, ('y', 'core'), pairs)  39.3 us
    all_to_all x3, blocking collectives, y_sums(): return lax.all_to_all(part, 'y', 0, 0)  30 us
    ppermute x14, waiting for transfers between devices, swap(): return lax.ppermute(part, ('y', 'core'), pairs)  16.8 us
    pallas_call x11, Pallas kernels, call(): pl.pallas_call(kernel, out_shape=[jax.ShapeDtypeStruct(shape, dtype) for...  12.2 us
    ppermute x2, starting transfers between devices, shift(): return lax.ppermute(part, axis, [(i, (i + by) % size) for i in range(size)])  11.1 us
    all_to_all x1, starting transfers between devices, on_device(): part = lax.all_to_all(part, ('x', 'z'), 0, 0)  5.14 us
  transfers between devices with their start and end apart: 17, of which 6 were waited for; matrix products, arithmetic and copies ran while one was open for 1% of the time, Pallas kernels for 3%

profile of v5, /device:TPU:1, one launch (start us, length us, event | category | flops | bytes accessed | tf_op | source)
XLA Modules:
  0.0 183.4 jit_solution(12148727958000004816)
XLA Ops:
  0.6 8.8 %collective-permute-start = (bf16[256,2,768]{2,1,0:T(2,128)(2,1)}, bf16[256,2,768]{2,1,0:T(2,128)(2,1)S(1)}, u32[]{:S(2)}, u32[]{:S(2)}) collective-permute-start(bf16[256,2,768]{2,1,0:T(2,128)(2,1)} %param.2), channel_id=1, source_target_pairs={{0,32},{32,0},{1,33},{33,1},{2,34},{34,2},{3,35},{35,3},{4,36},{36... | collective-permute-start | bytes 2359304 | tf_op jit(solution)/shard_map/ppermute | solution.py:240
  9.4 1.9 %collective-permute-start.3 = (bf16[128,768]{1,0:T(8,128)(2,1)}, bf16[128,768]{1,0:T(8,128)(2,1)S(1)}, u32[]{:S(2)}, u32[]{:S(2)}) collective-permute-start(bf16[128,768]{1,0:T(8,128)(2,1)} %refs_0_.1), channel_id=1, source_target_pairs={{0,128},{128,0},{64,192},{192,64},{256,384},{384,256},{320,448},{4... | collective-permute-start | bytes 589832 | tf_op jit(solution)/shard_map/ppermute | solution.py:257
  11.4 2.4 %collective-permute-start.4 = (bf16[128,768]{1,0:T(8,128)(2,1)}, bf16[128,768]{1,0:T(8,128)(2,1)S(1)}, u32[]{:S(2)}, u32[]{:S(2)}) collective-permute-start(bf16[128,768]{1,0:T(8,128)(2,1)} %refs_0_.1), channel_id=1, source_target_pairs={{128,256},{256,128},{192,320},{320,192},{384,0},{0,384},{448,64},{... | collective-permute-start | bytes 589832 | tf_op jit(solution)/shard_map/ppermute | solution.py:257
  13.7 2.3 %collective-permute-start.2 = (bf16[128,768]{1,0:T(8,128)(2,1)}, bf16[128,768]{1,0:T(8,128)(2,1)S(1)}, u32[]{:S(2)}, u32[]{:S(2)}) collective-permute-start(bf16[128,768]{1,0:T(8,128)(2,1)} %refs_0_.1), channel_id=1, source_target_pairs={{64,128},{128,64},{192,256},{256,192},{320,384},{384,320},{448,0},... | collective-permute-start | bytes 589832 | tf_op jit(solution)/shard_map/ppermute | solution.py:257
  16.0 4.9 %collective-permute-start.1 = (bf16[128,768]{1,0:T(8,128)(2,1)}, bf16[128,768]{1,0:T(8,128)(2,1)S(1)}, u32[]{:S(2)}, u32[]{:S(2)}) collective-permute-start(bf16[128,768]{1,0:T(8,128)(2,1)} %refs_0_.1), channel_id=1, source_target_pairs={{0,64},{64,0},{128,192},{192,128},{256,320},{320,256},{384,448},{4... | collective-permute-start | bytes 589832 | tf_op jit(solution)/shard_map/ppermute | solution.py:257
  21.0 1.6 collective-permute-done.3.refs_3_
  22.6 0.0 collective-permute-done.4.refs_4_
  22.6 1.9 %collective-permute-start.5 = (bf16[128,768]{1,0:T(8,128)(2,1)S(1)}, bf16[128,768]{1,0:T(8,128)(2,1)S(1)}, u32[]{:S(2)}, u32[]{:S(2)}) collective-permute-start(bf16[128,768]{1,0:T(8,128)(2,1)S(1)} %get-tuple-element.75), channel_id=1, source_target_pairs={{64,128},{128,64},{192,256},{256,192},{320,384},{384,320},{448,0},... | collective-permute-start | bytes 589832 | tf_op jit(solution)/shard_map/ppermute | solution.py:257
  24.6 3.3 %collective-permute-start.7 = (bf16[128,768]{1,0:T(8,128)(2,1)S(1)}, bf16[128,768]{1,0:T(8,128)(2,1)S(1)}, u32[]{:S(2)}, u32[]{:S(2)}) collective-permute-start(bf16[128,768]{1,0:T(8,128)(2,1)S(1)} %collective-permute-done.4.refs_4_), channel_id=1, source_target_pairs={{0,128},{128,0},{64,192},{192,64},{256,384},{384,256},{320,448},{4... | collective-permute-start | bytes 589832 | tf_op jit(solution)/shard_map/ppermute | solution.py:257
  27.9 4.4 %collective-permute-start.6 = (bf16[128,768]{1,0:T(8,128)(2,1)S(1)}, bf16[128,768]{1,0:T(8,128)(2,1)S(1)}, u32[]{:S(2)}, u32[]{:S(2)}) collective-permute-start(bf16[128,768]{1,0:T(8,128)(2,1)S(1)} %get-tuple-element.74), channel_id=1, source_target_pairs={{0,64},{64,0},{128,192},{192,128},{256,320},{320,256},{384,448},{4... | collective-permute-start | bytes 589832 | tf_op jit(solution)/shard_map/ppermute | solution.py:257
  32.2 1.2 copy.12
  33.5 0.0 copy-start
  33.5 0.1 copy.11
  33.6 0.9 shard_map.41
  34.6 1.9 %shard_map.42 = (f32[2,512,768]{2,1,0:T(8,128)S(1)}, f32[16,128]{1,0:T(8,128)S(1)}, f32[8,128]{1,0:T(8,128)S(1)}, bf16[768,768]{1,0:T(8,128)(2,1)S(1)}) custom-call(bf16[2,512,768]{2,1,0:T(8,128)(2,1)S(1)} %get-tuple-element.36.rows, bf16[128,768]{1,0:T(8,128)(2,1)S(1)} %copy-done, bf16[128,768]{1,0:T(8,128)(2,1)S(1)} %collective-permute-done.1.refs_1_, ...), custom_call_target="tpu_custom_call" | custom-call | flops 1207959552 | bytes 2097152 | tf_op jit(solution)/shard_map/pallas_call | solution.py:30
  36.5 2.3 %collective-permute-done.6.refs_0_ = bf16[128,768]{1,0:T(8,128)(2,1)S(1)} collective-permute-done((bf16[128,768]{1,0:T(8,128)(2,1)S(1)}, bf16[128,768]{1,0:T(8,128)(2,1)S(1)}, u32[]{:S(2)}, u32[]{:S(2)}) %collective-permute-start.6) | collective-permute-done | bytes 196640 | tf_op jit(solution)/shard_map/ppermute | solution.py:257
  38.7 0.9 shard_map.43
  39.6 10.9 %all_to_all.35.recv_ref = f32[8,16,128]{2,1,0:T(8,128)S(1)} all-to-all(f32[8,16,128]{2,1,0:T(8,128)S(1)} %get-tuple-element.41), channel_id=1, replica_groups=mesh['y'=8,'core'=2,'x'=4,'z'=8] {'y'}, dimensions={0} | all-to-all | bytes 131072 | tf_op jit(solution)/shard_map/all_to_all | solution.py:281
  50.5 0.6 shard_map.44
  51.1 26.5 %all_to_all.36.recv_ref = bf16[64,16,128]{2,1,0:T(8,128)(2,1)S(1)} all-to-all(bf16[64,16,128]{2,1,0:T(8,128)(2,1)S(1)} %shard_map.44), channel_id=1, replica_groups=mesh['y'=8,'core'=2,'x'=4,'z'=8] {'x','z','core'}, dimensions={0} | all-to-all | bytes 524288 | tf_op jit(solution)/shard_map/all_to_all | solution.py:285
  77.6 0.6 shard_map.45
  78.2 9.6 %all_to_all.37.recv_ref = f32[8,16,128]{2,1,0:T(8,128)S(1)} all-to-all(f32[8,16,128]{2,1,0:T(8,128)S(1)} %get-tuple-element.43), channel_id=1, replica_groups=mesh['y'=8,'core'=2,'x'=4,'z'=8] {'y'}, dimensions={0} | all-to-all | bytes 131072 | tf_op jit(solution)/shard_map/all_to_all | solution.py:281
  87.8 0.6 shard_map.46
  88.3 19.0 %all_to_all.38.recv_ref = f32[64,8,128]{2,1,0:T(8,128)S(1)} all-to-all(f32[64,8,128]{2,1,0:T(8,128)S(1)} %shard_map.46), channel_id=1, replica_groups=mesh['y'=8,'core'=2,'x'=4,'z'=8] {'x','z','core'}, dimensions={0} | all-to-all | bytes 524288 | tf_op jit(solution)/shard_map/all_to_all | solution.py:285
  107.4 0.6 shard_map.47
  108.0 9.6 %all_to_all.39.recv_ref.col_ref = f32[8,16,128]{2,1,0:T(8,128)S(1)} all-to-all(f32[8,16,128]{2,1,0:T(8,128)S(1)} %shard_map.47), channel_id=1, replica_groups=mesh['y'=8,'core'=2,'x'=4,'z'=8] {'y'}, dimensions={0} | all-to-all | bytes 131072 | tf_op jit(solution)/shard_map/all_to_all | solution.py:281
  117.5 0.6 shard_map.48
  118.1 19.0 %all_to_all.40.row_ref = f32[64,8,128]{2,1,0:T(8,128)S(1)} all-to-all(f32[64,8,128]{2,1,0:T(8,128)S(1)} %shard_map.48), channel_id=1, replica_groups=mesh['y'=8,'core'=2,'x'=4,'z'=8] {'x','z','core'}, dimensions={0} | all-to-all | bytes 524288 | tf_op jit(solution)/shard_map/all_to_all | solution.py:285
  137.1 2.8 %shard_map.49 = (bf16[32,16,768]{2,1,0:T(8,128)(2,1)S(1)}, bf16[32,16,768]{2,1,0:T(8,128)(2,1)S(1)}, bf16[1024,1024]{1,0:T(8,128)(2,1)S(1)}) custom-call(f32[2,512,768]{2,1,0:T(8,128)S(1)} %get-tuple-element.37.early, f32[2,512,256]{2,1,0:T(8,128)S(1)} %get-tuple-element.40.late, f32[64,8,128]{2,1,0:T(8,128)S(1)} %all_to_all.40.row_ref, ...), custom_call_target="tpu_custom_call" | custom-call | flops 1610612736 | bytes 2097152 | tf_op jit(solution)/shard_map/pallas_call | solution.py:30
  140.0 2.4 %collective-permute-start.8 = (bf16[32,16,768]{2,1,0:T(8,128)(2,1)S(1)}, bf16[32,16,768]{2,1,0:T(8,128)(2,1)S(1)}, u32[]{:S(2)}, u32[]{:S(2)}) collective-permute-start(bf16[32,16,768]{2,1,0:T(8,128)(2,1)S(1)} %get-tuple-element.60), channel_id=1, source_target_pairs={{0,32},{32,0},{1,33},{33,1},{2,34},{34,2},{3,35},{35,3},{4,36},{36... | collective-permute-start | bytes 2359304 | tf_op jit(solution)/shard_map/ppermute | solution.py:240
  142.3 1.8 shard_map.50
  144.1 0.1 collective-permute-done.8
  144.2 1.1 add_convert_fusion
  145.3 5.1 %all-to-all-start.6 = ((bf16[32,16,768]{2,1,0:T(8,128)(2,1)}), bf16[32,16,768]{2,1,0:T(8,128)(2,1)S(1)}, u32[]{:S(2)}, u32[]{:S(2)}) async-start(bf16[32,16,768]{2,1,0:T(8,128)(2,1)} %add_convert_fusion), calls=%async_computation.6 | async-start | bytes 1572864 | tf_op jit(solution)/shard_map/all_to_all | solution.py:349
  150.4 2.2 %collective-permute-start.11 = (bf16[768,128]{1,0:T(8,128)(2,1)S(1)}, bf16[768,128]{1,0:T(8,128)(2,1)S(1)}, u32[]{:S(2)}, u32[]{:S(2)}) collective-permute-start(bf16[768,128]{1,0:T(8,128)(2,1)S(1)} %get-tuple-element.66), channel_id=1, source_target_pairs={{64,128},{128,64},{192,256},{256,192},{320,384},{384,320},{448,0},... | collective-permute-start | bytes 589832 | tf_op jit(solution)/shard_map/ppermute | solution.py:257
  152.6 2.0 %collective-permute-start.12 = (bf16[768,128]{1,0:T(8,128)(2,1)S(1)}, bf16[768,128]{1,0:T(8,128)(2,1)S(1)}, u32[]{:S(2)}, u32[]{:S(2)}) collective-permute-start(bf16[768,128]{1,0:T(8,128)(2,1)S(1)} %get-tuple-element.67), channel_id=1, source_target_pairs={{0,64},{64,0},{128,192},{192,128},{256,320},{320,256},{384,448},{4... | collective-permute-start | bytes 589832 | tf_op jit(solution)/shard_map/ppermute | solution.py:257
  154.7 2.6 %collective-permute-start.14 = (bf16[768,128]{1,0:T(8,128)(2,1)S(1)}, bf16[768,128]{1,0:T(8,128)(2,1)S(1)}, u32[]{:S(2)}, u32[]{:S(2)}) collective-permute-start(bf16[768,128]{1,0:T(8,128)(2,1)S(1)} %get-tuple-element.69), channel_id=1, source_target_pairs={{0,128},{128,0},{64,192},{192,64},{256,384},{384,256},{320,448},{4... | collective-permute-start | bytes 589832 | tf_op jit(solution)/shard_map/ppermute | solution.py:257
  157.3 4.7 %collective-permute-start.9 = (bf16[768,128]{1,0:T(8,128)(2,1)S(1)}, bf16[768,128]{1,0:T(8,128)(2,1)S(1)}, u32[]{:S(2)}, u32[]{:S(2)}) collective-permute-start(bf16[768,128]{1,0:T(8,128)(2,1)S(1)} %get-tuple-element.63), channel_id=1, source_target_pairs={{0,64},{64,0},{128,192},{192,128},{256,320},{320,256},{384,448},{4... | collective-permute-start | bytes 589832 | tf_op jit(solution)/shard_map/ppermute | solution.py:257
  162.0 2.4 %collective-permute-start.10 = (bf16[768,128]{1,0:T(8,128)(2,1)S(1)}, bf16[768,128]{1,0:T(8,128)(2,1)S(1)}, u32[]{:S(2)}, u32[]{:S(2)}) collective-permute-start(bf16[768,128]{1,0:T(8,128)(2,1)S(1)} %get-tuple-element.64), channel_id=1, source_target_pairs={{64,128},{128,64},{192,256},{256,192},{320,384},{384,320},{448,0},... | collective-permute-start | bytes 589832 | tf_op jit(solution)/shard_map/ppermute | solution.py:257
  164.4 2.4 %collective-permute-done.14 = bf16[768,128]{1,0:T(8,128)(2,1)S(1)} collective-permute-done((bf16[768,128]{1,0:T(8,128)(2,1)S(1)}, bf16[768,128]{1,0:T(8,128)(2,1)S(1)}, u32[]{:S(2)}, u32[]{:S(2)}) %collective-permute-start.14) | collective-permute-done | bytes 196640 | tf_op jit(solution)/shard_map/ppermute | solution.py:257
  166.8 0.2 add_convert_fusion.1
  167.0 2.3 %collective-permute-start.15 = (bf16[768,128]{1,0:T(8,128)(2,1)S(1)}, bf16[768,128]{1,0:T(8,128)(2,1)S(1)}, u32[]{:S(2)}, u32[]{:S(2)}) collective-permute-start(bf16[768,128]{1,0:T(8,128)(2,1)S(1)} %get-tuple-element.72), channel_id=1, source_target_pairs={{128,256},{256,128},{192,320},{320,192},{384,0},{0,384},{448,64},{... | collective-permute-start | bytes 589832 | tf_op jit(solution)/shard_map/ppermute | solution.py:257
  169.3 1.9 %collective-permute-start.13 = (bf16[768,128]{1,0:T(8,128)(2,1)S(1)}, bf16[768,128]{1,0:T(8,128)(2,1)S(1)}, u32[]{:S(2)}, u32[]{:S(2)}) collective-permute-start(bf16[768,128]{1,0:T(8,128)(2,1)S(1)} %get-tuple-element.73), channel_id=1, source_target_pairs={{0,128},{128,0},{64,192},{192,64},{256,384},{384,256},{320,448},{4... | collective-permute-start | bytes 589832 | tf_op jit(solution)/shard_map/ppermute | solution.py:257
  171.3 0.1 reduce_sum.12
  171.4 0.6 copy.8
  172.0 3.6 %collective-permute-done.15.refs_3_ = bf16[768,128]{1,0:T(8,128)(2,1)S(1)} collective-permute-done((bf16[768,128]{1,0:T(8,128)(2,1)S(1)}, bf16[768,128]{1,0:T(8,128)(2,1)S(1)}, u32[]{:S(2)}, u32[]{:S(2)}) %collective-permute-start.15) | collective-permute-done | bytes 196640 | tf_op jit(solution)/shard_map/ppermute | solution.py:257
  175.7 6.8 %collective-permute-done.13.refs_2_ = bf16[768,128]{1,0:T(8,128)(2,1)S(1)} collective-permute-done((bf16[768,128]{1,0:T(8,128)(2,1)S(1)}, bf16[768,128]{1,0:T(8,128)(2,1)S(1)}, u32[]{:S(2)}, u32[]{:S(2)}) %collective-permute-start.13) | collective-permute-done | bytes 196640 | tf_op jit(solution)/shard_map/ppermute | solution.py:257
  182.5 0.9 shard_map.51
  (12 shorter events, 0.1 us)
Async XLA Ops:
  0.6 27.2 %collective-permute-start = (bf16[256,2,768]{2,1,0:T(2,128)(2,1)}, bf16[256,2,768]{2,1,0:T(2,128)(2,1)S(1)}, u32[]{:S(2)}, u32[]{:S(2)}) collective-permute-start(bf16[256,2,768]{2,1,0:T(2,128)(2,1)} %param.2), channel_id=1, source_target_pairs={{0,32},{32,0},{1,33},{33,1},{2,34},{34,2},{3,35},{35,3},{4,36},{36... | collective-permute-start | bytes 2359304 | tf_op jit(solution)/shard_map/ppermute | solution.py:240
  9.4 13.2 %collective-permute-start.3 = (bf16[128,768]{1,0:T(8,128)(2,1)}, bf16[128,768]{1,0:T(8,128)(2,1)S(1)}, u32[]{:S(2)}, u32[]{:S(2)}) collective-permute-start(bf16[128,768]{1,0:T(8,128)(2,1)} %refs_0_.1), channel_id=1, source_target_pairs={{0,128},{128,0},{64,192},{192,64},{256,384},{384,256},{320,448},{4... | collective-permute-start | bytes 589832 | tf_op jit(solution)/shard_map/ppermute | solution.py:257
  11.4 11.2 %collective-permute-start.4 = (bf16[128,768]{1,0:T(8,128)(2,1)}, bf16[128,768]{1,0:T(8,128)(2,1)S(1)}, u32[]{:S(2)}, u32[]{:S(2)}) collective-permute-start(bf16[128,768]{1,0:T(8,128)(2,1)} %refs_0_.1), channel_id=1, source_target_pairs={{128,256},{256,128},{192,320},{320,192},{384,0},{0,384},{448,64},{... | collective-permute-start | bytes 589832 | tf_op jit(solution)/shard_map/ppermute | solution.py:257
  13.7 20.8 %collective-permute-start.2 = (bf16[128,768]{1,0:T(8,128)(2,1)}, bf16[128,768]{1,0:T(8,128)(2,1)S(1)}, u32[]{:S(2)}, u32[]{:S(2)}) collective-permute-start(bf16[128,768]{1,0:T(8,128)(2,1)} %refs_0_.1), channel_id=1, source_target_pairs={{64,128},{128,64},{192,256},{256,192},{320,384},{384,320},{448,0},... | collective-permute-start | bytes 589832 | tf_op jit(solution)/shard_map/ppermute | solution.py:257
  16.0 18.5 %collective-permute-start.1 = (bf16[128,768]{1,0:T(8,128)(2,1)}, bf16[128,768]{1,0:T(8,128)(2,1)S(1)}, u32[]{:S(2)}, u32[]{:S(2)}) collective-permute-start(bf16[128,768]{1,0:T(8,128)(2,1)} %refs_0_.1), channel_id=1, source_target_pairs={{0,64},{64,0},{128,192},{192,128},{256,320},{320,256},{384,448},{4... | collective-permute-start | bytes 589832 | tf_op jit(solution)/shard_map/ppermute | solution.py:257
  22.6 11.9 %collective-permute-start.5 = (bf16[128,768]{1,0:T(8,128)(2,1)S(1)}, bf16[128,768]{1,0:T(8,128)(2,1)S(1)}, u32[]{:S(2)}, u32[]{:S(2)}) collective-permute-start(bf16[128,768]{1,0:T(8,128)(2,1)S(1)} %get-tuple-element.75), channel_id=1, source_target_pairs={{64,128},{128,64},{192,256},{256,192},{320,384},{384,320},{448,0},... | collective-permute-start | bytes 589832 | tf_op jit(solution)/shard_map/ppermute | solution.py:257
  24.6 11.9 %collective-permute-start.7 = (bf16[128,768]{1,0:T(8,128)(2,1)S(1)}, bf16[128,768]{1,0:T(8,128)(2,1)S(1)}, u32[]{:S(2)}, u32[]{:S(2)}) collective-permute-start(bf16[128,768]{1,0:T(8,128)(2,1)S(1)} %collective-permute-done.4.refs_4_), channel_id=1, source_target_pairs={{0,128},{128,0},{64,192},{192,64},{256,384},{384,256},{320,448},{4... | collective-permute-start | bytes 589832 | tf_op jit(solution)/shard_map/ppermute | solution.py:257
  27.9 10.9 %collective-permute-start.6 = (bf16[128,768]{1,0:T(8,128)(2,1)S(1)}, bf16[128,768]{1,0:T(8,128)(2,1)S(1)}, u32[]{:S(2)}, u32[]{:S(2)}) collective-permute-start(bf16[128,768]{1,0:T(8,128)(2,1)S(1)} %get-tuple-element.74), channel_id=1, source_target_pairs={{0,64},{64,0},{128,192},{192,128},{256,320},{320,256},{384,448},{4... | collective-permute-start | bytes 589832 | tf_op jit(solution)/shard_map/ppermute | solution.py:257
  33.5 1.1 copy-start
  140.0 4.3 %collective-permute-start.8 = (bf16[32,16,768]{2,1,0:T(8,128)(2,1)S(1)}, bf16[32,16,768]{2,1,0:T(8,128)(2,1)S(1)}, u32[]{:S(2)}, u32[]{:S(2)}) collective-permute-start(bf16[32,16,768]{2,1,0:T(8,128)(2,1)S(1)} %get-tuple-element.60), channel_id=1, source_target_pairs={{0,32},{32,0},{1,33},{33,1},{2,34},{34,2},{3,35},{35,3},{4,36},{36... | collective-permute-start | bytes 2359304 | tf_op jit(solution)/shard_map/ppermute | solution.py:240
  145.3 26.0 %all-to-all-start.6 = ((bf16[32,16,768]{2,1,0:T(8,128)(2,1)}), bf16[32,16,768]{2,1,0:T(8,128)(2,1)S(1)}, u32[]{:S(2)}, u32[]{:S(2)}) async-start(bf16[32,16,768]{2,1,0:T(8,128)(2,1)} %add_convert_fusion), calls=%async_computation.6 | async-start | bytes 1572864 | tf_op jit(solution)/shard_map/all_to_all | solution.py:349
  150.4 13.9 %collective-permute-start.11 = (bf16[768,128]{1,0:T(8,128)(2,1)S(1)}, bf16[768,128]{1,0:T(8,128)(2,1)S(1)}, u32[]{:S(2)}, u32[]{:S(2)}) collective-permute-start(bf16[768,128]{1,0:T(8,128)(2,1)S(1)} %get-tuple-element.66), channel_id=1, source_target_pairs={{64,128},{128,64},{192,256},{256,192},{320,384},{384,320},{448,0},... | collective-permute-start | bytes 589832 | tf_op jit(solution)/shard_map/ppermute | solution.py:257
  152.6 11.7 %collective-permute-start.12 = (bf16[768,128]{1,0:T(8,128)(2,1)S(1)}, bf16[768,128]{1,0:T(8,128)(2,1)S(1)}, u32[]{:S(2)}, u32[]{:S(2)}) collective-permute-start(bf16[768,128]{1,0:T(8,128)(2,1)S(1)} %get-tuple-element.67), channel_id=1, source_target_pairs={{0,64},{64,0},{128,192},{192,128},{256,320},{320,256},{384,448},{4... | collective-permute-start | bytes 589832 | tf_op jit(solution)/shard_map/ppermute | solution.py:257
  154.7 12.1 %collective-permute-start.14 = (bf16[768,128]{1,0:T(8,128)(2,1)S(1)}, bf16[768,128]{1,0:T(8,128)(2,1)S(1)}, u32[]{:S(2)}, u32[]{:S(2)}) collective-permute-start(bf16[768,128]{1,0:T(8,128)(2,1)S(1)} %get-tuple-element.69), channel_id=1, source_target_pairs={{0,128},{128,0},{64,192},{192,64},{256,384},{384,256},{320,448},{4... | collective-permute-start | bytes 589832 | tf_op jit(solution)/shard_map/ppermute | solution.py:257
  157.3 14.7 %collective-permute-start.9 = (bf16[768,128]{1,0:T(8,128)(2,1)S(1)}, bf16[768,128]{1,0:T(8,128)(2,1)S(1)}, u32[]{:S(2)}, u32[]{:S(2)}) collective-permute-start(bf16[768,128]{1,0:T(8,128)(2,1)S(1)} %get-tuple-element.63), channel_id=1, source_target_pairs={{0,64},{64,0},{128,192},{192,128},{256,320},{320,256},{384,448},{4... | collective-permute-start | bytes 589832 | tf_op jit(solution)/shard_map/ppermute | solution.py:257
  162.0 10.0 %collective-permute-start.10 = (bf16[768,128]{1,0:T(8,128)(2,1)S(1)}, bf16[768,128]{1,0:T(8,128)(2,1)S(1)}, u32[]{:S(2)}, u32[]{:S(2)}) collective-permute-start(bf16[768,128]{1,0:T(8,128)(2,1)S(1)} %get-tuple-element.64), channel_id=1, source_target_pairs={{64,128},{128,64},{192,256},{256,192},{320,384},{384,320},{448,0},... | collective-permute-start | bytes 589832 | tf_op jit(solution)/shard_map/ppermute | solution.py:257
  167.0 8.7 %collective-permute-start.15 = (bf16[768,128]{1,0:T(8,128)(2,1)S(1)}, bf16[768,128]{1,0:T(8,128)(2,1)S(1)}, u32[]{:S(2)}, u32[]{:S(2)}) collective-permute-start(bf16[768,128]{1,0:T(8,128)(2,1)S(1)} %get-tuple-element.72), channel_id=1, source_target_pairs={{128,256},{256,128},{192,320},{320,192},{384,0},{0,384},{448,64},{... | collective-permute-start | bytes 589832 | tf_op jit(solution)/shard_map/ppermute | solution.py:257
  169.3 13.2 %collective-permute-start.13 = (bf16[768,128]{1,0:T(8,128)(2,1)S(1)}, bf16[768,128]{1,0:T(8,128)(2,1)S(1)}, u32[]{:S(2)}, u32[]{:S(2)}) collective-permute-start(bf16[768,128]{1,0:T(8,128)(2,1)S(1)} %get-tuple-element.73), channel_id=1, source_target_pairs={{0,128},{128,0},{64,192},{192,64},{256,384},{384,256},{320,448},{4... | collective-permute-start | bytes 589832 | tf_op jit(solution)/shard_map/ppermute | solution.py:257

commit v6 on v5

--- a/solution.py
+++ b/solution.py
@@ -21,7 +21,7 @@
 ROWS = CORES * MINE
 SPLIT = EARLY * LANES
 COLS = SLOTS * LANES
-GROUP = XS * ZS * CORES
+GROUP = XS * ZS
 VIEWS = 2
 BLOCKS = [(view, half) for view in range(VIEWS) for half in range(CORES)]
 
@@ -89,7 +89,7 @@
 
 
 def copies(ref, value):
-    ref[...] = jnp.broadcast_to(value[None], ref.shape)
+    ref[...] = jnp.broadcast_to(value.astype(ref.dtype)[None], ref.shape)
 
 
 def units(values):
@@ -159,7 +159,7 @@
         soft_ref, out_ref, total, sums = refs
     else:
         out_ref, total, sums = refs
-    total[...] = jnp.sum(recv_ref[...], axis=0)
+    total[...] = jnp.sum(recv_ref[...].astype(F32), axis=0)
     for view, half in BLOCKS:
         acc = None
         for slot in range(SLOTS):
@@ -169,8 +169,8 @@
         put_clips(s, view, half, acc, sums)
     both = sums[...]
     if first:
-        both = jnp.concatenate([both, soft_ref[...]]).astype(BF16)
-    copies(out_ref, both)
+        both = jnp.concatenate([both, soft_ref[...]])
+    out_ref[...] = both
 
 
 def col_kernel(first, early, late, recv_ref, *refs):
@@ -197,7 +197,7 @@
     mine_ref, other_ref, grads, total, clips,
 ):
     s = places()
-    total[...] = jnp.sum(col_ref[...], axis=0)
+    total[...] = jnp.sum(col_ref[...].astype(F32), axis=0)
     clips[...] = jnp.sum(row_ref[...], axis=0)
     for half, ref in ((1, other_ref), (0, mine_ref)):
         rows = clips_of(half)
@@ -281,8 +281,10 @@
     return lax.all_to_all(part, "y", 0, 0)
 
 
-def group_sums(part):
-    return lax.all_to_all(part, ("x", "z", "core"), 0, 0)
+def group_sums(part, dtype):
+    part = (part + shift(part, "core", CORES, 1)).astype(dtype)
+    part = jnp.broadcast_to(part[None], (GROUP,) + part.shape)
+    return lax.all_to_all(part, ("z", "x"), 0, 0)
 
 
 def on_device(embeddings, prototypes):
@@ -297,9 +299,9 @@
         [((VIEWS, ROWS, WIDTH), BF16), ((WIDTH, VIEWS * ROWS), BF16)],
     )
     cols, rows8, rows16 = ((16, LANES), F32), ((8, LANES), F32), ((16, LANES), F32)
-    col_out = ((YS, 16, LANES), F32)
-    row_out = ((GROUP, 8, LANES), F32)
-    both_out = ((GROUP, 16, LANES), BF16)
+    col_out = ((YS, 16, LANES), BF16)
+    row_out = ((8, LANES), F32)
+    both_out = ((16, LANES), F32)
     work = 4 * ROWS * WIDTH
     early, col_part, soft, near_centers = call(
         early_kernel, (rows, *pieces[:EARLY]),
@@ -315,7 +317,7 @@
         functools.partial(row_kernel, True), (early, late, col_part, soft), [both_out],
         [cols, rows8],
     )
-    row_part = group_sums(row_part)
+    row_part = group_sums(row_part, BF16)
     col_part, soft = call(
         functools.partial(col_kernel, True), (early, late, row_part), [col_out, rows8],
         [rows16, cols],
@@ -324,7 +326,7 @@
     (row_part,) = call(
         functools.partial(row_kernel, False), (early, late, col_part), [row_out], [cols, rows8]
     )
-    row_part = group_sums(row_part)
+    row_part = group_sums(row_part, F32)
     (col_part,) = call(
         functools.partial(col_kernel, False), (early, late, row_part), [col_out], [rows8, cols]
     )
@@ -332,7 +334,7 @@
     (row_part,) = call(
         functools.partial(row_kernel, False), (early, late, col_part), [row_out], [cols, rows8]
     )
-    row_part = group_sums(row_part)
+    row_part = group_sums(row_part, F32)
 
     ge_out = ((XS * ZS, 16, WIDTH), BF16)
     mine, other, grads = call(

time: 184 us -> 182 us (0.989)
  blocking collectives: 94.5 us -> 75 us
  starting transfers between devices: 55.5 us -> 70.9 us
    all_to_all x3, blocking collectives: 64.5 us -> 46 us  [group_sums(): return lax.all_to_all(part, ('z', 'x'), 0, 0)]
    ppermute x2 -> x5, starting transfers between devices: 11.1 us -> 27.3 us  [shift(): return lax.ppermute(part, axis, [(i, (i + by) % size) for i in range(size)])]
    ppermute x2 -> x5, waiting for transfers between devices: 0.1 us -> 2.41 us  [shift(): return lax.ppermute(part, axis, [(i, (i + by) % size) for i in range(size)])]
  transfers between devices with their start and end apart: 17 -> 20, of which waited for: 6 -> 8; matrix products, arithmetic and copies ran while one was open for 1% -> 1% of each run, Pallas kernels for 3% -> 3%
where the time goes in v6:
time: 182 us; the launch traced here: 181 us
  blocking collectives  75 us (41%)
  starting transfers between devices  70.9 us (39%)
  waiting for transfers between devices  18.4 us (10%)
  Pallas kernels  12 us (7%)
  local copies, waits for them, and re-layouts  1.98 us (1%)
    all_to_all x3, blocking collectives, group_sums(): return lax.all_to_all(part, ('z', 'x'), 0, 0)  46 us
    ppermute x14, starting transfers between devices, swap(): return lax.ppermute(part, ('y', 'core'), pairs)  39.7 us
    all_to_all x3, blocking collectives, y_sums(): return lax.all_to_all(part, 'y', 0, 0)  29 us
    ppermute x5, starting transfers between devices, shift(): return lax.ppermute(part, axis, [(i, (i + by) % size) for i in range(size)])  27.3 us
    ppermute x14, waiting for transfers between devices, swap(): return lax.ppermute(part, ('y', 'core'), pairs)  16 us
    pallas_call x11, Pallas kernels, call(): pl.pallas_call(kernel, out_shape=[jax.ShapeDtypeStruct(shape, dtype) for...  12 us
    all_to_all x1, starting transfers between devices, on_device(): part = lax.all_to_all(part, ('x', 'z'), 0, 0)  3.91 us
  transfers between devices with their start and end apart: 20, of which 8 were waited for; matrix products, arithmetic and copies ran while one was open for 1% of the time, Pallas kernels for 3%

profile of v6, /device:TPU:1, one launch (start us, length us, event | category | flops | bytes accessed | tf_op | source)
XLA Modules:
  0.0 180.7 jit_solution(17203100361047365184)
XLA Ops:
  0.6 8.8 %collective-permute-start = (bf16[256,2,768]{2,1,0:T(2,128)(2,1)}, bf16[256,2,768]{2,1,0:T(2,128)(2,1)S(1)}, u32[]{:S(2)}, u32[]{:S(2)}) collective-permute-start(bf16[256,2,768]{2,1,0:T(2,128)(2,1)} %param.2), channel_id=1, source_target_pairs={{0,32},{32,0},{1,33},{33,1},{2,34},{34,2},{3,35},{35,3},{4,36},{36... | collective-permute-start | bytes 2359304 | tf_op jit(solution)/shard_map/ppermute | solution.py:240
  9.4 1.9 %collective-permute-start.3 = (bf16[128,768]{1,0:T(8,128)(2,1)}, bf16[128,768]{1,0:T(8,128)(2,1)S(1)}, u32[]{:S(2)}, u32[]{:S(2)}) collective-permute-start(bf16[128,768]{1,0:T(8,128)(2,1)} %refs_0_.1), channel_id=1, source_target_pairs={{0,128},{128,0},{64,192},{192,64},{256,384},{384,256},{320,448},{4... | collective-permute-start | bytes 589832 | tf_op jit(solution)/shard_map/ppermute | solution.py:257
  11.4 2.4 %collective-permute-start.4 = (bf16[128,768]{1,0:T(8,128)(2,1)}, bf16[128,768]{1,0:T(8,128)(2,1)S(1)}, u32[]{:S(2)}, u32[]{:S(2)}) collective-permute-start(bf16[128,768]{1,0:T(8,128)(2,1)} %refs_0_.1), channel_id=1, source_target_pairs={{128,256},{256,128},{192,320},{320,192},{384,0},{0,384},{448,64},{... | collective-permute-start | bytes 589832 | tf_op jit(solution)/shard_map/ppermute | solution.py:257
  13.7 2.3 %collective-permute-start.2 = (bf16[128,768]{1,0:T(8,128)(2,1)}, bf16[128,768]{1,0:T(8,128)(2,1)S(1)}, u32[]{:S(2)}, u32[]{:S(2)}) collective-permute-start(bf16[128,768]{1,0:T(8,128)(2,1)} %refs_0_.1), channel_id=1, source_target_pairs={{64,128},{128,64},{192,256},{256,192},{320,384},{384,320},{448,0},... | collective-permute-start | bytes 589832 | tf_op jit(solution)/shard_map/ppermute | solution.py:257
  16.0 4.9 %collective-permute-start.1 = (bf16[128,768]{1,0:T(8,128)(2,1)}, bf16[128,768]{1,0:T(8,128)(2,1)S(1)}, u32[]{:S(2)}, u32[]{:S(2)}) collective-permute-start(bf16[128,768]{1,0:T(8,128)(2,1)} %refs_0_.1), channel_id=1, source_target_pairs={{0,64},{64,0},{128,192},{192,128},{256,320},{320,256},{384,448},{4... | collective-permute-start | bytes 589832 | tf_op jit(solution)/shard_map/ppermute | solution.py:257
  21.0 1.6 collective-permute-done.3.refs_3_
  22.6 1.9 %collective-permute-start.5 = (bf16[128,768]{1,0:T(8,128)(2,1)S(1)}, bf16[128,768]{1,0:T(8,128)(2,1)S(1)}, u32[]{:S(2)}, u32[]{:S(2)}) collective-permute-start(bf16[128,768]{1,0:T(8,128)(2,1)S(1)} %get-tuple-element.75), channel_id=1, source_target_pairs={{64,128},{128,64},{192,256},{256,192},{320,384},{384,320},{448,0},... | collective-permute-start | bytes 589832 | tf_op jit(solution)/shard_map/ppermute | solution.py:257
  24.6 3.3 %collective-permute-start.7 = (bf16[128,768]{1,0:T(8,128)(2,1)S(1)}, bf16[128,768]{1,0:T(8,128)(2,1)S(1)}, u32[]{:S(2)}, u32[]{:S(2)}) collective-permute-start(bf16[128,768]{1,0:T(8,128)(2,1)S(1)} %collective-permute-done.4.refs_4_), channel_id=1, source_target_pairs={{0,128},{128,0},{64,192},{192,64},{256,384},{384,256},{320,448},{4... | collective-permute-start | bytes 589832 | tf_op jit(solution)/shard_map/ppermute | solution.py:257
  27.9 4.4 %collective-permute-start.6 = (bf16[128,768]{1,0:T(8,128)(2,1)S(1)}, bf16[128,768]{1,0:T(8,128)(2,1)S(1)}, u32[]{:S(2)}, u32[]{:S(2)}) collective-permute-start(bf16[128,768]{1,0:T(8,128)(2,1)S(1)} %get-tuple-element.74), channel_id=1, source_target_pairs={{0,64},{64,0},{128,192},{192,128},{256,320},{320,256},{384,448},{4... | collective-permute-start | bytes 589832 | tf_op jit(solution)/shard_map/ppermute | solution.py:257
  32.2 1.2 copy.12
  33.6 0.9 shard_map.41
  34.6 1.9 %shard_map.42 = (f32[2,512,768]{2,1,0:T(8,128)S(1)}, f32[16,128]{1,0:T(8,128)S(1)}, f32[8,128]{1,0:T(8,128)S(1)}, bf16[768,768]{1,0:T(8,128)(2,1)S(1)}) custom-call(bf16[2,512,768]{2,1,0:T(8,128)(2,1)S(1)} %get-tuple-element.36.rows, bf16[128,768]{1,0:T(8,128)(2,1)S(1)} %copy-done, bf16[128,768]{1,0:T(8,128)(2,1)S(1)} %collective-permute-done.1.refs_1_, ...), custom_call_target="tpu_custom_call" | custom-call | flops 1207959552 | bytes 2097152 | tf_op jit(solution)/shard_map/pallas_call | solution.py:30
  36.5 2.3 %collective-permute-done.6.refs_0_ = bf16[128,768]{1,0:T(8,128)(2,1)S(1)} collective-permute-done((bf16[128,768]{1,0:T(8,128)(2,1)S(1)}, bf16[128,768]{1,0:T(8,128)(2,1)S(1)}, u32[]{:S(2)}, u32[]{:S(2)}) %collective-permute-start.6) | collective-permute-done | bytes 196640 | tf_op jit(solution)/shard_map/ppermute | solution.py:257
  38.7 0.9 shard_map.43
  39.6 10.5 %all_to_all.35.recv_ref = bf16[8,16,128]{2,1,0:T(8,128)(2,1)S(1)} all-to-all(bf16[8,16,128]{2,1,0:T(8,128)(2,1)S(1)} %get-tuple-element.41), channel_id=1, replica_groups=mesh['y'=8,'core'=2,'x'=4,'z'=8] {'y'}, dimensions={0} | all-to-all | bytes 65536 | tf_op jit(solution)/shard_map/all_to_all | solution.py:281
  50.1 0.6 shard_map.44
  50.6 4.0 %collective-permute-start.8 = (f32[16,128]{1,0:T(8,128)S(1)}, f32[16,128]{1,0:T(8,128)S(1)}, u32[]{:S(2)}, u32[]{:S(2)}) collective-permute-start(f32[16,128]{1,0:T(8,128)S(1)} %shard_map.44), channel_id=1, source_target_pairs={{0,32},{32,0},{1,33},{33,1},{2,34},{34,2},{3,35},{35,3},{4,36},{36... | collective-permute-start | bytes 24584 | tf_op jit(solution)/shard_map/ppermute | solution.py:240
  54.7 0.8 collective-permute-done.8
  55.5 21.3 %all_to_all.36.recv_ref = bf16[32,16,128]{2,1,0:T(8,128)(2,1)S(1)} all-to-all(bf16[32,16,128]{2,1,0:T(8,128)(2,1)S(1)} %broadcast_in_dim.6), channel_id=1, replica_groups=mesh['y'=8,'core'=2,'x'=4,'z'=8] {'z','x'}, dimensions={0} | all-to-all | bytes 262144 | tf_op jit(solution)/shard_map/all_to_all | solution.py:287
  76.9 0.6 shard_map.45
  77.4 9.2 %all_to_all.37.recv_ref = bf16[8,16,128]{2,1,0:T(8,128)(2,1)S(1)} all-to-all(bf16[8,16,128]{2,1,0:T(8,128)(2,1)S(1)} %get-tuple-element.43), channel_id=1, replica_groups=mesh['y'=8,'core'=2,'x'=4,'z'=8] {'y'}, dimensions={0} | all-to-all | bytes 65536 | tf_op jit(solution)/shard_map/all_to_all | solution.py:281
  86.7 0.6 shard_map.46
  87.2 5.1 %collective-permute-start.9 = (f32[8,128]{1,0:T(8,128)S(1)}, f32[8,128]{1,0:T(8,128)S(1)}, u32[]{:S(2)}, u32[]{:S(2)}) collective-permute-start(f32[8,128]{1,0:T(8,128)S(1)} %shard_map.46), channel_id=1, source_target_pairs={{0,32},{32,0},{1,33},{33,1},{2,34},{34,2},{3,35},{35,3},{4,36},{36... | collective-permute-start | bytes 12296 | tf_op jit(solution)/shard_map/ppermute | solution.py:240
  92.4 0.8 collective-permute-done.9
  93.2 12.3 %all_to_all.38.recv_ref = f32[32,8,128]{2,1,0:T(8,128)S(1)} all-to-all(f32[32,8,128]{2,1,0:T(8,128)S(1)} %broadcast_in_dim.7), channel_id=1, replica_groups=mesh['y'=8,'core'=2,'x'=4,'z'=8] {'z','x'}, dimensions={0} | all-to-all | bytes 262144 | tf_op jit(solution)/shard_map/all_to_all | solution.py:287
  105.6 0.6 shard_map.47
  106.1 9.2 %all_to_all.39.recv_ref.col_ref = bf16[8,16,128]{2,1,0:T(8,128)(2,1)S(1)} all-to-all(bf16[8,16,128]{2,1,0:T(8,128)(2,1)S(1)} %shard_map.47), channel_id=1, replica_groups=mesh['y'=8,'core'=2,'x'=4,'z'=8] {'y'}, dimensions={0} | all-to-all | bytes 65536 | tf_op jit(solution)/shard_map/all_to_all | solution.py:281
  115.4 0.6 shard_map.48
  115.9 5.1 %collective-permute-start.10 = (f32[8,128]{1,0:T(8,128)S(1)}, f32[8,128]{1,0:T(8,128)S(1)}, u32[]{:S(2)}, u32[]{:S(2)}) collective-permute-start(f32[8,128]{1,0:T(8,128)S(1)} %shard_map.48), channel_id=1, source_target_pairs={{0,32},{32,0},{1,33},{33,1},{2,34},{34,2},{3,35},{35,3},{4,36},{36... | collective-permute-start | bytes 12296 | tf_op jit(solution)/shard_map/ppermute | solution.py:240
  121.1 0.8 collective-permute-done.10
  121.9 12.3 %all_to_all.40.row_ref = f32[32,8,128]{2,1,0:T(8,128)S(1)} all-to-all(f32[32,8,128]{2,1,0:T(8,128)S(1)} %broadcast_in_dim.8), channel_id=1, replica_groups=mesh['y'=8,'core'=2,'x'=4,'z'=8] {'z','x'}, dimensions={0} | all-to-all | bytes 262144 | tf_op jit(solution)/shard_map/all_to_all | solution.py:287
  134.3 2.8 %shard_map.49 = (bf16[32,16,768]{2,1,0:T(8,128)(2,1)S(1)}, bf16[32,16,768]{2,1,0:T(8,128)(2,1)S(1)}, bf16[1024,1024]{1,0:T(8,128)(2,1)S(1)}) custom-call(f32[2,512,768]{2,1,0:T(8,128)S(1)} %get-tuple-element.37.early, f32[2,512,256]{2,1,0:T(8,128)S(1)} %get-tuple-element.40.late, f32[32,8,128]{2,1,0:T(8,128)S(1)} %all_to_all.40.row_ref, ...), custom_call_target="tpu_custom_call" | custom-call | flops 1610612736 | bytes 2097152 | tf_op jit(solution)/shard_map/pallas_call | solution.py:30
  137.1 4.2 %collective-permute-start.11 = (bf16[32,16,768]{2,1,0:T(8,128)(2,1)S(1)}, bf16[32,16,768]{2,1,0:T(8,128)(2,1)S(1)}, u32[]{:S(2)}, u32[]{:S(2)}) collective-permute-start(bf16[32,16,768]{2,1,0:T(8,128)(2,1)S(1)} %get-tuple-element.60), channel_id=1, source_target_pairs={{0,32},{32,0},{1,33},{33,1},{2,34},{34,2},{3,35},{35,3},{4,36},{36... | collective-permute-start | bytes 2359304 | tf_op jit(solution)/shard_map/ppermute | solution.py:240
  141.3 1.8 shard_map.50
  143.1 1.1 add_convert_fusion
  144.2 3.9 %all-to-all-start.6 = ((bf16[32,16,768]{2,1,0:T(8,128)(2,1)}), bf16[32,16,768]{2,1,0:T(8,128)(2,1)S(1)}, u32[]{:S(2)}, u32[]{:S(2)}) async-start(bf16[32,16,768]{2,1,0:T(8,128)(2,1)} %add_convert_fusion), calls=%async_computation.6 | async-start | bytes 1572864 | tf_op jit(solution)/shard_map/all_to_all | solution.py:351
  148.1 2.2 %collective-permute-start.14 = (bf16[768,128]{1,0:T(8,128)(2,1)S(1)}, bf16[768,128]{1,0:T(8,128)(2,1)S(1)}, u32[]{:S(2)}, u32[]{:S(2)}) collective-permute-start(bf16[768,128]{1,0:T(8,128)(2,1)S(1)} %get-tuple-element.66), channel_id=1, source_target_pairs={{64,128},{128,64},{192,256},{256,192},{320,384},{384,320},{448,0},... | collective-permute-start | bytes 589832 | tf_op jit(solution)/shard_map/ppermute | solution.py:257
  150.3 2.2 %collective-permute-start.15 = (bf16[768,128]{1,0:T(8,128)(2,1)S(1)}, bf16[768,128]{1,0:T(8,128)(2,1)S(1)}, u32[]{:S(2)}, u32[]{:S(2)}) collective-permute-start(bf16[768,128]{1,0:T(8,128)(2,1)S(1)} %get-tuple-element.67), channel_id=1, source_target_pairs={{0,64},{64,0},{128,192},{192,128},{256,320},{320,256},{384,448},{4... | collective-permute-start | bytes 589832 | tf_op jit(solution)/shard_map/ppermute | solution.py:257
  152.5 2.8 %collective-permute-start.17 = (bf16[768,128]{1,0:T(8,128)(2,1)S(1)}, bf16[768,128]{1,0:T(8,128)(2,1)S(1)}, u32[]{:S(2)}, u32[]{:S(2)}) collective-permute-start(bf16[768,128]{1,0:T(8,128)(2,1)S(1)} %get-tuple-element.69), channel_id=1, source_target_pairs={{0,128},{128,0},{64,192},{192,64},{256,384},{384,256},{320,448},{4... | collective-permute-start | bytes 589832 | tf_op jit(solution)/shard_map/ppermute | solution.py:257
  155.2 4.4 %collective-permute-start.12 = (bf16[768,128]{1,0:T(8,128)(2,1)S(1)}, bf16[768,128]{1,0:T(8,128)(2,1)S(1)}, u32[]{:S(2)}, u32[]{:S(2)}) collective-permute-start(bf16[768,128]{1,0:T(8,128)(2,1)S(1)} %get-tuple-element.63), channel_id=1, source_target_pairs={{0,64},{64,0},{128,192},{192,128},{256,320},{320,256},{384,448},{4... | collective-permute-start | bytes 589832 | tf_op jit(solution)/shard_map/ppermute | solution.py:257
  159.6 2.3 %collective-permute-start.13 = (bf16[768,128]{1,0:T(8,128)(2,1)S(1)}, bf16[768,128]{1,0:T(8,128)(2,1)S(1)}, u32[]{:S(2)}, u32[]{:S(2)}) collective-permute-start(bf16[768,128]{1,0:T(8,128)(2,1)S(1)} %get-tuple-element.64), channel_id=1, source_target_pairs={{64,128},{128,64},{192,256},{256,192},{320,384},{384,320},{448,0},... | collective-permute-start | bytes 589832 | tf_op jit(solution)/shard_map/ppermute | solution.py:257
  162.0 2.6 %collective-permute-done.17 = bf16[768,128]{1,0:T(8,128)(2,1)S(1)} collective-permute-done((bf16[768,128]{1,0:T(8,128)(2,1)S(1)}, bf16[768,128]{1,0:T(8,128)(2,1)S(1)}, u32[]{:S(2)}, u32[]{:S(2)}) %collective-permute-start.17) | collective-permute-done | bytes 196640 | tf_op jit(solution)/shard_map/ppermute | solution.py:257
  164.7 1.9 %collective-permute-start.18 = (bf16[768,128]{1,0:T(8,128)(2,1)S(1)}, bf16[768,128]{1,0:T(8,128)(2,1)S(1)}, u32[]{:S(2)}, u32[]{:S(2)}) collective-permute-start(bf16[768,128]{1,0:T(8,128)(2,1)S(1)} %get-tuple-element.72), channel_id=1, source_target_pairs={{128,256},{256,128},{192,320},{320,192},{384,0},{0,384},{448,64},{... | collective-permute-start | bytes 589832 | tf_op jit(solution)/shard_map/ppermute | solution.py:257
  166.7 2.8 %collective-permute-start.16 = (bf16[768,128]{1,0:T(8,128)(2,1)S(1)}, bf16[768,128]{1,0:T(8,128)(2,1)S(1)}, u32[]{:S(2)}, u32[]{:S(2)}) collective-permute-start(bf16[768,128]{1,0:T(8,128)(2,1)S(1)} %get-tuple-element.73), channel_id=1, source_target_pairs={{0,128},{128,0},{64,192},{192,64},{256,384},{384,256},{320,448},{4... | collective-permute-start | bytes 589832 | tf_op jit(solution)/shard_map/ppermute | solution.py:257
  169.7 0.6 copy.8
  170.3 2.8 %collective-permute-done.18.refs_3_ = bf16[768,128]{1,0:T(8,128)(2,1)S(1)} collective-permute-done((bf16[768,128]{1,0:T(8,128)(2,1)S(1)}, bf16[768,128]{1,0:T(8,128)(2,1)S(1)}, u32[]{:S(2)}, u32[]{:S(2)}) %collective-permute-start.18) | collective-permute-done | bytes 196640 | tf_op jit(solution)/shard_map/ppermute | solution.py:257
  173.1 6.8 %collective-permute-done.16.refs_2_ = bf16[768,128]{1,0:T(8,128)(2,1)S(1)} collective-permute-done((bf16[768,128]{1,0:T(8,128)(2,1)S(1)}, bf16[768,128]{1,0:T(8,128)(2,1)S(1)}, u32[]{:S(2)}, u32[]{:S(2)}) %collective-permute-start.16) | collective-permute-done | bytes 196640 | tf_op jit(solution)/shard_map/ppermute | solution.py:257
  179.9 0.9 shard_map.51
  (24 shorter events, 0.5 us)
Async XLA Ops:
  0.6 27.2 %collective-permute-start = (bf16[256,2,768]{2,1,0:T(2,128)(2,1)}, bf16[256,2,768]{2,1,0:T(2,128)(2,1)S(1)}, u32[]{:S(2)}, u32[]{:S(2)}) collective-permute-start(bf16[256,2,768]{2,1,0:T(2,128)(2,1)} %param.2), channel_id=1, source_target_pairs={{0,32},{32,0},{1,33},{33,1},{2,34},{34,2},{3,35},{35,3},{4,36},{36... | collective-permute-start | bytes 2359304 | tf_op jit(solution)/shard_map/ppermute | solution.py:240
  9.4 13.2 %collective-permute-start.3 = (bf16[128,768]{1,0:T(8,128)(2,1)}, bf16[128,768]{1,0:T(8,128)(2,1)S(1)}, u32[]{:S(2)}, u32[]{:S(2)}) collective-permute-start(bf16[128,768]{1,0:T(8,128)(2,1)} %refs_0_.1), channel_id=1, source_target_pairs={{0,128},{128,0},{64,192},{192,64},{256,384},{384,256},{320,448},{4... | collective-permute-start | bytes 589832 | tf_op jit(solution)/shard_map/ppermute | solution.py:257
  11.4 11.2 %collective-permute-start.4 = (bf16[128,768]{1,0:T(8,128)(2,1)}, bf16[128,768]{1,0:T(8,128)(2,1)S(1)}, u32[]{:S(2)}, u32[]{:S(2)}) collective-permute-start(bf16[128,768]{1,0:T(8,128)(2,1)} %refs_0_.1), channel_id=1, source_target_pairs={{128,256},{256,128},{192,320},{320,192},{384,0},{0,384},{448,64},{... | collective-permute-start | bytes 589832 | tf_op jit(solution)/shard_map/ppermute | solution.py:257
  13.7 20.8 %collective-permute-start.2 = (bf16[128,768]{1,0:T(8,128)(2,1)}, bf16[128,768]{1,0:T(8,128)(2,1)S(1)}, u32[]{:S(2)}, u32[]{:S(2)}) collective-permute-start(bf16[128,768]{1,0:T(8,128)(2,1)} %refs_0_.1), channel_id=1, source_target_pairs={{64,128},{128,64},{192,256},{256,192},{320,384},{384,320},{448,0},... | collective-permute-start | bytes 589832 | tf_op jit(solution)/shard_map/ppermute | solution.py:257
  16.0 18.5 %collective-permute-start.1 = (bf16[128,768]{1,0:T(8,128)(2,1)}, bf16[128,768]{1,0:T(8,128)(2,1)S(1)}, u32[]{:S(2)}, u32[]{:S(2)}) collective-permute-start(bf16[128,768]{1,0:T(8,128)(2,1)} %refs_0_.1), channel_id=1, source_target_pairs={{0,64},{64,0},{128,192},{192,128},{256,320},{320,256},{384,448},{4... | collective-permute-start | bytes 589832 | tf_op jit(solution)/shard_map/ppermute | solution.py:257
  22.6 11.9 %collective-permute-start.5 = (bf16[128,768]{1,0:T(8,128)(2,1)S(1)}, bf16[128,768]{1,0:T(8,128)(2,1)S(1)}, u32[]{:S(2)}, u32[]{:S(2)}) collective-permute-start(bf16[128,768]{1,0:T(8,128)(2,1)S(1)} %get-tuple-element.75), channel_id=1, source_target_pairs={{64,128},{128,64},{192,256},{256,192},{320,384},{384,320},{448,0},... | collective-permute-start | bytes 589832 | tf_op jit(solution)/shard_map/ppermute | solution.py:257
  24.6 11.9 %collective-permute-start.7 = (bf16[128,768]{1,0:T(8,128)(2,1)S(1)}, bf16[128,768]{1,0:T(8,128)(2,1)S(1)}, u32[]{:S(2)}, u32[]{:S(2)}) collective-permute-start(bf16[128,768]{1,0:T(8,128)(2,1)S(1)} %collective-permute-done.4.refs_4_), channel_id=1, source_target_pairs={{0,128},{128,0},{64,192},{192,64},{256,384},{384,256},{320,448},{4... | collective-permute-start | bytes 589832 | tf_op jit(solution)/shard_map/ppermute | solution.py:257
  27.9 10.9 %collective-permute-start.6 = (bf16[128,768]{1,0:T(8,128)(2,1)S(1)}, bf16[128,768]{1,0:T(8,128)(2,1)S(1)}, u32[]{:S(2)}, u32[]{:S(2)}) collective-permute-start(bf16[128,768]{1,0:T(8,128)(2,1)S(1)} %get-tuple-element.74), channel_id=1, source_target_pairs={{0,64},{64,0},{128,192},{192,128},{256,320},{320,256},{384,448},{4... | collective-permute-start | bytes 589832 | tf_op jit(solution)/shard_map/ppermute | solution.py:257
  33.5 1.1 copy-start
  50.6 4.8 %collective-permute-start.8 = (f32[16,128]{1,0:T(8,128)S(1)}, f32[16,128]{1,0:T(8,128)S(1)}, u32[]{:S(2)}, u32[]{:S(2)}) collective-permute-start(f32[16,128]{1,0:T(8,128)S(1)} %shard_map.44), channel_id=1, source_target_pairs={{0,32},{32,0},{1,33},{33,1},{2,34},{34,2},{3,35},{35,3},{4,36},{36... | collective-permute-start | bytes 24584 | tf_op jit(solution)/shard_map/ppermute | solution.py:240
  87.2 6.0 %collective-permute-start.9 = (f32[8,128]{1,0:T(8,128)S(1)}, f32[8,128]{1,0:T(8,128)S(1)}, u32[]{:S(2)}, u32[]{:S(2)}) collective-permute-start(f32[8,128]{1,0:T(8,128)S(1)} %shard_map.46), channel_id=1, source_target_pairs={{0,32},{32,0},{1,33},{33,1},{2,34},{34,2},{3,35},{35,3},{4,36},{36... | collective-permute-start | bytes 12296 | tf_op jit(solution)/shard_map/ppermute | solution.py:240
  115.9 6.0 %collective-permute-start.10 = (f32[8,128]{1,0:T(8,128)S(1)}, f32[8,128]{1,0:T(8,128)S(1)}, u32[]{:S(2)}, u32[]{:S(2)}) collective-permute-start(f32[8,128]{1,0:T(8,128)S(1)} %shard_map.48), channel_id=1, source_target_pairs={{0,32},{32,0},{1,33},{33,1},{2,34},{34,2},{3,35},{35,3},{4,36},{36... | collective-permute-start | bytes 12296 | tf_op jit(solution)/shard_map/ppermute | solution.py:240
  137.1 6.0 %collective-permute-start.11 = (bf16[32,16,768]{2,1,0:T(8,128)(2,1)S(1)}, bf16[32,16,768]{2,1,0:T(8,128)(2,1)S(1)}, u32[]{:S(2)}, u32[]{:S(2)}) collective-permute-start(bf16[32,16,768]{2,1,0:T(8,128)(2,1)S(1)} %get-tuple-element.60), channel_id=1, source_target_pairs={{0,32},{32,0},{1,33},{33,1},{2,34},{34,2},{3,35},{35,3},{4,36},{36... | collective-permute-start | bytes 2359304 | tf_op jit(solution)/shard_map/ppermute | solution.py:240
  144.2 25.4 %all-to-all-start.6 = ((bf16[32,16,768]{2,1,0:T(8,128)(2,1)}), bf16[32,16,768]{2,1,0:T(8,128)(2,1)S(1)}, u32[]{:S(2)}, u32[]{:S(2)}) async-start(bf16[32,16,768]{2,1,0:T(8,128)(2,1)} %add_convert_fusion), calls=%async_computation.6 | async-start | bytes 1572864 | tf_op jit(solution)/shard_map/all_to_all | solution.py:351
  148.1 13.9 %collective-permute-start.14 = (bf16[768,128]{1,0:T(8,128)(2,1)S(1)}, bf16[768,128]{1,0:T(8,128)(2,1)S(1)}, u32[]{:S(2)}, u32[]{:S(2)}) collective-permute-start(bf16[768,128]{1,0:T(8,128)(2,1)S(1)} %get-tuple-element.66), channel_id=1, source_target_pairs={{64,128},{128,64},{192,256},{256,192},{320,384},{384,320},{448,0},... | collective-permute-start | bytes 589832 | tf_op jit(solution)/shard_map/ppermute | solution.py:257
  150.3 11.7 %collective-permute-start.15 = (bf16[768,128]{1,0:T(8,128)(2,1)S(1)}, bf16[768,128]{1,0:T(8,128)(2,1)S(1)}, u32[]{:S(2)}, u32[]{:S(2)}) collective-permute-start(bf16[768,128]{1,0:T(8,128)(2,1)S(1)} %get-tuple-element.67), channel_id=1, source_target_pairs={{0,64},{64,0},{128,192},{192,128},{256,320},{320,256},{384,448},{4... | collective-permute-start | bytes 589832 | tf_op jit(solution)/shard_map/ppermute | solution.py:257
  152.5 12.1 %collective-permute-start.17 = (bf16[768,128]{1,0:T(8,128)(2,1)S(1)}, bf16[768,128]{1,0:T(8,128)(2,1)S(1)}, u32[]{:S(2)}, u32[]{:S(2)}) collective-permute-start(bf16[768,128]{1,0:T(8,128)(2,1)S(1)} %get-tuple-element.69), channel_id=1, source_target_pairs={{0,128},{128,0},{64,192},{192,64},{256,384},{384,256},{320,448},{4... | collective-permute-start | bytes 589832 | tf_op jit(solution)/shard_map/ppermute | solution.py:257
  155.2 15.1 %collective-permute-start.12 = (bf16[768,128]{1,0:T(8,128)(2,1)S(1)}, bf16[768,128]{1,0:T(8,128)(2,1)S(1)}, u32[]{:S(2)}, u32[]{:S(2)}) collective-permute-start(bf16[768,128]{1,0:T(8,128)(2,1)S(1)} %get-tuple-element.63), channel_id=1, source_target_pairs={{0,64},{64,0},{128,192},{192,128},{256,320},{320,256},{384,448},{4... | collective-permute-start | bytes 589832 | tf_op jit(solution)/shard_map/ppermute | solution.py:257
  159.6 10.7 %collective-permute-start.13 = (bf16[768,128]{1,0:T(8,128)(2,1)S(1)}, bf16[768,128]{1,0:T(8,128)(2,1)S(1)}, u32[]{:S(2)}, u32[]{:S(2)}) collective-permute-start(bf16[768,128]{1,0:T(8,128)(2,1)S(1)} %get-tuple-element.64), channel_id=1, source_target_pairs={{64,128},{128,64},{192,256},{256,192},{320,384},{384,320},{448,0},... | collective-permute-start | bytes 589832 | tf_op jit(solution)/shard_map/ppermute | solution.py:257
  164.7 8.4 %collective-permute-start.18 = (bf16[768,128]{1,0:T(8,128)(2,1)S(1)}, bf16[768,128]{1,0:T(8,128)(2,1)S(1)}, u32[]{:S(2)}, u32[]{:S(2)}) collective-permute-start(bf16[768,128]{1,0:T(8,128)(2,1)S(1)} %get-tuple-element.72), channel_id=1, source_target_pairs={{128,256},{256,128},{192,320},{320,192},{384,0},{0,384},{448,64},{... | collective-permute-start | bytes 589832 | tf_op jit(solution)/shard_map/ppermute | solution.py:257
  166.7 13.2 %collective-permute-start.16 = (bf16[768,128]{1,0:T(8,128)(2,1)S(1)}, bf16[768,128]{1,0:T(8,128)(2,1)S(1)}, u32[]{:S(2)}, u32[]{:S(2)}) collective-permute-start(bf16[768,128]{1,0:T(8,128)(2,1)S(1)} %get-tuple-element.73), channel_id=1, source_target_pairs={{0,128},{128,0},{64,192},{192,64},{256,384},{384,256},{320,448},{4... | collective-permute-start | bytes 589832 | tf_op jit(solution)/shard_map/ppermute | solution.py:257

commit v7 on v6

--- a/solution.py
+++ b/solution.py
@@ -198,7 +198,7 @@
 ):
     s = places()
     total[...] = jnp.sum(col_ref[...].astype(F32), axis=0)
-    clips[...] = jnp.sum(row_ref[...], axis=0)
+    clips[...] = jnp.sum(row_ref[...].astype(F32), axis=0)
     for half, ref in ((1, other_ref), (0, mine_ref)):
         rows = clips_of(half)
         code = [clip_scale(s, view, half, clips, SCALE) for view in range(VIEWS)]
@@ -326,7 +326,7 @@
     (row_part,) = call(
         functools.partial(row_kernel, False), (early, late, col_part), [row_out], [cols, rows8]
     )
-    row_part = group_sums(row_part, F32)
+    row_part = group_sums(row_part, BF16)
     (col_part,) = call(
         functools.partial(col_kernel, False), (early, late, row_part), [col_out], [rows8, cols]
     )
@@ -334,7 +334,7 @@
     (row_part,) = call(
         functools.partial(row_kernel, False), (early, late, col_part), [row_out], [cols, rows8]
     )
-    row_part = group_sums(row_part, F32)
+    row_part = group_sums(row_part, BF16)
 
     ge_out = ((XS * ZS, 16, WIDTH), BF16)
     mine, other, grads = call(

time: 182 us -> 180 us (0.989)
  no operation moved by 1% of the time
where the time goes in v7:
time: 180 us; the launch traced here: 179 us
  blocking collectives  74 us (41%)
  starting transfers between devices  70.1 us (39%)
  waiting for transfers between devices  18.5 us (10%)
  Pallas kernels  12 us (7%)
  local copies, waits for them, and re-layouts  1.98 us (1%)
    all_to_all x3, blocking collectives, group_sums(): return lax.all_to_all(part, ('z', 'x'), 0, 0)  45 us
    ppermute x14, starting transfers between devices, swap(): return lax.ppermute(part, ('y', 'core'), pairs)  39.7 us
    all_to_all x3, blocking collectives, y_sums(): return lax.all_to_all(part, 'y', 0, 0)  29 us
    ppermute x5, starting transfers between devices, shift(): return lax.ppermute(part, axis, [(i, (i + by) % size) for i in range(size)])  26.5 us
    ppermute x14, waiting for transfers between devices, swap(): return lax.ppermute(part, ('y', 'core'), pairs)  16 us
    pallas_call x11, Pallas kernels, call(): pl.pallas_call(kernel, out_shape=[jax.ShapeDtypeStruct(shape, dtype) for...  12 us
    all_to_all x1, starting transfers between devices, on_device(): part = lax.all_to_all(part, ('x', 'z'), 0, 0)  3.91 us
  transfers between devices with their start and end apart: 20, of which 8 were waited for; matrix products, arithmetic and copies ran while one was open for 1% of the time, Pallas kernels for 3%

profile of v7, /device:TPU:1, one launch (start us, length us, event | category | flops | bytes accessed | tf_op | source)
XLA Modules:
  0.0 178.9 jit_solution(14733915945513928695)
XLA Ops:
  0.6 8.8 %collective-permute-start = (bf16[256,2,768]{2,1,0:T(2,128)(2,1)}, bf16[256,2,768]{2,1,0:T(2,128)(2,1)S(1)}, u32[]{:S(2)}, u32[]{:S(2)}) collective-permute-start(bf16[256,2,768]{2,1,0:T(2,128)(2,1)} %param.2), channel_id=1, source_target_pairs={{0,32},{32,0},{1,33},{33,1},{2,34},{34,2},{3,35},{35,3},{4,36},{36... | collective-permute-start | bytes 2359304 | tf_op jit(solution)/shard_map/ppermute | solution.py:240
  9.4 1.9 %collective-permute-start.3 = (bf16[128,768]{1,0:T(8,128)(2,1)}, bf16[128,768]{1,0:T(8,128)(2,1)S(1)}, u32[]{:S(2)}, u32[]{:S(2)}) collective-permute-start(bf16[128,768]{1,0:T(8,128)(2,1)} %refs_0_.1), channel_id=1, source_target_pairs={{0,128},{128,0},{64,192},{192,64},{256,384},{384,256},{320,448},{4... | collective-permute-start | bytes 589832 | tf_op jit(solution)/shard_map/ppermute | solution.py:257
  11.4 2.4 %collective-permute-start.4 = (bf16[128,768]{1,0:T(8,128)(2,1)}, bf16[128,768]{1,0:T(8,128)(2,1)S(1)}, u32[]{:S(2)}, u32[]{:S(2)}) collective-permute-start(bf16[128,768]{1,0:T(8,128)(2,1)} %refs_0_.1), channel_id=1, source_target_pairs={{128,256},{256,128},{192,320},{320,192},{384,0},{0,384},{448,64},{... | collective-permute-start | bytes 589832 | tf_op jit(solution)/shard_map/ppermute | solution.py:257
  13.7 2.3 %collective-permute-start.2 = (bf16[128,768]{1,0:T(8,128)(2,1)}, bf16[128,768]{1,0:T(8,128)(2,1)S(1)}, u32[]{:S(2)}, u32[]{:S(2)}) collective-permute-start(bf16[128,768]{1,0:T(8,128)(2,1)} %refs_0_.1), channel_id=1, source_target_pairs={{64,128},{128,64},{192,256},{256,192},{320,384},{384,320},{448,0},... | collective-permute-start | bytes 589832 | tf_op jit(solution)/shard_map/ppermute | solution.py:257
  16.0 4.9 %collective-permute-start.1 = (bf16[128,768]{1,0:T(8,128)(2,1)}, bf16[128,768]{1,0:T(8,128)(2,1)S(1)}, u32[]{:S(2)}, u32[]{:S(2)}) collective-permute-start(bf16[128,768]{1,0:T(8,128)(2,1)} %refs_0_.1), channel_id=1, source_target_pairs={{0,64},{64,0},{128,192},{192,128},{256,320},{320,256},{384,448},{4... | collective-permute-start | bytes 589832 | tf_op jit(solution)/shard_map/ppermute | solution.py:257
  21.0 1.6 collective-permute-done.3.refs_3_
  22.6 1.9 %collective-permute-start.5 = (bf16[128,768]{1,0:T(8,128)(2,1)S(1)}, bf16[128,768]{1,0:T(8,128)(2,1)S(1)}, u32[]{:S(2)}, u32[]{:S(2)}) collective-permute-start(bf16[128,768]{1,0:T(8,128)(2,1)S(1)} %get-tuple-element.75), channel_id=1, source_target_pairs={{64,128},{128,64},{192,256},{256,192},{320,384},{384,320},{448,0},... | collective-permute-start | bytes 589832 | tf_op jit(solution)/shard_map/ppermute | solution.py:257
  24.6 3.3 %collective-permute-start.7 = (bf16[128,768]{1,0:T(8,128)(2,1)S(1)}, bf16[128,768]{1,0:T(8,128)(2,1)S(1)}, u32[]{:S(2)}, u32[]{:S(2)}) collective-permute-start(bf16[128,768]{1,0:T(8,128)(2,1)S(1)} %collective-permute-done.4.refs_4_), channel_id=1, source_target_pairs={{0,128},{128,0},{64,192},{192,64},{256,384},{384,256},{320,448},{4... | collective-permute-start | bytes 589832 | tf_op jit(solution)/shard_map/ppermute | solution.py:257
  27.9 4.4 %collective-permute-start.6 = (bf16[128,768]{1,0:T(8,128)(2,1)S(1)}, bf16[128,768]{1,0:T(8,128)(2,1)S(1)}, u32[]{:S(2)}, u32[]{:S(2)}) collective-permute-start(bf16[128,768]{1,0:T(8,128)(2,1)S(1)} %get-tuple-element.74), channel_id=1, source_target_pairs={{0,64},{64,0},{128,192},{192,128},{256,320},{320,256},{384,448},{4... | collective-permute-start | bytes 589832 | tf_op jit(solution)/shard_map/ppermute | solution.py:257
  32.2 1.2 copy.12
  33.6 0.9 shard_map.41
  34.6 1.9 %shard_map.42 = (f32[2,512,768]{2,1,0:T(8,128)S(1)}, f32[16,128]{1,0:T(8,128)S(1)}, f32[8,128]{1,0:T(8,128)S(1)}, bf16[768,768]{1,0:T(8,128)(2,1)S(1)}) custom-call(bf16[2,512,768]{2,1,0:T(8,128)(2,1)S(1)} %get-tuple-element.36.rows, bf16[128,768]{1,0:T(8,128)(2,1)S(1)} %copy-done, bf16[128,768]{1,0:T(8,128)(2,1)S(1)} %collective-permute-done.1.refs_1_, ...), custom_call_target="tpu_custom_call" | custom-call | flops 1207959552 | bytes 2097152 | tf_op jit(solution)/shard_map/pallas_call | solution.py:30
  36.5 2.3 %collective-permute-done.6.refs_0_ = bf16[128,768]{1,0:T(8,128)(2,1)S(1)} collective-permute-done((bf16[128,768]{1,0:T(8,128)(2,1)S(1)}, bf16[128,768]{1,0:T(8,128)(2,1)S(1)}, u32[]{:S(2)}, u32[]{:S(2)}) %collective-permute-start.6) | collective-permute-done | bytes 196640 | tf_op jit(solution)/shard_map/ppermute | solution.py:257
  38.7 0.9 shard_map.43
  39.6 10.5 %all_to_all.35.recv_ref = bf16[8,16,128]{2,1,0:T(8,128)(2,1)S(1)} all-to-all(bf16[8,16,128]{2,1,0:T(8,128)(2,1)S(1)} %get-tuple-element.41), channel_id=1, replica_groups=mesh['y'=8,'core'=2,'x'=4,'z'=8] {'y'}, dimensions={0} | all-to-all | bytes 65536 | tf_op jit(solution)/shard_map/all_to_all | solution.py:281
  50.1 0.6 shard_map.44
  50.6 4.0 %collective-permute-start.8 = (f32[16,128]{1,0:T(8,128)S(1)}, f32[16,128]{1,0:T(8,128)S(1)}, u32[]{:S(2)}, u32[]{:S(2)}) collective-permute-start(f32[16,128]{1,0:T(8,128)S(1)} %shard_map.44), channel_id=1, source_target_pairs={{0,32},{32,0},{1,33},{33,1},{2,34},{34,2},{3,35},{35,3},{4,36},{36... | collective-permute-start | bytes 24584 | tf_op jit(solution)/shard_map/ppermute | solution.py:240
  54.7 0.8 collective-permute-done.8
  55.5 21.3 %all_to_all.36.recv_ref = bf16[32,16,128]{2,1,0:T(8,128)(2,1)S(1)} all-to-all(bf16[32,16,128]{2,1,0:T(8,128)(2,1)S(1)} %broadcast_in_dim.6), channel_id=1, replica_groups=mesh['y'=8,'core'=2,'x'=4,'z'=8] {'z','x'}, dimensions={0} | all-to-all | bytes 262144 | tf_op jit(solution)/shard_map/all_to_all | solution.py:287
  76.9 0.6 shard_map.45
  77.4 9.2 %all_to_all.37.recv_ref = bf16[8,16,128]{2,1,0:T(8,128)(2,1)S(1)} all-to-all(bf16[8,16,128]{2,1,0:T(8,128)(2,1)S(1)} %get-tuple-element.43), channel_id=1, replica_groups=mesh['y'=8,'core'=2,'x'=4,'z'=8] {'y'}, dimensions={0} | all-to-all | bytes 65536 | tf_op jit(solution)/shard_map/all_to_all | solution.py:281
  86.7 0.6 shard_map.46
  87.2 5.1 %collective-permute-start.9 = (f32[8,128]{1,0:T(8,128)S(1)}, f32[8,128]{1,0:T(8,128)S(1)}, u32[]{:S(2)}, u32[]{:S(2)}) collective-permute-start(f32[8,128]{1,0:T(8,128)S(1)} %shard_map.46), channel_id=1, source_target_pairs={{0,32},{32,0},{1,33},{33,1},{2,34},{34,2},{3,35},{35,3},{4,36},{36... | collective-permute-start | bytes 12296 | tf_op jit(solution)/shard_map/ppermute | solution.py:240
  92.4 0.8 collective-permute-done.9
  93.2 11.8 %all_to_all.38.recv_ref = bf16[32,8,128]{2,1,0:T(8,128)(2,1)S(1)} all-to-all(bf16[32,8,128]{2,1,0:T(8,128)(2,1)S(1)} %broadcast_in_dim.7), channel_id=1, replica_groups=mesh['y'=8,'core'=2,'x'=4,'z'=8] {'z','x'}, dimensions={0} | all-to-all | bytes 131072 | tf_op jit(solution)/shard_map/all_to_all | solution.py:287
  105.0 0.6 shard_map.47
  105.6 9.2 %all_to_all.39.recv_ref.col_ref = bf16[8,16,128]{2,1,0:T(8,128)(2,1)S(1)} all-to-all(bf16[8,16,128]{2,1,0:T(8,128)(2,1)S(1)} %shard_map.47), channel_id=1, replica_groups=mesh['y'=8,'core'=2,'x'=4,'z'=8] {'y'}, dimensions={0} | all-to-all | bytes 65536 | tf_op jit(solution)/shard_map/all_to_all | solution.py:281
  114.9 0.6 shard_map.48
  115.4 4.8 %collective-permute-start.10 = (f32[8,128]{1,0:T(8,128)S(1)}, f32[8,128]{1,0:T(8,128)S(1)}, u32[]{:S(2)}, u32[]{:S(2)}) collective-permute-start(f32[8,128]{1,0:T(8,128)S(1)} %shard_map.48), channel_id=1, source_target_pairs={{0,32},{32,0},{1,33},{33,1},{2,34},{34,2},{3,35},{35,3},{4,36},{36... | collective-permute-start | bytes 12296 | tf_op jit(solution)/shard_map/ppermute | solution.py:240
  120.3 0.8 collective-permute-done.10
  121.1 11.8 %all_to_all.40.row_ref = bf16[32,8,128]{2,1,0:T(8,128)(2,1)S(1)} all-to-all(bf16[32,8,128]{2,1,0:T(8,128)(2,1)S(1)} %broadcast_in_dim.8), channel_id=1, replica_groups=mesh['y'=8,'core'=2,'x'=4,'z'=8] {'z','x'}, dimensions={0} | all-to-all | bytes 131072 | tf_op jit(solution)/shard_map/all_to_all | solution.py:287
  132.9 2.8 %shard_map.49 = (bf16[32,16,768]{2,1,0:T(8,128)(2,1)S(1)}, bf16[32,16,768]{2,1,0:T(8,128)(2,1)S(1)}, bf16[1024,1024]{1,0:T(8,128)(2,1)S(1)}) custom-call(f32[2,512,768]{2,1,0:T(8,128)S(1)} %get-tuple-element.37.early, f32[2,512,256]{2,1,0:T(8,128)S(1)} %get-tuple-element.40.late, bf16[32,8,128]{2,1,0:T(8,128)(2,1)S(1)} %all_to_all.40.row_ref, ...), custom_call_target="tpu_custom_call" | custom-call | flops 1610612736 | bytes 2097152 | tf_op jit(solution)/shard_map/pallas_call | solution.py:30
  135.7 3.7 %collective-permute-start.11 = (bf16[32,16,768]{2,1,0:T(8,128)(2,1)S(1)}, bf16[32,16,768]{2,1,0:T(8,128)(2,1)S(1)}, u32[]{:S(2)}, u32[]{:S(2)}) collective-permute-start(bf16[32,16,768]{2,1,0:T(8,128)(2,1)S(1)} %get-tuple-element.60), channel_id=1, source_target_pairs={{0,32},{32,0},{1,33},{33,1},{2,34},{34,2},{3,35},{35,3},{4,36},{36... | collective-permute-start | bytes 2359304 | tf_op jit(solution)/shard_map/ppermute | solution.py:240
  139.4 1.8 %shard_map.50 = (bf16[768,128]{1,0:T(8,128)(2,1)S(1)}, bf16[768,128]{1,0:T(8,128)(2,1)S(1)}, bf16[768,128]{1,0:T(8,128)(2,1)S(1)}, bf16[768,128]{1,0:T(8,128)(2,...) custom-call(bf16[768,1024]{1,0:T(8,128)(2,1)S(1)} %get-tuple-element, ...), custom_call_target="tpu_custom_call" | custom-call | flops 1610612736 | bytes 2097152 | tf_op jit(solution)/shard_map/pallas_call | solution.py:30
  141.2 1.1 add_convert_fusion
  142.3 3.9 %all-to-all-start.6 = ((bf16[32,16,768]{2,1,0:T(8,128)(2,1)}), bf16[32,16,768]{2,1,0:T(8,128)(2,1)S(1)}, u32[]{:S(2)}, u32[]{:S(2)}) async-start(bf16[32,16,768]{2,1,0:T(8,128)(2,1)} %add_convert_fusion), calls=%async_computation.6 | async-start | bytes 1572864 | tf_op jit(solution)/shard_map/all_to_all | solution.py:351
  146.2 2.2 %collective-permute-start.14 = (bf16[768,128]{1,0:T(8,128)(2,1)S(1)}, bf16[768,128]{1,0:T(8,128)(2,1)S(1)}, u32[]{:S(2)}, u32[]{:S(2)}) collective-permute-start(bf16[768,128]{1,0:T(8,128)(2,1)S(1)} %get-tuple-element.66), channel_id=1, source_target_pairs={{64,128},{128,64},{192,256},{256,192},{320,384},{384,320},{448,0},... | collective-permute-start | bytes 589832 | tf_op jit(solution)/shard_map/ppermute | solution.py:257
  148.4 2.2 %collective-permute-start.15 = (bf16[768,128]{1,0:T(8,128)(2,1)S(1)}, bf16[768,128]{1,0:T(8,128)(2,1)S(1)}, u32[]{:S(2)}, u32[]{:S(2)}) collective-permute-start(bf16[768,128]{1,0:T(8,128)(2,1)S(1)} %get-tuple-element.67), channel_id=1, source_target_pairs={{0,64},{64,0},{128,192},{192,128},{256,320},{320,256},{384,448},{4... | collective-permute-start | bytes 589832 | tf_op jit(solution)/shard_map/ppermute | solution.py:257
  150.6 2.8 %collective-permute-start.17 = (bf16[768,128]{1,0:T(8,128)(2,1)S(1)}, bf16[768,128]{1,0:T(8,128)(2,1)S(1)}, u32[]{:S(2)}, u32[]{:S(2)}) collective-permute-start(bf16[768,128]{1,0:T(8,128)(2,1)S(1)} %get-tuple-element.69), channel_id=1, source_target_pairs={{0,128},{128,0},{64,192},{192,64},{256,384},{384,256},{320,448},{4... | collective-permute-start | bytes 589832 | tf_op jit(solution)/shard_map/ppermute | solution.py:257
  153.4 4.4 %collective-permute-start.12 = (bf16[768,128]{1,0:T(8,128)(2,1)S(1)}, bf16[768,128]{1,0:T(8,128)(2,1)S(1)}, u32[]{:S(2)}, u32[]{:S(2)}) collective-permute-start(bf16[768,128]{1,0:T(8,128)(2,1)S(1)} %get-tuple-element.63), channel_id=1, source_target_pairs={{0,64},{64,0},{128,192},{192,128},{256,320},{320,256},{384,448},{4... | collective-permute-start | bytes 589832 | tf_op jit(solution)/shard_map/ppermute | solution.py:257
  157.8 2.3 %collective-permute-start.13 = (bf16[768,128]{1,0:T(8,128)(2,1)S(1)}, bf16[768,128]{1,0:T(8,128)(2,1)S(1)}, u32[]{:S(2)}, u32[]{:S(2)}) collective-permute-start(bf16[768,128]{1,0:T(8,128)(2,1)S(1)} %get-tuple-element.64), channel_id=1, source_target_pairs={{64,128},{128,64},{192,256},{256,192},{320,384},{384,320},{448,0},... | collective-permute-start | bytes 589832 | tf_op jit(solution)/shard_map/ppermute | solution.py:257
  160.1 2.6 %collective-permute-done.17 = bf16[768,128]{1,0:T(8,128)(2,1)S(1)} collective-permute-done((bf16[768,128]{1,0:T(8,128)(2,1)S(1)}, bf16[768,128]{1,0:T(8,128)(2,1)S(1)}, u32[]{:S(2)}, u32[]{:S(2)}) %collective-permute-start.17) | collective-permute-done | bytes 196640 | tf_op jit(solution)/shard_map/ppermute | solution.py:257
  162.9 1.9 %collective-permute-start.18 = (bf16[768,128]{1,0:T(8,128)(2,1)S(1)}, bf16[768,128]{1,0:T(8,128)(2,1)S(1)}, u32[]{:S(2)}, u32[]{:S(2)}) collective-permute-start(bf16[768,128]{1,0:T(8,128)(2,1)S(1)} %get-tuple-element.72), channel_id=1, source_target_pairs={{128,256},{256,128},{192,320},{320,192},{384,0},{0,384},{448,64},{... | collective-permute-start | bytes 589832 | tf_op jit(solution)/shard_map/ppermute | solution.py:257
  164.8 2.9 %collective-permute-start.16 = (bf16[768,128]{1,0:T(8,128)(2,1)S(1)}, bf16[768,128]{1,0:T(8,128)(2,1)S(1)}, u32[]{:S(2)}, u32[]{:S(2)}) collective-permute-start(bf16[768,128]{1,0:T(8,128)(2,1)S(1)} %get-tuple-element.73), channel_id=1, source_target_pairs={{0,128},{128,0},{64,192},{192,64},{256,384},{384,256},{320,448},{4... | collective-permute-start | bytes 589832 | tf_op jit(solution)/shard_map/ppermute | solution.py:257
  167.8 0.6 copy.8
  168.4 2.8 %collective-permute-done.18.refs_3_ = bf16[768,128]{1,0:T(8,128)(2,1)S(1)} collective-permute-done((bf16[768,128]{1,0:T(8,128)(2,1)S(1)}, bf16[768,128]{1,0:T(8,128)(2,1)S(1)}, u32[]{:S(2)}, u32[]{:S(2)}) %collective-permute-start.18) | collective-permute-done | bytes 196640 | tf_op jit(solution)/shard_map/ppermute | solution.py:257
  171.2 6.8 %collective-permute-done.16.refs_2_ = bf16[768,128]{1,0:T(8,128)(2,1)S(1)} collective-permute-done((bf16[768,128]{1,0:T(8,128)(2,1)S(1)}, bf16[768,128]{1,0:T(8,128)(2,1)S(1)}, u32[]{:S(2)}, u32[]{:S(2)}) %collective-permute-start.16) | collective-permute-done | bytes 196640 | tf_op jit(solution)/shard_map/ppermute | solution.py:257
  178.0 0.9 shard_map.51
  (24 shorter events, 0.5 us)
Async XLA Ops:
  0.6 27.2 %collective-permute-start = (bf16[256,2,768]{2,1,0:T(2,128)(2,1)}, bf16[256,2,768]{2,1,0:T(2,128)(2,1)S(1)}, u32[]{:S(2)}, u32[]{:S(2)}) collective-permute-start(bf16[256,2,768]{2,1,0:T(2,128)(2,1)} %param.2), channel_id=1, source_target_pairs={{0,32},{32,0},{1,33},{33,1},{2,34},{34,2},{3,35},{35,3},{4,36},{36... | collective-permute-start | bytes 2359304 | tf_op jit(solution)/shard_map/ppermute | solution.py:240
  9.4 13.2 %collective-permute-start.3 = (bf16[128,768]{1,0:T(8,128)(2,1)}, bf16[128,768]{1,0:T(8,128)(2,1)S(1)}, u32[]{:S(2)}, u32[]{:S(2)}) collective-permute-start(bf16[128,768]{1,0:T(8,128)(2,1)} %refs_0_.1), channel_id=1, source_target_pairs={{0,128},{128,0},{64,192},{192,64},{256,384},{384,256},{320,448},{4... | collective-permute-start | bytes 589832 | tf_op jit(solution)/shard_map/ppermute | solution.py:257
  11.4 11.2 %collective-permute-start.4 = (bf16[128,768]{1,0:T(8,128)(2,1)}, bf16[128,768]{1,0:T(8,128)(2,1)S(1)}, u32[]{:S(2)}, u32[]{:S(2)}) collective-permute-start(bf16[128,768]{1,0:T(8,128)(2,1)} %refs_0_.1), channel_id=1, source_target_pairs={{128,256},{256,128},{192,320},{320,192},{384,0},{0,384},{448,64},{... | collective-permute-start | bytes 589832 | tf_op jit(solution)/shard_map/ppermute | solution.py:257
  13.7 20.8 %collective-permute-start.2 = (bf16[128,768]{1,0:T(8,128)(2,1)}, bf16[128,768]{1,0:T(8,128)(2,1)S(1)}, u32[]{:S(2)}, u32[]{:S(2)}) collective-permute-start(bf16[128,768]{1,0:T(8,128)(2,1)} %refs_0_.1), channel_id=1, source_target_pairs={{64,128},{128,64},{192,256},{256,192},{320,384},{384,320},{448,0},... | collective-permute-start | bytes 589832 | tf_op jit(solution)/shard_map/ppermute | solution.py:257
  16.0 18.5 %collective-permute-start.1 = (bf16[128,768]{1,0:T(8,128)(2,1)}, bf16[128,768]{1,0:T(8,128)(2,1)S(1)}, u32[]{:S(2)}, u32[]{:S(2)}) collective-permute-start(bf16[128,768]{1,0:T(8,128)(2,1)} %refs_0_.1), channel_id=1, source_target_pairs={{0,64},{64,0},{128,192},{192,128},{256,320},{320,256},{384,448},{4... | collective-permute-start | bytes 589832 | tf_op jit(solution)/shard_map/ppermute | solution.py:257
  22.6 11.9 %collective-permute-start.5 = (bf16[128,768]{1,0:T(8,128)(2,1)S(1)}, bf16[128,768]{1,0:T(8,128)(2,1)S(1)}, u32[]{:S(2)}, u32[]{:S(2)}) collective-permute-start(bf16[128,768]{1,0:T(8,128)(2,1)S(1)} %get-tuple-element.75), channel_id=1, source_target_pairs={{64,128},{128,64},{192,256},{256,192},{320,384},{384,320},{448,0},... | collective-permute-start | bytes 589832 | tf_op jit(solution)/shard_map/ppermute | solution.py:257
  24.6 11.9 %collective-permute-start.7 = (bf16[128,768]{1,0:T(8,128)(2,1)S(1)}, bf16[128,768]{1,0:T(8,128)(2,1)S(1)}, u32[]{:S(2)}, u32[]{:S(2)}) collective-permute-start(bf16[128,768]{1,0:T(8,128)(2,1)S(1)} %collective-permute-done.4.refs_4_), channel_id=1, source_target_pairs={{0,128},{128,0},{64,192},{192,64},{256,384},{384,256},{320,448},{4... | collective-permute-start | bytes 589832 | tf_op jit(solution)/shard_map/ppermute | solution.py:257
  27.9 10.9 %collective-permute-start.6 = (bf16[128,768]{1,0:T(8,128)(2,1)S(1)}, bf16[128,768]{1,0:T(8,128)(2,1)S(1)}, u32[]{:S(2)}, u32[]{:S(2)}) collective-permute-start(bf16[128,768]{1,0:T(8,128)(2,1)S(1)} %get-tuple-element.74), channel_id=1, source_target_pairs={{0,64},{64,0},{128,192},{192,128},{256,320},{320,256},{384,448},{4... | collective-permute-start | bytes 589832 | tf_op jit(solution)/shard_map/ppermute | solution.py:257
  33.5 1.1 copy-start
  50.6 4.8 %collective-permute-start.8 = (f32[16,128]{1,0:T(8,128)S(1)}, f32[16,128]{1,0:T(8,128)S(1)}, u32[]{:S(2)}, u32[]{:S(2)}) collective-permute-start(f32[16,128]{1,0:T(8,128)S(1)} %shard_map.44), channel_id=1, source_target_pairs={{0,32},{32,0},{1,33},{33,1},{2,34},{34,2},{3,35},{35,3},{4,36},{36... | collective-permute-start | bytes 24584 | tf_op jit(solution)/shard_map/ppermute | solution.py:240
  87.2 6.0 %collective-permute-start.9 = (f32[8,128]{1,0:T(8,128)S(1)}, f32[8,128]{1,0:T(8,128)S(1)}, u32[]{:S(2)}, u32[]{:S(2)}) collective-permute-start(f32[8,128]{1,0:T(8,128)S(1)} %shard_map.46), channel_id=1, source_target_pairs={{0,32},{32,0},{1,33},{33,1},{2,34},{34,2},{3,35},{35,3},{4,36},{36... | collective-permute-start | bytes 12296 | tf_op jit(solution)/shard_map/ppermute | solution.py:240
  115.4 5.6 %collective-permute-start.10 = (f32[8,128]{1,0:T(8,128)S(1)}, f32[8,128]{1,0:T(8,128)S(1)}, u32[]{:S(2)}, u32[]{:S(2)}) collective-permute-start(f32[8,128]{1,0:T(8,128)S(1)} %shard_map.48), channel_id=1, source_target_pairs={{0,32},{32,0},{1,33},{33,1},{2,34},{34,2},{3,35},{35,3},{4,36},{36... | collective-permute-start | bytes 12296 | tf_op jit(solution)/shard_map/ppermute | solution.py:240
  135.7 5.5 %collective-permute-start.11 = (bf16[32,16,768]{2,1,0:T(8,128)(2,1)S(1)}, bf16[32,16,768]{2,1,0:T(8,128)(2,1)S(1)}, u32[]{:S(2)}, u32[]{:S(2)}) collective-permute-start(bf16[32,16,768]{2,1,0:T(8,128)(2,1)S(1)} %get-tuple-element.60), channel_id=1, source_target_pairs={{0,32},{32,0},{1,33},{33,1},{2,34},{34,2},{3,35},{35,3},{4,36},{36... | collective-permute-start | bytes 2359304 | tf_op jit(solution)/shard_map/ppermute | solution.py:240
  142.3 25.4 %all-to-all-start.6 = ((bf16[32,16,768]{2,1,0:T(8,128)(2,1)}), bf16[32,16,768]{2,1,0:T(8,128)(2,1)S(1)}, u32[]{:S(2)}, u32[]{:S(2)}) async-start(bf16[32,16,768]{2,1,0:T(8,128)(2,1)} %add_convert_fusion), calls=%async_computation.6 | async-start | bytes 1572864 | tf_op jit(solution)/shard_map/all_to_all | solution.py:351
  146.2 13.9 %collective-permute-start.14 = (bf16[768,128]{1,0:T(8,128)(2,1)S(1)}, bf16[768,128]{1,0:T(8,128)(2,1)S(1)}, u32[]{:S(2)}, u32[]{:S(2)}) collective-permute-start(bf16[768,128]{1,0:T(8,128)(2,1)S(1)} %get-tuple-element.66), channel_id=1, source_target_pairs={{64,128},{128,64},{192,256},{256,192},{320,384},{384,320},{448,0},... | collective-permute-start | bytes 589832 | tf_op jit(solution)/shard_map/ppermute | solution.py:257
  148.4 11.7 %collective-permute-start.15 = (bf16[768,128]{1,0:T(8,128)(2,1)S(1)}, bf16[768,128]{1,0:T(8,128)(2,1)S(1)}, u32[]{:S(2)}, u32[]{:S(2)}) collective-permute-start(bf16[768,128]{1,0:T(8,128)(2,1)S(1)} %get-tuple-element.67), channel_id=1, source_target_pairs={{0,64},{64,0},{128,192},{192,128},{256,320},{320,256},{384,448},{4... | collective-permute-start | bytes 589832 | tf_op jit(solution)/shard_map/ppermute | solution.py:257
  150.6 12.1 %collective-permute-start.17 = (bf16[768,128]{1,0:T(8,128)(2,1)S(1)}, bf16[768,128]{1,0:T(8,128)(2,1)S(1)}, u32[]{:S(2)}, u32[]{:S(2)}) collective-permute-start(bf16[768,128]{1,0:T(8,128)(2,1)S(1)} %get-tuple-element.69), channel_id=1, source_target_pairs={{0,128},{128,0},{64,192},{192,64},{256,384},{384,256},{320,448},{4... | collective-permute-start | bytes 589832 | tf_op jit(solution)/shard_map/ppermute | solution.py:257
  153.4 15.1 %collective-permute-start.12 = (bf16[768,128]{1,0:T(8,128)(2,1)S(1)}, bf16[768,128]{1,0:T(8,128)(2,1)S(1)}, u32[]{:S(2)}, u32[]{:S(2)}) collective-permute-start(bf16[768,128]{1,0:T(8,128)(2,1)S(1)} %get-tuple-element.63), channel_id=1, source_target_pairs={{0,64},{64,0},{128,192},{192,128},{256,320},{320,256},{384,448},{4... | collective-permute-start | bytes 589832 | tf_op jit(solution)/shard_map/ppermute | solution.py:257
  157.8 10.7 %collective-permute-start.13 = (bf16[768,128]{1,0:T(8,128)(2,1)S(1)}, bf16[768,128]{1,0:T(8,128)(2,1)S(1)}, u32[]{:S(2)}, u32[]{:S(2)}) collective-permute-start(bf16[768,128]{1,0:T(8,128)(2,1)S(1)} %get-tuple-element.64), channel_id=1, source_target_pairs={{64,128},{128,64},{192,256},{256,192},{320,384},{384,320},{448,0},... | collective-permute-start | bytes 589832 | tf_op jit(solution)/shard_map/ppermute | solution.py:257
  162.9 8.4 %collective-permute-start.18 = (bf16[768,128]{1,0:T(8,128)(2,1)S(1)}, bf16[768,128]{1,0:T(8,128)(2,1)S(1)}, u32[]{:S(2)}, u32[]{:S(2)}) collective-permute-start(bf16[768,128]{1,0:T(8,128)(2,1)S(1)} %get-tuple-element.72), channel_id=1, source_target_pairs={{128,256},{256,128},{192,320},{320,192},{384,0},{0,384},{448,64},{... | collective-permute-start | bytes 589832 | tf_op jit(solution)/shard_map/ppermute | solution.py:257
  164.8 13.2 %collective-permute-start.16 = (bf16[768,128]{1,0:T(8,128)(2,1)S(1)}, bf16[768,128]{1,0:T(8,128)(2,1)S(1)}, u32[]{:S(2)}, u32[]{:S(2)}) collective-permute-start(bf16[768,128]{1,0:T(8,128)(2,1)S(1)} %get-tuple-element.73), channel_id=1, source_target_pairs={{0,128},{128,0},{64,192},{192,64},{256,384},{384,256},{320,448},{4... | collective-permute-start | bytes 589832 | tf_op jit(solution)/shard_map/ppermute | solution.py:257

commit v8 on v7

--- a/solution.py
+++ b/solution.py
@@ -217,7 +217,7 @@
         out = out + jnp.dot(grads[part, SPLIT:], far_centers[...], preferred_element_type=F32)
         for place in range(XS * ZS):
             eight = [out[view * MINE + place * 8 : view * MINE + place * 8 + 8] for view in range(2)]
-            ref[place] = jnp.concatenate(eight).astype(BF16)
+            ref[place % ZS * XS + place // ZS] = jnp.concatenate(eight).astype(BF16)
 
 
 def proto_kernel(flat_ref, grads, *outs):
@@ -348,7 +348,7 @@
     theirs = shift(other, "core", CORES, 1)
     mine, sums = lax.optimization_barrier((mine, sums))
     part = add(mine, theirs)
-    part = lax.all_to_all(part, ("x", "z"), 0, 0)
+    part = lax.all_to_all(part, ("z", "x"), 0, 0)
     part = jnp.sum(part.astype(F32), axis=0).astype(BF16)
     grad_embed = part.reshape(2, 8, WIDTH).transpose(1, 0, 2)
     own, grad_embed = lax.optimization_barrier((sums[0], grad_embed))

time: 180 us -> 180 us (level)
  transfers between devices with their start and end apart: 20 -> 20, of which waited for: 8 -> 9; matrix products, arithmetic and copies ran while one was open for 1% -> 1% of each run, Pallas kernels for 3% -> 3%
where the time goes in v8:
time: 180 us; the launch traced here: 179 us
  blocking collectives  74 us (41%)
  starting transfers between devices  70.1 us (39%)
  waiting for transfers between devices  18.5 us (10%)
  Pallas kernels  12 us (7%)
  local copies, waits for them, and re-layouts  1.98 us (1%)
    all_to_all x3, blocking collectives, group_sums(): return lax.all_to_all(part, ('z', 'x'), 0, 0)  45 us
    ppermute x14, starting transfers between devices, swap(): return lax.ppermute(part, ('y', 'core'), pairs)  39.7 us
    all_to_all x3, blocking collectives, y_sums(): return lax.all_to_all(part, 'y', 0, 0)  29 us
    ppermute x5, starting transfers between devices, shift(): return lax.ppermute(part, axis, [(i, (i + by) % size) for i in range(size)])  26.5 us
    ppermute x14, waiting for transfers between devices, swap(): return lax.ppermute(part, ('y', 'core'), pairs)  15.5 us
    pallas_call x11, Pallas kernels, call(): pl.pallas_call(kernel, out_shape=[jax.ShapeDtypeStruct(shape, dtype) for...  12 us
    all_to_all x1, starting transfers between devices, on_device(): part = lax.all_to_all(part, ('z', 'x'), 0, 0)  3.91 us
  transfers between devices with their start and end apart: 20, of which 9 were waited for; matrix products, arithmetic and copies ran while one was open for 1% of the time, Pallas kernels for 3%

profile of v8, /device:TPU:1, one launch (start us, length us, event | category | flops | bytes accessed | tf_op | source)
XLA Modules:
  0.0 178.9 jit_solution(9321943606362125452)
XLA Ops:
  0.6 8.8 %collective-permute-start = (bf16[256,2,768]{2,1,0:T(2,128)(2,1)}, bf16[256,2,768]{2,1,0:T(2,128)(2,1)S(1)}, u32[]{:S(2)}, u32[]{:S(2)}) collective-permute-start(bf16[256,2,768]{2,1,0:T(2,128)(2,1)} %param.2), channel_id=1, source_target_pairs={{0,32},{32,0},{1,33},{33,1},{2,34},{34,2},{3,35},{35,3},{4,36},{36... | collective-permute-start | bytes 2359304 | tf_op jit(solution)/shard_map/ppermute | solution.py:240
  9.4 1.9 %collective-permute-start.3 = (bf16[128,768]{1,0:T(8,128)(2,1)}, bf16[128,768]{1,0:T(8,128)(2,1)S(1)}, u32[]{:S(2)}, u32[]{:S(2)}) collective-permute-start(bf16[128,768]{1,0:T(8,128)(2,1)} %refs_0_.1), channel_id=1, source_target_pairs={{0,128},{128,0},{64,192},{192,64},{256,384},{384,256},{320,448},{4... | collective-permute-start | bytes 589832 | tf_op jit(solution)/shard_map/ppermute | solution.py:257
  11.4 2.4 %collective-permute-start.4 = (bf16[128,768]{1,0:T(8,128)(2,1)}, bf16[128,768]{1,0:T(8,128)(2,1)S(1)}, u32[]{:S(2)}, u32[]{:S(2)}) collective-permute-start(bf16[128,768]{1,0:T(8,128)(2,1)} %refs_0_.1), channel_id=1, source_target_pairs={{128,256},{256,128},{192,320},{320,192},{384,0},{0,384},{448,64},{... | collective-permute-start | bytes 589832 | tf_op jit(solution)/shard_map/ppermute | solution.py:257
  13.7 2.3 %collective-permute-start.2 = (bf16[128,768]{1,0:T(8,128)(2,1)}, bf16[128,768]{1,0:T(8,128)(2,1)S(1)}, u32[]{:S(2)}, u32[]{:S(2)}) collective-permute-start(bf16[128,768]{1,0:T(8,128)(2,1)} %refs_0_.1), channel_id=1, source_target_pairs={{64,128},{128,64},{192,256},{256,192},{320,384},{384,320},{448,0},... | collective-permute-start | bytes 589832 | tf_op jit(solution)/shard_map/ppermute | solution.py:257
  16.0 4.9 %collective-permute-start.1 = (bf16[128,768]{1,0:T(8,128)(2,1)}, bf16[128,768]{1,0:T(8,128)(2,1)S(1)}, u32[]{:S(2)}, u32[]{:S(2)}) collective-permute-start(bf16[128,768]{1,0:T(8,128)(2,1)} %refs_0_.1), channel_id=1, source_target_pairs={{0,64},{64,0},{128,192},{192,128},{256,320},{320,256},{384,448},{4... | collective-permute-start | bytes 589832 | tf_op jit(solution)/shard_map/ppermute | solution.py:257
  21.0 1.6 collective-permute-done.3.refs_3_
  22.6 1.9 %collective-permute-start.5 = (bf16[128,768]{1,0:T(8,128)(2,1)S(1)}, bf16[128,768]{1,0:T(8,128)(2,1)S(1)}, u32[]{:S(2)}, u32[]{:S(2)}) collective-permute-start(bf16[128,768]{1,0:T(8,128)(2,1)S(1)} %get-tuple-element.75), channel_id=1, source_target_pairs={{64,128},{128,64},{192,256},{256,192},{320,384},{384,320},{448,0},... | collective-permute-start | bytes 589832 | tf_op jit(solution)/shard_map/ppermute | solution.py:257
  24.6 3.3 %collective-permute-start.7 = (bf16[128,768]{1,0:T(8,128)(2,1)S(1)}, bf16[128,768]{1,0:T(8,128)(2,1)S(1)}, u32[]{:S(2)}, u32[]{:S(2)}) collective-permute-start(bf16[128,768]{1,0:T(8,128)(2,1)S(1)} %collective-permute-done.4.refs_4_), channel_id=1, source_target_pairs={{0,128},{128,0},{64,192},{192,64},{256,384},{384,256},{320,448},{4... | collective-permute-start | bytes 589832 | tf_op jit(solution)/shard_map/ppermute | solution.py:257
  27.9 4.4 %collective-permute-start.6 = (bf16[128,768]{1,0:T(8,128)(2,1)S(1)}, bf16[128,768]{1,0:T(8,128)(2,1)S(1)}, u32[]{:S(2)}, u32[]{:S(2)}) collective-permute-start(bf16[128,768]{1,0:T(8,128)(2,1)S(1)} %get-tuple-element.74), channel_id=1, source_target_pairs={{0,64},{64,0},{128,192},{192,128},{256,320},{320,256},{384,448},{4... | collective-permute-start | bytes 589832 | tf_op jit(solution)/shard_map/ppermute | solution.py:257
  32.2 1.2 copy.12
  33.6 0.9 shard_map.41
  34.6 1.9 %shard_map.42 = (f32[2,512,768]{2,1,0:T(8,128)S(1)}, f32[16,128]{1,0:T(8,128)S(1)}, f32[8,128]{1,0:T(8,128)S(1)}, bf16[768,768]{1,0:T(8,128)(2,1)S(1)}) custom-call(bf16[2,512,768]{2,1,0:T(8,128)(2,1)S(1)} %get-tuple-element.36.rows, bf16[128,768]{1,0:T(8,128)(2,1)S(1)} %copy-done, bf16[128,768]{1,0:T(8,128)(2,1)S(1)} %collective-permute-done.1.refs_1_, ...), custom_call_target="tpu_custom_call" | custom-call | flops 1207959552 | bytes 2097152 | tf_op jit(solution)/shard_map/pallas_call | solution.py:30
  36.5 2.3 %collective-permute-done.6.refs_0_ = bf16[128,768]{1,0:T(8,128)(2,1)S(1)} collective-permute-done((bf16[128,768]{1,0:T(8,128)(2,1)S(1)}, bf16[128,768]{1,0:T(8,128)(2,1)S(1)}, u32[]{:S(2)}, u32[]{:S(2)}) %collective-permute-start.6) | collective-permute-done | bytes 196640 | tf_op jit(solution)/shard_map/ppermute | solution.py:257
  38.7 0.9 shard_map.43
  39.6 10.5 %all_to_all.35.recv_ref = bf16[8,16,128]{2,1,0:T(8,128)(2,1)S(1)} all-to-all(bf16[8,16,128]{2,1,0:T(8,128)(2,1)S(1)} %get-tuple-element.41), channel_id=1, replica_groups=mesh['y'=8,'core'=2,'x'=4,'z'=8] {'y'}, dimensions={0} | all-to-all | bytes 65536 | tf_op jit(solution)/shard_map/all_to_all | solution.py:281
  50.6 4.0 %collective-permute-start.8 = (f32[16,128]{1,0:T(8,128)S(1)}, f32[16,128]{1,0:T(8,128)S(1)}, u32[]{:S(2)}, u32[]{:S(2)}) collective-permute-start(f32[16,128]{1,0:T(8,128)S(1)} %shard_map.44), channel_id=1, source_target_pairs={{0,32},{32,0},{1,33},{33,1},{2,34},{34,2},{3,35},{35,3},{4,36},{36... | collective-permute-start | bytes 24584 | tf_op jit(solution)/shard_map/ppermute | solution.py:240
  54.7 0.8 collective-permute-done.8
  55.5 21.3 %all_to_all.36.recv_ref = bf16[32,16,128]{2,1,0:T(8,128)(2,1)S(1)} all-to-all(bf16[32,16,128]{2,1,0:T(8,128)(2,1)S(1)} %broadcast_in_dim.6), channel_id=1, replica_groups=mesh['y'=8,'core'=2,'x'=4,'z'=8] {'z','x'}, dimensions={0} | all-to-all | bytes 262144 | tf_op jit(solution)/shard_map/all_to_all | solution.py:287
  76.9 0.6 shard_map.45
  77.4 9.2 %all_to_all.37.recv_ref = bf16[8,16,128]{2,1,0:T(8,128)(2,1)S(1)} all-to-all(bf16[8,16,128]{2,1,0:T(8,128)(2,1)S(1)} %get-tuple-element.43), channel_id=1, replica_groups=mesh['y'=8,'core'=2,'x'=4,'z'=8] {'y'}, dimensions={0} | all-to-all | bytes 65536 | tf_op jit(solution)/shard_map/all_to_all | solution.py:281
  86.7 0.6 shard_map.46
  87.2 5.1 %collective-permute-start.9 = (f32[8,128]{1,0:T(8,128)S(1)}, f32[8,128]{1,0:T(8,128)S(1)}, u32[]{:S(2)}, u32[]{:S(2)}) collective-permute-start(f32[8,128]{1,0:T(8,128)S(1)} %shard_map.46), channel_id=1, source_target_pairs={{0,32},{32,0},{1,33},{33,1},{2,34},{34,2},{3,35},{35,3},{4,36},{36... | collective-permute-start | bytes 12296 | tf_op jit(solution)/shard_map/ppermute | solution.py:240
  92.4 0.8 collective-permute-done.9
  93.2 11.8 %all_to_all.38.recv_ref = bf16[32,8,128]{2,1,0:T(8,128)(2,1)S(1)} all-to-all(bf16[32,8,128]{2,1,0:T(8,128)(2,1)S(1)} %broadcast_in_dim.7), channel_id=1, replica_groups=mesh['y'=8,'core'=2,'x'=4,'z'=8] {'z','x'}, dimensions={0} | all-to-all | bytes 131072 | tf_op jit(solution)/shard_map/all_to_all | solution.py:287
  105.0 0.6 shard_map.47
  105.6 9.2 %all_to_all.39.recv_ref.col_ref = bf16[8,16,128]{2,1,0:T(8,128)(2,1)S(1)} all-to-all(bf16[8,16,128]{2,1,0:T(8,128)(2,1)S(1)} %shard_map.47), channel_id=1, replica_groups=mesh['y'=8,'core'=2,'x'=4,'z'=8] {'y'}, dimensions={0} | all-to-all | bytes 65536 | tf_op jit(solution)/shard_map/all_to_all | solution.py:281
  114.9 0.6 shard_map.48
  115.4 4.8 %collective-permute-start.10 = (f32[8,128]{1,0:T(8,128)S(1)}, f32[8,128]{1,0:T(8,128)S(1)}, u32[]{:S(2)}, u32[]{:S(2)}) collective-permute-start(f32[8,128]{1,0:T(8,128)S(1)} %shard_map.48), channel_id=1, source_target_pairs={{0,32},{32,0},{1,33},{33,1},{2,34},{34,2},{3,35},{35,3},{4,36},{36... | collective-permute-start | bytes 12296 | tf_op jit(solution)/shard_map/ppermute | solution.py:240
  120.3 0.8 collective-permute-done.10
  121.1 11.8 %all_to_all.40.row_ref = bf16[32,8,128]{2,1,0:T(8,128)(2,1)S(1)} all-to-all(bf16[32,8,128]{2,1,0:T(8,128)(2,1)S(1)} %broadcast_in_dim.8), channel_id=1, replica_groups=mesh['y'=8,'core'=2,'x'=4,'z'=8] {'z','x'}, dimensions={0} | all-to-all | bytes 131072 | tf_op jit(solution)/shard_map/all_to_all | solution.py:287
  132.9 2.8 %shard_map.49 = (bf16[32,16,768]{2,1,0:T(8,128)(2,1)S(1)}, bf16[32,16,768]{2,1,0:T(8,128)(2,1)S(1)}, bf16[1024,1024]{1,0:T(8,128)(2,1)S(1)}) custom-call(f32[2,512,768]{2,1,0:T(8,128)S(1)} %get-tuple-element.37.early, f32[2,512,256]{2,1,0:T(8,128)S(1)} %get-tuple-element.40.late, bf16[32,8,128]{2,1,0:T(8,128)(2,1)S(1)} %all_to_all.40.row_ref, ...), custom_call_target="tpu_custom_call" | custom-call | flops 1610612736 | bytes 2097152 | tf_op jit(solution)/shard_map/pallas_call | solution.py:30
  135.7 3.7 %collective-permute-start.11 = (bf16[32,16,768]{2,1,0:T(8,128)(2,1)S(1)}, bf16[32,16,768]{2,1,0:T(8,128)(2,1)S(1)}, u32[]{:S(2)}, u32[]{:S(2)}) collective-permute-start(bf16[32,16,768]{2,1,0:T(8,128)(2,1)S(1)} %get-tuple-element.60), channel_id=1, source_target_pairs={{0,32},{32,0},{1,33},{33,1},{2,34},{34,2},{3,35},{35,3},{4,36},{36... | collective-permute-start | bytes 2359304 | tf_op jit(solution)/shard_map/ppermute | solution.py:240
  139.4 1.8 %shard_map.50 = (bf16[768,128]{1,0:T(8,128)(2,1)S(1)}, bf16[768,128]{1,0:T(8,128)(2,1)S(1)}, bf16[768,128]{1,0:T(8,128)(2,1)S(1)}, bf16[768,128]{1,0:T(8,128)(2,...) custom-call(bf16[768,1024]{1,0:T(8,128)(2,1)S(1)} %get-tuple-element, ...), custom_call_target="tpu_custom_call" | custom-call | flops 1610612736 | bytes 2097152 | tf_op jit(solution)/shard_map/pallas_call | solution.py:30
  141.2 1.1 add_convert_fusion
  142.3 3.9 %all-to-all-start.6 = ((bf16[32,16,768]{2,1,0:T(8,128)(2,1)}), bf16[32,16,768]{2,1,0:T(8,128)(2,1)S(1)}, u32[]{:S(2)}, u32[]{:S(2)}) async-start(bf16[32,16,768]{2,1,0:T(8,128)(2,1)} %add_convert_fusion), calls=%async_computation.6 | async-start | bytes 1572864 | tf_op jit(solution)/shard_map/all_to_all | solution.py:351
  146.2 2.2 %collective-permute-start.14 = (bf16[768,128]{1,0:T(8,128)(2,1)S(1)}, bf16[768,128]{1,0:T(8,128)(2,1)S(1)}, u32[]{:S(2)}, u32[]{:S(2)}) collective-permute-start(bf16[768,128]{1,0:T(8,128)(2,1)S(1)} %get-tuple-element.66), channel_id=1, source_target_pairs={{64,128},{128,64},{192,256},{256,192},{320,384},{384,320},{448,0},... | collective-permute-start | bytes 589832 | tf_op jit(solution)/shard_map/ppermute | solution.py:257
  148.4 2.2 %collective-permute-start.15 = (bf16[768,128]{1,0:T(8,128)(2,1)S(1)}, bf16[768,128]{1,0:T(8,128)(2,1)S(1)}, u32[]{:S(2)}, u32[]{:S(2)}) collective-permute-start(bf16[768,128]{1,0:T(8,128)(2,1)S(1)} %get-tuple-element.67), channel_id=1, source_target_pairs={{0,64},{64,0},{128,192},{192,128},{256,320},{320,256},{384,448},{4... | collective-permute-start | bytes 589832 | tf_op jit(solution)/shard_map/ppermute | solution.py:257
  150.6 2.8 %collective-permute-start.17 = (bf16[768,128]{1,0:T(8,128)(2,1)S(1)}, bf16[768,128]{1,0:T(8,128)(2,1)S(1)}, u32[]{:S(2)}, u32[]{:S(2)}) collective-permute-start(bf16[768,128]{1,0:T(8,128)(2,1)S(1)} %get-tuple-element.69), channel_id=1, source_target_pairs={{0,128},{128,0},{64,192},{192,64},{256,384},{384,256},{320,448},{4... | collective-permute-start | bytes 589832 | tf_op jit(solution)/shard_map/ppermute | solution.py:257
  153.4 4.4 %collective-permute-start.12 = (bf16[768,128]{1,0:T(8,128)(2,1)S(1)}, bf16[768,128]{1,0:T(8,128)(2,1)S(1)}, u32[]{:S(2)}, u32[]{:S(2)}) collective-permute-start(bf16[768,128]{1,0:T(8,128)(2,1)S(1)} %get-tuple-element.63), channel_id=1, source_target_pairs={{0,64},{64,0},{128,192},{192,128},{256,320},{320,256},{384,448},{4... | collective-permute-start | bytes 589832 | tf_op jit(solution)/shard_map/ppermute | solution.py:257
  157.8 2.3 %collective-permute-start.13 = (bf16[768,128]{1,0:T(8,128)(2,1)S(1)}, bf16[768,128]{1,0:T(8,128)(2,1)S(1)}, u32[]{:S(2)}, u32[]{:S(2)}) collective-permute-start(bf16[768,128]{1,0:T(8,128)(2,1)S(1)} %get-tuple-element.64), channel_id=1, source_target_pairs={{64,128},{128,64},{192,256},{256,192},{320,384},{384,320},{448,0},... | collective-permute-start | bytes 589832 | tf_op jit(solution)/shard_map/ppermute | solution.py:257
  160.1 2.6 %collective-permute-done.17 = bf16[768,128]{1,0:T(8,128)(2,1)S(1)} collective-permute-done((bf16[768,128]{1,0:T(8,128)(2,1)S(1)}, bf16[768,128]{1,0:T(8,128)(2,1)S(1)}, u32[]{:S(2)}, u32[]{:S(2)}) %collective-permute-start.17) | collective-permute-done | bytes 196640 | tf_op jit(solution)/shard_map/ppermute | solution.py:257
  162.9 1.9 %collective-permute-start.18 = (bf16[768,128]{1,0:T(8,128)(2,1)S(1)}, bf16[768,128]{1,0:T(8,128)(2,1)S(1)}, u32[]{:S(2)}, u32[]{:S(2)}) collective-permute-start(bf16[768,128]{1,0:T(8,128)(2,1)S(1)} %get-tuple-element.72), channel_id=1, source_target_pairs={{128,256},{256,128},{192,320},{320,192},{384,0},{0,384},{448,64},{... | collective-permute-start | bytes 589832 | tf_op jit(solution)/shard_map/ppermute | solution.py:257
  164.8 2.9 %collective-permute-start.16 = (bf16[768,128]{1,0:T(8,128)(2,1)S(1)}, bf16[768,128]{1,0:T(8,128)(2,1)S(1)}, u32[]{:S(2)}, u32[]{:S(2)}) collective-permute-start(bf16[768,128]{1,0:T(8,128)(2,1)S(1)} %get-tuple-element.73), channel_id=1, source_target_pairs={{0,128},{128,0},{64,192},{192,64},{256,384},{384,256},{320,448},{4... | collective-permute-start | bytes 589832 | tf_op jit(solution)/shard_map/ppermute | solution.py:257
  167.7 0.6 all-to-all-done.6
  168.4 0.6 copy.8
  169.0 2.2 %collective-permute-done.18.refs_3_ = bf16[768,128]{1,0:T(8,128)(2,1)S(1)} collective-permute-done((bf16[768,128]{1,0:T(8,128)(2,1)S(1)}, bf16[768,128]{1,0:T(8,128)(2,1)S(1)}, u32[]{:S(2)}, u32[]{:S(2)}) %collective-permute-start.18) | collective-permute-done | bytes 196640 | tf_op jit(solution)/shard_map/ppermute | solution.py:257
  171.2 6.8 %collective-permute-done.16.refs_2_ = bf16[768,128]{1,0:T(8,128)(2,1)S(1)} collective-permute-done((bf16[768,128]{1,0:T(8,128)(2,1)S(1)}, bf16[768,128]{1,0:T(8,128)(2,1)S(1)}, u32[]{:S(2)}, u32[]{:S(2)}) %collective-permute-start.16) | collective-permute-done | bytes 196640 | tf_op jit(solution)/shard_map/ppermute | solution.py:257
  178.0 0.9 shard_map.51
  (24 shorter events, 1.0 us)
Async XLA Ops:
  0.6 27.2 %collective-permute-start = (bf16[256,2,768]{2,1,0:T(2,128)(2,1)}, bf16[256,2,768]{2,1,0:T(2,128)(2,1)S(1)}, u32[]{:S(2)}, u32[]{:S(2)}) collective-permute-start(bf16[256,2,768]{2,1,0:T(2,128)(2,1)} %param.2), channel_id=1, source_target_pairs={{0,32},{32,0},{1,33},{33,1},{2,34},{34,2},{3,35},{35,3},{4,36},{36... | collective-permute-start | bytes 2359304 | tf_op jit(solution)/shard_map/ppermute | solution.py:240
  9.4 13.2 %collective-permute-start.3 = (bf16[128,768]{1,0:T(8,128)(2,1)}, bf16[128,768]{1,0:T(8,128)(2,1)S(1)}, u32[]{:S(2)}, u32[]{:S(2)}) collective-permute-start(bf16[128,768]{1,0:T(8,128)(2,1)} %refs_0_.1), channel_id=1, source_target_pairs={{0,128},{128,0},{64,192},{192,64},{256,384},{384,256},{320,448},{4... | collective-permute-start | bytes 589832 | tf_op jit(solution)/shard_map/ppermute | solution.py:257
  11.4 11.2 %collective-permute-start.4 = (bf16[128,768]{1,0:T(8,128)(2,1)}, bf16[128,768]{1,0:T(8,128)(2,1)S(1)}, u32[]{:S(2)}, u32[]{:S(2)}) collective-permute-start(bf16[128,768]{1,0:T(8,128)(2,1)} %refs_0_.1), channel_id=1, source_target_pairs={{128,256},{256,128},{192,320},{320,192},{384,0},{0,384},{448,64},{... | collective-permute-start | bytes 589832 | tf_op jit(solution)/shard_map/ppermute | solution.py:257
  13.7 20.8 %collective-permute-start.2 = (bf16[128,768]{1,0:T(8,128)(2,1)}, bf16[128,768]{1,0:T(8,128)(2,1)S(1)}, u32[]{:S(2)}, u32[]{:S(2)}) collective-permute-start(bf16[128,768]{1,0:T(8,128)(2,1)} %refs_0_.1), channel_id=1, source_target_pairs={{64,128},{128,64},{192,256},{256,192},{320,384},{384,320},{448,0},... | collective-permute-start | bytes 589832 | tf_op jit(solution)/shard_map/ppermute | solution.py:257
  16.0 18.5 %collective-permute-start.1 = (bf16[128,768]{1,0:T(8,128)(2,1)}, bf16[128,768]{1,0:T(8,128)(2,1)S(1)}, u32[]{:S(2)}, u32[]{:S(2)}) collective-permute-start(bf16[128,768]{1,0:T(8,128)(2,1)} %refs_0_.1), channel_id=1, source_target_pairs={{0,64},{64,0},{128,192},{192,128},{256,320},{320,256},{384,448},{4... | collective-permute-start | bytes 589832 | tf_op jit(solution)/shard_map/ppermute | solution.py:257
  22.6 11.9 %collective-permute-start.5 = (bf16[128,768]{1,0:T(8,128)(2,1)S(1)}, bf16[128,768]{1,0:T(8,128)(2,1)S(1)}, u32[]{:S(2)}, u32[]{:S(2)}) collective-permute-start(bf16[128,768]{1,0:T(8,128)(2,1)S(1)} %get-tuple-element.75), channel_id=1, source_target_pairs={{64,128},{128,64},{192,256},{256,192},{320,384},{384,320},{448,0},... | collective-permute-start | bytes 589832 | tf_op jit(solution)/shard_map/ppermute | solution.py:257
  24.6 11.9 %collective-permute-start.7 = (bf16[128,768]{1,0:T(8,128)(2,1)S(1)}, bf16[128,768]{1,0:T(8,128)(2,1)S(1)}, u32[]{:S(2)}, u32[]{:S(2)}) collective-permute-start(bf16[128,768]{1,0:T(8,128)(2,1)S(1)} %collective-permute-done.4.refs_4_), channel_id=1, source_target_pairs={{0,128},{128,0},{64,192},{192,64},{256,384},{384,256},{320,448},{4... | collective-permute-start | bytes 589832 | tf_op jit(solution)/shard_map/ppermute | solution.py:257
  27.9 10.9 %collective-permute-start.6 = (bf16[128,768]{1,0:T(8,128)(2,1)S(1)}, bf16[128,768]{1,0:T(8,128)(2,1)S(1)}, u32[]{:S(2)}, u32[]{:S(2)}) collective-permute-start(bf16[128,768]{1,0:T(8,128)(2,1)S(1)} %get-tuple-element.74), channel_id=1, source_target_pairs={{0,64},{64,0},{128,192},{192,128},{256,320},{320,256},{384,448},{4... | collective-permute-start | bytes 589832 | tf_op jit(solution)/shard_map/ppermute | solution.py:257
  33.5 1.1 copy-start
  50.6 4.8 %collective-permute-start.8 = (f32[16,128]{1,0:T(8,128)S(1)}, f32[16,128]{1,0:T(8,128)S(1)}, u32[]{:S(2)}, u32[]{:S(2)}) collective-permute-start(f32[16,128]{1,0:T(8,128)S(1)} %shard_map.44), channel_id=1, source_target_pairs={{0,32},{32,0},{1,33},{33,1},{2,34},{34,2},{3,35},{35,3},{4,36},{36... | collective-permute-start | bytes 24584 | tf_op jit(solution)/shard_map/ppermute | solution.py:240
  87.2 6.0 %collective-permute-start.9 = (f32[8,128]{1,0:T(8,128)S(1)}, f32[8,128]{1,0:T(8,128)S(1)}, u32[]{:S(2)}, u32[]{:S(2)}) collective-permute-start(f32[8,128]{1,0:T(8,128)S(1)} %shard_map.46), channel_id=1, source_target_pairs={{0,32},{32,0},{1,33},{33,1},{2,34},{34,2},{3,35},{35,3},{4,36},{36... | collective-permute-start | bytes 12296 | tf_op jit(solution)/shard_map/ppermute | solution.py:240
  115.4 5.6 %collective-permute-start.10 = (f32[8,128]{1,0:T(8,128)S(1)}, f32[8,128]{1,0:T(8,128)S(1)}, u32[]{:S(2)}, u32[]{:S(2)}) collective-permute-start(f32[8,128]{1,0:T(8,128)S(1)} %shard_map.48), channel_id=1, source_target_pairs={{0,32},{32,0},{1,33},{33,1},{2,34},{34,2},{3,35},{35,3},{4,36},{36... | collective-permute-start | bytes 12296 | tf_op jit(solution)/shard_map/ppermute | solution.py:240
  135.7 5.5 %collective-permute-start.11 = (bf16[32,16,768]{2,1,0:T(8,128)(2,1)S(1)}, bf16[32,16,768]{2,1,0:T(8,128)(2,1)S(1)}, u32[]{:S(2)}, u32[]{:S(2)}) collective-permute-start(bf16[32,16,768]{2,1,0:T(8,128)(2,1)S(1)} %get-tuple-element.60), channel_id=1, source_target_pairs={{0,32},{32,0},{1,33},{33,1},{2,34},{34,2},{3,35},{35,3},{4,36},{36... | collective-permute-start | bytes 2359304 | tf_op jit(solution)/shard_map/ppermute | solution.py:240
  142.3 25.9 %all-to-all-start.6 = ((bf16[32,16,768]{2,1,0:T(8,128)(2,1)}), bf16[32,16,768]{2,1,0:T(8,128)(2,1)S(1)}, u32[]{:S(2)}, u32[]{:S(2)}) async-start(bf16[32,16,768]{2,1,0:T(8,128)(2,1)} %add_convert_fusion), calls=%async_computation.6 | async-start | bytes 1572864 | tf_op jit(solution)/shard_map/all_to_all | solution.py:351
  146.2 13.9 %collective-permute-start.14 = (bf16[768,128]{1,0:T(8,128)(2,1)S(1)}, bf16[768,128]{1,0:T(8,128)(2,1)S(1)}, u32[]{:S(2)}, u32[]{:S(2)}) collective-permute-start(bf16[768,128]{1,0:T(8,128)(2,1)S(1)} %get-tuple-element.66), channel_id=1, source_target_pairs={{64,128},{128,64},{192,256},{256,192},{320,384},{384,320},{448,0},... | collective-permute-start | bytes 589832 | tf_op jit(solution)/shard_map/ppermute | solution.py:257
  148.4 11.7 %collective-permute-start.15 = (bf16[768,128]{1,0:T(8,128)(2,1)S(1)}, bf16[768,128]{1,0:T(8,128)(2,1)S(1)}, u32[]{:S(2)}, u32[]{:S(2)}) collective-permute-start(bf16[768,128]{1,0:T(8,128)(2,1)S(1)} %get-tuple-element.67), channel_id=1, source_target_pairs={{0,64},{64,0},{128,192},{192,128},{256,320},{320,256},{384,448},{4... | collective-permute-start | bytes 589832 | tf_op jit(solution)/shard_map/ppermute | solution.py:257
  150.6 12.1 %collective-permute-start.17 = (bf16[768,128]{1,0:T(8,128)(2,1)S(1)}, bf16[768,128]{1,0:T(8,128)(2,1)S(1)}, u32[]{:S(2)}, u32[]{:S(2)}) collective-permute-start(bf16[768,128]{1,0:T(8,128)(2,1)S(1)} %get-tuple-element.69), channel_id=1, source_target_pairs={{0,128},{128,0},{64,192},{192,64},{256,384},{384,256},{320,448},{4... | collective-permute-start | bytes 589832 | tf_op jit(solution)/shard_map/ppermute | solution.py:257
  153.4 15.7 %collective-permute-start.12 = (bf16[768,128]{1,0:T(8,128)(2,1)S(1)}, bf16[768,128]{1,0:T(8,128)(2,1)S(1)}, u32[]{:S(2)}, u32[]{:S(2)}) collective-permute-start(bf16[768,128]{1,0:T(8,128)(2,1)S(1)} %get-tuple-element.63), channel_id=1, source_target_pairs={{0,64},{64,0},{128,192},{192,128},{256,320},{320,256},{384,448},{4... | collective-permute-start | bytes 589832 | tf_op jit(solution)/shard_map/ppermute | solution.py:257
  157.8 11.2 %collective-permute-start.13 = (bf16[768,128]{1,0:T(8,128)(2,1)S(1)}, bf16[768,128]{1,0:T(8,128)(2,1)S(1)}, u32[]{:S(2)}, u32[]{:S(2)}) collective-permute-start(bf16[768,128]{1,0:T(8,128)(2,1)S(1)} %get-tuple-element.64), channel_id=1, source_target_pairs={{64,128},{128,64},{192,256},{256,192},{320,384},{384,320},{448,0},... | collective-permute-start | bytes 589832 | tf_op jit(solution)/shard_map/ppermute | solution.py:257
  162.9 8.4 %collective-permute-start.18 = (bf16[768,128]{1,0:T(8,128)(2,1)S(1)}, bf16[768,128]{1,0:T(8,128)(2,1)S(1)}, u32[]{:S(2)}, u32[]{:S(2)}) collective-permute-start(bf16[768,128]{1,0:T(8,128)(2,1)S(1)} %get-tuple-element.72), channel_id=1, source_target_pairs={{128,256},{256,128},{192,320},{320,192},{384,0},{0,384},{448,64},{... | collective-permute-start | bytes 589832 | tf_op jit(solution)/shard_map/ppermute | solution.py:257
  164.8 13.2 %collective-permute-start.16 = (bf16[768,128]{1,0:T(8,128)(2,1)S(1)}, bf16[768,128]{1,0:T(8,128)(2,1)S(1)}, u32[]{:S(2)}, u32[]{:S(2)}) collective-permute-start(bf16[768,128]{1,0:T(8,128)(2,1)S(1)} %get-tuple-element.73), channel_id=1, source_target_pairs={{0,128},{128,0},{64,192},{192,64},{256,384},{384,256},{320,448},{4... | collective-permute-start | bytes 589832 | tf_op jit(solution)/shard_map/ppermute | solution.py:257
